TPU v7x, 32 devices: a whole 2x2x4 slice. The times are simulated.
32 devices in a mesh: row: 8 (over z, x), col: 4 (over y, core).
Axes of the slice: x: 2, y: 2, z: 4, core: 2. Of those that a mesh axis runs over, the one named last changes fastest.
Arguments:
- pair: bfloat16 [2, 256, 256, 128], P(None, 'row', 'col'), may hold values from -6 to 6
- frames: float32 [2, 6, 256], replicated, may hold values from -6 to 6
- target: float32 [2, 6, 256], replicated, may hold values from -25 to 25
- lengths: int32 [2], replicated, may hold values from 128 to 256, as said below
- motif: int32 [2, 256], replicated, may hold values 0 or 1
- neighbours: int32 [2, 256, 32], P(None, 'row'), may hold values from 0 to 255, as said below
- weights: float32 [17, 128, 128], P(None, 'row')
- weights_m: float32 [17, 128, 128], P(None, 'row'), may hold values from -0.4375 to 0.4375
- weights_v: float32 [17, 128, 128], P(None, 'row'), may hold values from 0.00076293945 to 0.0030517578
- struct_w: float32 [6, 128], P(None, 'row'), may hold values from -0.0625 to 0.0625
- struct_m: float32 [6, 128], P(None, 'row'), may hold values from -12 to 12
- struct_v: float32 [6, 128], P(None, 'row'), may hold values from 4 to 16
- gains: float32 [6, 128], P(None, 'row'), may hold values from 0.5 to 1.5
- gains_m: float32 [6, 128], P(None, 'row'), may hold values from -0.875 to 0.875
- gains_v: float32 [6, 128], P(None, 'row'), may hold values from 0.0030517578 to 0.012207031
Outputs:
- loss_sum: float32 [], replicated
- loss_count: float32 [], replicated
- new_weights_m: float32 [17, 128, 128], P(None, 'row')
- new_weights_v: float32 [17, 128, 128], P(None, 'row')
- new_weights: float32 [17, 128, 128], P(None, 'row')
- new_struct_m: float32 [6, 128], P(None, 'row')
- new_struct_v: float32 [6, 128], P(None, 'row')
- new_struct: float32 [6, 128], P(None, 'row')
- new_gains_m: float32 [6, 128], P(None, 'row')
- new_gains_v: float32 [6, 128], P(None, 'row')
- new_gains: float32 [6, 128], P(None, 'row')
Inputs may be any that keep to these rules, and one draw needn't show every extreme that they name: `lengths`: every draw has a crop of exactly 256 residues. `neighbours`: every entry of crop n lies below that crop's residue count.
All inputs are finite; a program needn't handle non-finite values.
Results may differ from a plain program's by a relative error of at most 0.02.
The roundings to bfloat16 on the way count: a program that leaves them out, or rounds other values in their place, can miss the bound.
Values may be sent and summed in bfloat16 or wider, within the bound.
A program may use at most 256 MiB of HBM per device.

v0:
```python
import jax
import jax.numpy as jnp
from jax import lax
from jax.sharding import PartitionSpec as P

NH = 4
STEP = 5


BETA_ONE = 0.5
BETA_TWO = 0.5
ADAM_EPS = 1e-08


def layer_norm(values, gain_vec):
    center = values - jnp.mean(values, axis=-1, keepdims=True)
    spread = jnp.mean(center * center, axis=-1, keepdims=True)
    return center * lax.rsqrt(spread + 1e-05) * gain_vec


def row_panels(values):
    return lax.all_gather(values, "row", axis=1, tiled=True)


def col_panels(values):
    return lax.all_gather(values, "col", axis=2, tiled=True)


def col_sums(partial_term, row_total):
    return lax.psum_scatter(
        partial_term(jnp.int32(0), row_total * lax.axis_size("col")).astype(jnp.bfloat16),
        "col",
        scatter_dimension=0,
        tiled=True,
    ).astype(jnp.float32)


def row_sums(partial_term, row_total):
    return lax.psum_scatter(
        partial_term(jnp.int32(0), row_total * lax.axis_size("row")).astype(jnp.bfloat16),
        "row",
        scatter_dimension=0,
        tiled=True,
    ).astype(jnp.float32)


def tri_gates(projected, valid_mask):
    channels = projected.shape[-1] // 5
    left_side = (
        valid_mask[..., None]
        * jax.nn.sigmoid(projected[..., :channels])
        * projected[..., channels : 2 * channels]
    )
    right_side = (
        valid_mask[..., None]
        * jax.nn.sigmoid(projected[..., 2 * channels : 3 * channels])
        * projected[..., 3 * channels : 4 * channels]
    )
    return (left_side, right_side, jax.nn.sigmoid(projected[..., 4 * channels :]))


def tri_product(left_low, right_low, outgoing):
    if outgoing:
        panels = row_panels(right_low)

        def partial_term(first_row, num_rows):
            return jnp.einsum(
                "bikh,bjkh->jbih", left_low, panels, preferred_element_type=jnp.float32
            )

        summed = col_sums(partial_term, right_low.shape[2])
        return (jnp.transpose(summed, (1, 2, 0, 3)), panels)
    panels = col_panels(left_low)

    def partial_term(first_row, num_rows):
        return jnp.einsum("bkih,bkjh->ibjh", panels, right_low, preferred_element_type=jnp.float32)

    summed = row_sums(partial_term, left_low.shape[1])
    return (jnp.transpose(summed, (1, 0, 2, 3)), panels)


def tri_core(z, w_input, w_output, gain_in, gain_out, valid_mask, outgoing):
    normed, norm_back = jax.vjp(layer_norm, z, gain_in)
    normed_low = normed.astype(jnp.bfloat16)
    projected = jnp.einsum("bijd,de->bije", normed_low, w_input, preferred_element_type=jnp.float32)
    (left_side, right_side, gating), gate_back = jax.vjp(
        lambda values: tri_gates(values, valid_mask), projected
    )
    left_low = left_side.astype(jnp.bfloat16)
    right_low = right_side.astype(jnp.bfloat16)
    product, panels = tri_product(left_low, right_low, outgoing)
    mixture, mix_back = jax.vjp(layer_norm, product, gain_out)
    mixed_low = mixture.astype(jnp.bfloat16)
    branch = jnp.einsum("bijh,hd->bijd", mixed_low, w_output, preferred_element_type=jnp.float32)
    stored = (
        norm_back,
        normed_low,
        gate_back,
        left_low,
        right_low,
        panels,
        mix_back,
        mixed_low,
        branch,
        gating,
    )
    return (z + gating * branch, stored)


def tri_back(z, grad_out, w_input, w_output, gain_in, gain_out, valid_mask, outgoing):
    _, stored = tri_core(z, w_input, w_output, gain_in, gain_out, valid_mask, outgoing)
    (
        norm_back,
        normed_low,
        gate_back,
        left_low,
        right_low,
        panels,
        mix_back,
        mixed_low,
        branch,
        gating,
    ) = stored
    grad_gate = grad_out * branch
    grad_branch = (grad_out * gating).astype(jnp.bfloat16)
    grad_wout = jnp.einsum(
        "bijh,bijd->hd", mixed_low, grad_branch, preferred_element_type=jnp.float32
    )
    grad_mixed = jnp.einsum(
        "bijd,hd->bijh", grad_branch, w_output, preferred_element_type=jnp.float32
    )
    grad_prod, grad_gain_out = mix_back(grad_mixed)
    grad_low = grad_prod.astype(jnp.bfloat16)
    if outgoing:
        grad_cols = col_panels(grad_low)
        grad_left = jnp.einsum(
            "bijh,bjkh->bikh", grad_cols, panels, preferred_element_type=jnp.float32
        )

        def partial_term(first_row, num_rows):
            return jnp.einsum(
                "bijh,bikh->jbkh", grad_cols, left_low, preferred_element_type=jnp.float32
            )

        grad_right = jnp.transpose(row_sums(partial_term, left_low.shape[1]), (1, 0, 2, 3))
    else:
        grad_rows = row_panels(grad_low)
        grad_right = jnp.einsum(
            "bkih,bijh->bkjh", panels, grad_rows, preferred_element_type=jnp.float32
        )

        def partial_term(first_row, num_rows):
            return jnp.einsum(
                "bkjh,bijh->ibkh", right_low, grad_rows, preferred_element_type=jnp.float32
            )

        grad_left = jnp.transpose(col_sums(partial_term, right_low.shape[2]), (1, 2, 0, 3))
    (grad_proj,) = gate_back((grad_left, grad_right, grad_gate))
    grad_proj_low = grad_proj.astype(jnp.bfloat16)
    grad_win = jnp.einsum(
        "bijd,bije->de", normed_low, grad_proj_low, preferred_element_type=jnp.float32
    )
    grad_normed = jnp.einsum(
        "bije,de->bijd", grad_proj_low, w_input, preferred_element_type=jnp.float32
    )
    grad_state, grad_gain_in = norm_back(grad_normed)
    return (grad_out + grad_state, grad_win, grad_wout, grad_gain_in, grad_gain_out)


def attn_split(projected):
    channels = projected.shape[-1] // 4
    scaling = (channels // NH) ** (-0.5)
    return (
        projected[..., :channels] * scaling,
        projected[..., channels : 2 * channels],
        projected[..., 2 * channels : 3 * channels],
        jax.nn.sigmoid(projected[..., 3 * channels :]),
    )


def attn_core(z, w_input, w_output, gain_vec, key_bias):
    crops, row_count, col_count, channels = z.shape
    depth = channels // NH
    normed, norm_back = jax.vjp(layer_norm, z, gain_vec)
    normed_low = normed.astype(jnp.bfloat16)
    projected = jnp.einsum("bijd,de->bije", normed_low, w_input, preferred_element_type=jnp.float32)
    (query, keys, values, gating), split_back = jax.vjp(attn_split, projected)
    query_low = query.astype(jnp.bfloat16).reshape(crops, row_count, col_count, NH, depth)
    local_pairs = jnp.concatenate([keys.astype(jnp.bfloat16), values.astype(jnp.bfloat16)], axis=-1)
    joined = col_panels(local_pairs)
    length = joined.shape[2]
    key_all = joined[..., :channels].reshape(crops, row_count, length, NH, depth)
    value_all = joined[..., channels:].reshape(crops, row_count, length, NH, depth)
    scores = jnp.einsum(
        "bijhd,bikhd->bihjk", query_low, key_all, preferred_element_type=jnp.float32
    )
    probs = jax.nn.softmax(scores + key_bias[:, None, None, None, :], axis=-1)
    probs_low = probs.astype(jnp.bfloat16)
    attended = jnp.einsum(
        "bihjk,bikhd->bijhd", probs_low, value_all, preferred_element_type=jnp.float32
    )
    attended = attended.reshape(crops, row_count, col_count, channels)
    gated_low = (attended * gating).astype(jnp.bfloat16)
    branch = jnp.einsum("bijh,hd->bijd", gated_low, w_output, preferred_element_type=jnp.float32)
    stored = (
        norm_back,
        normed_low,
        split_back,
        query_low,
        key_all,
        value_all,
        probs,
        probs_low,
        attended,
        gating,
        gated_low,
    )
    return (z + branch, stored)


def attn_back(z, grad_out, w_input, w_output, gain_vec, key_bias):
    crops, row_count, col_count, channels = z.shape
    _, stored = attn_core(z, w_input, w_output, gain_vec, key_bias)
    (
        norm_back,
        normed_low,
        split_back,
        query_low,
        key_all,
        value_all,
        probs,
        probs_low,
        attended,
        gating,
        gated_low,
    ) = stored
    length = key_all.shape[2]
    grad_branch = grad_out.astype(jnp.bfloat16)
    grad_wout = jnp.einsum(
        "bijh,bijd->hd", gated_low, grad_branch, preferred_element_type=jnp.float32
    )
    grad_gated = jnp.einsum(
        "bijd,hd->bijh", grad_branch, w_output, preferred_element_type=jnp.float32
    )
    grad_gate = grad_gated * attended
    grad_att = (
        (grad_gated * gating)
        .astype(jnp.bfloat16)
        .reshape(crops, row_count, col_count, NH, channels // NH)
    )
    grad_soft = jnp.einsum(
        "bijhd,bikhd->bihjk", grad_att, value_all, preferred_element_type=jnp.float32
    )
    grad_scores = probs * (grad_soft - jnp.sum(probs * grad_soft, axis=-1, keepdims=True))
    grad_scores_low = grad_scores.astype(jnp.bfloat16)
    grad_query = jnp.einsum(
        "bihjk,bikhd->bijhd", grad_scores_low, key_all, preferred_element_type=jnp.float32
    )
    grad_keys = jnp.einsum(
        "bihjk,bijhd->bikhd", grad_scores_low, query_low, preferred_element_type=jnp.float32
    )
    grad_values = jnp.einsum(
        "bihjk,bijhd->bikhd", probs_low, grad_att, preferred_element_type=jnp.float32
    )
    grad_joined = jnp.concatenate(
        [
            grad_keys.reshape(crops, row_count, length, channels),
            grad_values.reshape(crops, row_count, length, channels),
        ],
        axis=-1,
    )
    grad_pairs = lax.psum_scatter(
        grad_joined.astype(jnp.bfloat16), "col", scatter_dimension=2, tiled=True
    ).astype(jnp.float32)
    (grad_proj,) = split_back(
        (
            grad_query.reshape(crops, row_count, col_count, channels),
            grad_pairs[..., :channels],
            grad_pairs[..., channels:],
            grad_gate,
        )
    )
    grad_proj_low = grad_proj.astype(jnp.bfloat16)
    grad_win = jnp.einsum(
        "bijd,bije->de", normed_low, grad_proj_low, preferred_element_type=jnp.float32
    )
    grad_normed = jnp.einsum(
        "bije,de->bijd", grad_proj_low, w_input, preferred_element_type=jnp.float32
    )
    grad_state, grad_gain = norm_back(grad_normed)
    return (grad_out + grad_state, grad_win, grad_wout, grad_gain)


def adam_update(param, first, second, gradient, rate, decay):
    first_new = BETA_ONE * first + (1.0 - BETA_ONE) * gradient
    second_new = BETA_TWO * second + (1.0 - BETA_TWO) * gradient * gradient
    first_hat = first_new / (1.0 - BETA_ONE**STEP)
    second_hat = second_new / (1.0 - BETA_TWO**STEP)
    return (
        first_new,
        second_new,
        param - rate * (first_hat / (jnp.sqrt(second_hat) + ADAM_EPS) + decay * param),
    )


def per_device(
    pair,
    frames,
    target,
    lengths,
    motif,
    neighbours,
    weights,
    weights_m,
    weights_v,
    struct_w,
    struct_m,
    struct_v,
    gains,
    gains_m,
    gains_v,
):
    mats, struct_full, gain_full = (
        lax.all_gather(weights.astype(jnp.bfloat16), "row", axis=1, tiled=True),
        lax.all_gather(struct_w.astype(jnp.bfloat16), "row", axis=1, tiled=True),
        lax.all_gather(gains.astype(jnp.bfloat16), "row", axis=1, tiled=True),
    )
    gain_all = gain_full.astype(jnp.float32)
    crops, row_count, col_count, channels = pair.shape
    length = frames.shape[-1]
    row_start = lax.axis_index("row") * row_count
    col_start = lax.axis_index("col") * col_count
    row_ids = row_start + jnp.arange(row_count, dtype=jnp.int32)
    col_ids = col_start + jnp.arange(col_count, dtype=jnp.int32)
    limits = lengths[:, None]
    positions = jnp.arange(length, dtype=jnp.int32)
    row_live = (row_ids[None, :] < limits).astype(jnp.float32)
    col_live = (col_ids[None, :] < limits).astype(jnp.float32)
    valid_mask = row_live[:, :, None] * col_live[:, None, :]
    key_bias = jnp.where(positions[None, :] < limits, 0.0, -1000000000.0).astype(jnp.float32)
    counts = jnp.sum(neighbours[:, :, :, None] == col_ids[None, None, None, :], axis=2).astype(
        jnp.float32
    )

    def stacked(first_mat, how_many):
        return jnp.transpose(mats[first_mat : first_mat + how_many], (1, 0, 2)).reshape(
            channels, how_many * channels
        )

    outgoing_in = stacked(0, 5)
    incoming_in = stacked(6, 5)
    attend_in = stacked(12, 4)
    state_zero = pair.astype(jnp.float32)
    state_one, _ = tri_core(
        state_zero, outgoing_in, mats[5], gain_all[0], gain_all[1], valid_mask, True
    )
    state_two, _ = tri_core(
        state_one, incoming_in, mats[11], gain_all[2], gain_all[3], valid_mask, False
    )
    state_three, _ = attn_core(state_two, attend_in, mats[16], gain_all[4], key_bias)
    normed, norm_back = jax.vjp(layer_norm, state_three, gain_all[5])
    normed_low = normed.astype(jnp.bfloat16)
    edges = jnp.einsum("cd,bijd->bcij", struct_full, normed_low, preferred_element_type=jnp.float32)
    frame_rows = lax.dynamic_slice_in_dim(frames, row_start, row_count, 2)
    frame_cols = lax.dynamic_slice_in_dim(frames, col_start, col_count, 2)
    offsets = frame_cols[:, :, None, :] - frame_rows[:, :, :, None]
    update = lax.psum(jnp.sum(counts[:, None] * edges * offsets, axis=-1), "col")
    residual = frame_rows + update - lax.dynamic_slice_in_dim(target, row_start, row_count, 2)
    loss_weight = (1 - lax.dynamic_slice_in_dim(motif, row_start, row_count, 1)).astype(
        jnp.float32
    ) * row_live
    loss_sum = lax.psum(jnp.sum(loss_weight[:, None] * residual * residual), "row")
    loss_count = jnp.sum(
        (1 - motif).astype(jnp.float32) * (positions[None, :] < limits).astype(jnp.float32)
    )
    grad_update = 2.0 * residual * (loss_weight[:, None] * (1.0 / loss_count))
    grad_edges = (grad_update[:, :, :, None] * (counts[:, None] * offsets)).astype(jnp.bfloat16)
    grad_struct = jnp.einsum(
        "bcij,bijd->cd", grad_edges, normed_low, preferred_element_type=jnp.float32
    )
    grad_normed = jnp.einsum(
        "bcij,cd->bijd", grad_edges, struct_full, preferred_element_type=jnp.float32
    )
    grad_state, grad_gain_five = norm_back(grad_normed)
    grad_state, grad_attend_in, grad_attend_out, grad_gain_four = attn_back(
        state_two, grad_state, attend_in, mats[16], gain_all[4], key_bias
    )
    grad_state, grad_incoming_in, grad_incoming_out, grad_gain_two, grad_gain_three = tri_back(
        state_one, grad_state, incoming_in, mats[11], gain_all[2], gain_all[3], valid_mask, False
    )
    _, grad_outgoing_in, grad_outgoing_out, grad_gain_zero, grad_gain_one = tri_back(
        state_zero, grad_state, outgoing_in, mats[5], gain_all[0], gain_all[1], valid_mask, True
    )

    def unstacked(gradient, how_many):
        return jnp.transpose(gradient.reshape(channels, how_many, channels), (1, 0, 2))

    grad_mats = jnp.concatenate(
        [
            unstacked(grad_outgoing_in, 5),
            grad_outgoing_out[None],
            unstacked(grad_incoming_in, 5),
            grad_incoming_out[None],
            unstacked(grad_attend_in, 4),
            grad_attend_out[None],
        ],
        axis=0,
    )
    grad_gains = jnp.stack(
        [
            grad_gain_zero,
            grad_gain_one,
            grad_gain_two,
            grad_gain_three,
            grad_gain_four,
            grad_gain_five,
        ],
        axis=0,
    )
    total_mats, total_struct, total_gains = lax.psum(
        (grad_mats, grad_struct, grad_gains), ("row", "col")
    )
    shard_rows = weights.shape[1]
    shard_start = lax.axis_index("row") * shard_rows
    own_mats = lax.dynamic_slice_in_dim(total_mats, shard_start, shard_rows, 1)
    own_struct = lax.dynamic_slice_in_dim(total_struct, shard_start, shard_rows, 1)
    own_gains = lax.dynamic_slice_in_dim(total_gains, shard_start, shard_rows, 1)
    weight_first, weight_second, weight_new = adam_update(
        weights, weights_m, weights_v, own_mats, 0.1, 0.01
    )
    struct_first, struct_second, struct_new = adam_update(
        struct_w, struct_m, struct_v, own_struct, 0.1, 0.01
    )
    gain_first, gain_second, gain_new = adam_update(gains, gains_m, gains_v, own_gains, 0.4, 0.0)
    return (
        loss_sum,
        loss_count,
        weight_first,
        weight_second,
        weight_new,
        struct_first,
        struct_second,
        struct_new,
        gain_first,
        gain_second,
        gain_new,
    )


def solution(mesh):
    in_specs = (
        P(None, "row", "col", None),
        P(),
        P(),
        P(),
        P(),
        P(None, "row", None),
        P(None, "row", None),
        P(None, "row", None),
        P(None, "row", None),
        P(None, "row"),
        P(None, "row"),
        P(None, "row"),
        P(None, "row"),
        P(None, "row"),
        P(None, "row"),
    )
    out_specs = (
        P(),
        P(),
        P(None, "row", None),
        P(None, "row", None),
        P(None, "row", None),
        P(None, "row"),
        P(None, "row"),
        P(None, "row"),
        P(None, "row"),
        P(None, "row"),
        P(None, "row"),
    )
    return jax.shard_map(
        per_device, mesh=mesh, in_specs=in_specs, out_specs=out_specs, check_vma=False
    )
```

profile of v0, /device:TPU:0, one launch (start us, length us, event | category | flops | bytes accessed | tf_op | source)
XLA Modules:
  0.0 1479.3 jit_solution(11403174122895235264)
XLA Ops:
  9.4 27.8 %all-gather = bf16[8,16,6]{1,2,0:T(8,128)(2,1)S(1)} all-gather(bf16[1,16,6]{1,2,0:T(8,128)(2,1)S(1)} %convert_bitcast_fusion.5), channel_id=1, replica_groups=mesh['row'=8,'col'=4] {'row'}, dimensions={0}, use_global_device_ids=true | all-gather | bytes 1728 | tf_op jit(solution)/shard_map/all_gather | solution.py:326
  42.1 31.3 %all_gather.28 = bf16[17,128,128]{2,1,0:T(8,128)(2,1)S(1)} all-gather(bf16[17,16,128]{2,1,0:T(8,128)(2,1)S(1)} %convert_element_type.177), channel_id=1, replica_groups=mesh['row'=8,'col'=4] {'row'}, dimensions={1}, use_global_device_ids=true | all-gather | bytes 626688 | tf_op jit(solution)/shard_map/all_gather | solution.py:324
  85.0 120.5 %all-gather.8.cloned.1.call-done = bf16[2,256,64,128]{3,2,1,0:T(8,128)(2,1)} async-done(((bf16[2,32,64,128]{3,2,1,0:T(8,128)(2,1)}), bf16[2,256,64,128]{3,2,1,0:T(8,128)(2,1)}) %all-gather.8.cloned.1.call-update) | async-done | bytes 8388624 | tf_op jit(solution)/shard_map/all_gather | solution.py:22
  205.5 24.0 %copy.423 = bf16[2,256,64,128]{2,1,3,0:T(8,128)(2,1)} copy(bf16[2,256,64,128]{3,2,1,0:T(8,128)(2,1)} %all-gather.8.cloned.1.call-done) | data formatting | bytes 16777216 | tf_op jit(solution)/shard_map/all_gather | solution.py:22
  249.8 42.4 %reduce-scatter.9.cloned.1.call-done = bf16[64,2,32,128]{3,2,1,0:T(8,128)(2,1)} async-done(((bf16[256,2,32,128]{3,2,1,0:T(8,128)(2,1)}), bf16[64,2,32,128]{3,2,1,0:T(8,128)(2,1)}) %reduce-scatter.9.cloned.1.call-update) | async-done | bytes 1048592 | tf_op jit(solution)/shard_map/reduce_scatter | solution.py:30
  314.8 30.9 %all-gather.10.cloned.1.call-done = bf16[2,32,256,128]{3,2,1,0:T(8,128)(2,1)} async-done(((bf16[2,32,64,128]{3,2,1,0:T(8,128)(2,1)}), bf16[2,32,256,128]{3,2,1,0:T(8,128)(2,1)}) %all-gather.10.cloned.1.call-update) | async-done | bytes 4194320 | tf_op jit(solution)/shard_map/all_gather | solution.py:26
  362.2 13.5 copy.431
  377.2 147.7 %reduce-scatter.11.cloned.1.call-done = bf16[32,2,64,128]{3,2,1,0:T(8,128)(2,1)} async-done(((bf16[256,2,64,128]{3,2,1,0:T(8,128)(2,1)}), bf16[32,2,64,128]{3,2,1,0:T(8,128)(2,1)}) %reduce-scatter.11.cloned.1.call-update) | async-done | bytes 1048592 | tf_op jit(solution)/shard_map/reduce_scatter | solution.py:39
  543.0 26.0 %all-gather.1 = bf16[8,16,6]{1,2,0:T(8,128)(2,1)S(1)} all-gather(bf16[1,16,6]{1,2,0:T(8,128)(2,1)S(1)} %convert_bitcast_fusion.4), channel_id=1, replica_groups=mesh['row'=8,'col'=4] {'row'}, dimensions={0}, use_global_device_ids=true | all-gather | bytes 1728 | tf_op jit(solution)/shard_map/all_gather | solution.py:325
  578.1 21.6 %all-gather.12.cloned.1.call-done = bf16[2,32,256,256]{3,2,1,0:T(8,128)(2,1)} async-done(((bf16[2,32,64,256]{3,2,1,0:T(8,128)(2,1)}), bf16[2,32,256,256]{3,2,1,0:T(8,128)(2,1)}) %all-gather.12.cloned.1.call-update) | async-done | bytes 8388624 | tf_op jit(solution)/shard_map/all_gather | solution.py:26
  686.4 13.2 multiply_reduce_fusion
  705.9 13.7 multiply_convert_fusion
  753.1 58.8 %reduce-scatter.13.cloned.1.call-done = bf16[2,32,64,256]{3,2,1,0:T(8,128)(2,1)} async-done(((bf16[2,32,256,256]{3,2,1,0:T(8,128)(2,1)}), bf16[2,32,64,256]{3,2,1,0:T(8,128)(2,1)}) %reduce-scatter.13.cloned.1.call-update) | async-done | bytes 2097168 | tf_op jit(solution)/shard_map/reduce_scatter | solution.py:272
  841.3 125.1 %all-gather.14.cloned.1.call-done = bf16[2,256,64,128]{3,2,0,1:T(8,128)(2,1)} async-done(((bf16[2,32,64,128]{3,2,0,1:T(8,128)(2,1)}), bf16[2,256,64,128]{3,2,0,1:T(8,128)(2,1)}) %all-gather.14.cloned.1.call-update) | async-done | bytes 8388624 | tf_op jit(solution)/shard_map/all_gather | solution.py:22
  966.4 24.3 %copy.457 = bf16[2,256,64,128]{2,1,3,0:T(8,128)(2,1)} copy(bf16[2,256,64,128]{3,2,0,1:T(8,128)(2,1)} %all-gather.14.cloned.1.call-done) | data formatting | bytes 16777216 | tf_op jit(solution)/shard_map/all_gather | solution.py:22
  1009.4 13.2 fusion.144
  1026.5 25.7 %reduce-scatter.15.cloned.1.call-done = bf16[64,2,32,128]{3,0,2,1:T(8,128)(2,1)} async-done(((bf16[256,2,32,128]{3,0,2,1:T(8,128)(2,1)}), bf16[64,2,32,128]{3,0,2,1:T(8,128)(2,1)}) %reduce-scatter.15.cloned.1.call-update) | async-done | bytes 1048592 | tf_op jit(solution)/shard_map/reduce_scatter | solution.py:30
  1081.5 34.6 %all-gather.16.cloned.1.call-done = bf16[2,32,256,128]{3,1,0,2:T(8,128)(2,1)} async-done(((bf16[2,32,64,128]{3,1,0,2:T(8,128)(2,1)}), bf16[2,32,256,128]{3,1,0,2:T(8,128)(2,1)}) %all-gather.16.cloned.1.call-update) | async-done | bytes 4194320 | tf_op jit(solution)/shard_map/all_gather | solution.py:26
  1133.2 13.9 copy.504
  1147.1 23.2 %copy.551 = bf16[32,8,128,128]{3,1,2,0:T(8,128)(2,1)} copy(bf16[32,8,128,128]{3,2,1,0:T(8,128)(2,1)} %bitcast.314) | data formatting | bytes 16777216
  1170.4 22.3 %psum.36 = f32[]{:T(128)} all-reduce(f32[]{:T(128)} %get-tuple-element.113), channel_id=1, replica_groups=mesh['row'=8,'col'=4] {'row'}, use_global_device_ids=true, to_apply=%region_20.21 | all-reduce | flops 1 | bytes 8 | tf_op jit(solution)/shard_map/psum | solution.py:372
  1227.1 91.8 %reduce-scatter.17.cloned.1.call-done = bf16[32,16384]{1,0:T(8,128)(2,1)} async-done(((bf16[256,16384]{1,0:T(8,128)(2,1)}), bf16[32,16384]{1,0:T(8,128)(2,1)}) %reduce-scatter.17.cloned.1.call-update) | async-done | bytes 1048592
  1345.2 39.4 %all-reduce.14 = (f32[6,128]{1,0:T(8,128)S(1)}, f32[6,128]{1,0:T(8,128)S(1)}) all-reduce(f32[6,128]{1,0:T(8,128)S(1)} %convolution_bitcast_fusion.3, f32[6,128]{1,0:T(8,128)S(1)} %stack.27), channel_id=1, replica_groups=mesh['row'=8,'col'=4] {'row','col'}, use_global_device_ids=true, to_apply=%region_37.38 | all-reduce | flops 1536 | bytes 12288 | tf_op jit(solution)/shard_map/psum | solution.py:420
  1385.2 85.5 %all-reduce.17.cloned.1.call-done = f32[17,128,128]{2,1,0:T(8,128)} async-done(((f32[17,128,128]{2,1,0:T(8,128)}), f32[17,128,128]{2,1,0:T(8,128)}) %all-reduce.17.cloned.1.call-update) | async-done | bytes 1114128 | tf_op jit(solution)/shard_map/psum | solution.py:420
  (426 shorter events, 392.3 us)
Async XLA Ops:
  7.2 535.2 %copy-start = (f32[2,6,256]{2,0,1:T(2,128)S(1)}, f32[2,6,256]{2,0,1:T(2,128)}, u32[]{:S(2)}) copy-start(f32[2,6,256]{2,0,1:T(2,128)} %param.16) | copy-start | bytes 36868
  7.2 198.3 %all-gather.8.cloned.1.call-start = ((), (), s32[]{:S(2)}) async-start(), calls=%async_computation.5 | async-start | bytes 9437184 | tf_op jit(solution)/shard_map/all_gather | solution.py:22
  37.8 259.6 %copy-start.108 = (f32[128]{0:T(128)}, f32[128]{0:T(128)S(1)}, u32[]{:S(2)}) copy-start(f32[128]{0:T(128)S(1)} %get-tuple-element.118) | copy-start | bytes 1540
  37.8 266.5 %copy-start.102 = (f32[128]{0:T(128)}, f32[128]{0:T(128)S(1)}, u32[]{:S(2)}) copy-start(f32[128]{0:T(128)S(1)} %get-tuple-element.117) | copy-start | bytes 1540
  37.8 630.8 %copy-start.111 = (f32[128]{0:T(128)}, f32[128]{0:T(128)S(1)}, u32[]{:S(2)}) copy-start(f32[128]{0:T(128)S(1)} %get-tuple-element.114) | copy-start | bytes 1540
  74.6 232.2 %copy-start.51 = (f32[2,32,64]{2,1,0:T(8,128)}, f32[2,32,64]{2,1,0:T(8,128)S(1)}, u32[]{:S(2)}) copy-start(f32[2,32,64]{2,1,0:T(8,128)S(1)} %broadcast_multiply_fusion.1) | copy-start | bytes 49156
  81.0 211.2 %reduce-scatter.9.cloned.1.call-start = ((), (), s32[]{:S(2)}) async-start(), calls=%async_computation.6 | async-start | bytes 5242880 | tf_op jit(solution)/shard_map/reduce_scatter | solution.py:30
  85.0 144.5 %copy-start.13 = (bf16[2,32,64,128]{2,1,3,0:T(8,128)(2,1)}, bf16[2,32,64,128]{2,1,3,0:T(8,128)(2,1)S(1)}, u32[]{:S(2)}) copy-start(bf16[2,32,64,128]{2,1,3,0:T(8,128)(2,1)S(1)} %copy.424) | copy-start | bytes 3145732
  249.4 96.3 %all-gather.10.cloned.1.call-start = ((), (), s32[]{:S(2)}) async-start(), calls=%async_computation.7 | async-start | bytes 5242880 | tf_op jit(solution)/shard_map/all_gather | solution.py:26
  303.0 226.3 %copy-start.5 = (f32[2,32,64,128]{3,2,1,0:T(8,128)}, f32[2,32,64,128]{3,2,1,0:T(8,128)S(1)}, u32[]{:S(2)}) copy-start(f32[2,32,64,128]{3,2,1,0:T(8,128)S(1)} %get-tuple-element.85) | copy-start | bytes 6291460
  311.1 213.8 %reduce-scatter.11.cloned.1.call-start = ((), (), s32[]{:S(2)}) async-start(), calls=%async_computation.8 | async-start | bytes 9437184 | tf_op jit(solution)/shard_map/reduce_scatter | solution.py:39
  375.7 224.1 %all-gather.12.cloned.1.call-start = ((), (), s32[]{:S(2)}) async-start(), calls=%async_computation.9 | async-start | bytes 10485760 | tf_op jit(solution)/shard_map/all_gather | solution.py:26
  377.2 158.1 %copy-start.68 = (bf16[128,4,128]{0,2,1:T(8,128)(2,1)}, bf16[128,4,128]{0,2,1:T(8,128)(2,1)S(1)}, u32[]{:S(2)}) copy-start(bf16[128,4,128]{0,2,1:T(8,128)(2,1)S(1)} %copy.437) | copy-start | bytes 393220
  526.8 310.1 %copy-start.60 = (f32[2,32,64]{2,1,0:T(8,128)}, f32[2,32,64]{2,1,0:T(8,128)S(1)}, u32[]{:S(2)}) copy-start(f32[2,32,64]{2,1,0:T(8,128)S(1)} %broadcast_multiply_fusion.4) | copy-start | bytes 49156
  529.2 307.7 %copy-start.75 = (f32[2,32,64]{2,1,0:T(8,128)}, f32[2,32,64]{2,1,0:T(8,128)S(1)}, u32[]{:S(2)}) copy-start(f32[2,32,64]{2,1,0:T(8,128)S(1)} %fusion.120) | copy-start | bytes 49156
  542.3 269.6 %reduce-scatter.13.cloned.1.call-start = ((), (), s32[]{:S(2)}) async-start(), calls=%async_computation.10 | async-start | bytes 10485760 | tf_op jit(solution)/shard_map/reduce_scatter | solution.py:272
  671.3 149.7 %copy-start.77 = (f32[2,32,64]{2,1,0:T(8,128)}, f32[2,32,64]{2,1,0:T(8,128)S(1)}, u32[]{:S(2)}) copy-start(f32[2,32,64]{2,1,0:T(8,128)S(1)} %negate_multiply_fusion.4) | copy-start | bytes 49156
  739.0 227.4 %all-gather.14.cloned.1.call-start = ((), (), s32[]{:S(2)}) async-start(), calls=%async_computation.11 | async-start | bytes 9437184 | tf_op jit(solution)/shard_map/all_gather | solution.py:22
  841.2 210.9 %reduce-scatter.15.cloned.1.call-start = ((), (), s32[]{:S(2)}) async-start(), calls=%async_computation.12 | async-start | bytes 5242880 | tf_op jit(solution)/shard_map/reduce_scatter | solution.py:30
  1009.3 106.8 %all-gather.16.cloned.1.call-start = ((), (), s32[]{:S(2)}) async-start(), calls=%async_computation.13 | async-start | bytes 5242880 | tf_op jit(solution)/shard_map/all_gather | solution.py:26
  1081.4 237.5 %reduce-scatter.17.cloned.1.call-start = ((), (), s32[]{:S(2)}) async-start(), calls=%async_computation.15 | async-start | bytes 9437184
  1170.4 300.4 %all-reduce.17.cloned.1.call-start = ((), (), s32[]{:S(2)}) async-start(), calls=%async_computation.14 | async-start | bytes 2228224 | tf_op jit(solution)/shard_map/psum | solution.py:420
  1341.3 129.5 %copy-start.65 = (f32[17,16,128]{2,1,0:T(8,128)S(1)}, f32[17,16,128]{2,1,0:T(8,128)}, u32[]{:S(2)}) copy-start(f32[17,16,128]{2,1,0:T(8,128)} %param.21) | copy-start | bytes 417796
  1341.3 131.2 %copy-start.1 = (f32[2,6,256]{2,0,1:T(2,128)S(1)}, f32[2,6,256]{2,0,1:T(2,128)}, u32[]{:S(2)}) copy-start(f32[2,6,256]{2,0,1:T(2,128)} %param.16) | copy-start | bytes 36868
  (118 other events, 1790.9 us)
Sparse Core Ops, SparseCore 0:
  81.1 124.3 all-gather.7
  249.5 42.6 reduce-scatter.8
  311.2 34.4 all-gather.9
  375.8 149.0 reduce-scatter.10
  542.4 57.2 all-gather.11
  739.1 72.7 reduce-scatter.12
  841.4 124.9 all-gather.13
  1009.4 42.6 reduce-scatter.14
  1081.5 34.4 all-gather.15
  1170.5 148.3 reduce-scatter.16
  1341.2 129.4 all-reduce.16
where the time goes:
time: 1490 us; the launch traced here: 1480 us
  waiting for transfers between devices  785 us (53%)
  local copies, waits for them, and re-layouts  222 us (15%)
  matrix products  187 us (13%)
  blocking collectives  159 us (11%)
  other arithmetic  109 us (7%)
  between operations  16.6 us (1%)
    all_gather x2, waiting for transfers between devices, row_panels(): return lax.all_gather(values, 'row', axis=1, tiled=True)  246 us
    reduce_scatter x1, waiting for transfers between devices, row_sums(): lax.psum_scatter(partial_term(jnp.int32(0), row_total * lax.axis_size('ro...  148 us
    unnamed x12, waiting for transfers between devices  92 us
    all_gather x3, waiting for transfers between devices, col_panels(): return lax.all_gather(values, 'col', axis=2, tiled=True)  87.1 us
    psum x1, waiting for transfers between devices, per_device(): lax.psum((grad_mats, grad_struct, grad_gains), ('row', 'col'))  85.5 us
    reduce_scatter x2, waiting for transfers between devices, col_sums(): lax.psum_scatter(partial_term(jnp.int32(0), row_total * lax.axis_size('co...  68.1 us
    reduce_scatter x1, waiting for transfers between devices, attn_back(): lax.psum_scatter(grad_joined.astype(jnp.bfloat16), 'col', scatter_dimensi...  58.8 us
    unnamed x271, local copies, waits for them, and re-layouts  55.8 us
  transfers between devices with their start and end apart: 11, of which 11 were waited for; matrix products, arithmetic and copies ran while one was open for 6% of the time, Pallas kernels for 0%

commit v1 on v0

v1 whole, which is shorter than its diff:
```python
import functools

import jax
import jax.numpy as jnp
from jax import lax
from jax.experimental import pallas as pl
from jax.experimental.pallas import tpu as pltpu
from jax.sharding import PartitionSpec as P

NH = 4
STEP = 5
BETA_ONE = 0.5
BETA_TWO = 0.5
ADAM_EPS = 1e-08
N_MATS = 17
N_GAINS = 6
STRUCT_LANE = 8
LOSS_LANE = 32

F32 = jnp.float32
BF16 = jnp.bfloat16
MESH = pl.DeviceIdType.MESH
VMEM_LIMIT = 60 * 2**20
NN = ((1,), (0,))
NT = ((1,), (1,))
TN = ((0,), (0,))


def dot(left, right, contract=NN):
    return lax.dot_general(left, right, (contract, ((), ())), preferred_element_type=F32)


class Plan:
    def __init__(self, mesh, pair, weights):
        self.rows, self.cols = mesh.shape["row"], mesh.shape["col"]
        self.half_rows = self.rows // 2
        self.members = self.half_rows * self.cols
        self.crops, self.length, _, self.channels = pair
        self.own_rows = self.length // self.members
        self.own_channels = self.channels // self.members
        self.block_rows = self.length // self.rows
        self.block_cols = self.length // self.cols
        self.pieces = self.block_rows // self.own_rows
        self.shard = self.channels // self.rows
        self.group_mats = -(-(N_MATS + 2) // self.cols)
        self.mats = self.group_mats * self.cols

    def here(self):
        row, col = lax.axis_index("row"), lax.axis_index("col")
        half = row // self.half_rows
        return row, col, half, (row % self.half_rows) * self.cols + col

    def member(self, half, index):
        return (half * self.half_rows + index // self.cols, index % self.cols)


def layer_norm(values):
    center = values - jnp.mean(values, axis=0, keepdims=True)
    scale = lax.rsqrt(jnp.mean(center * center, axis=0, keepdims=True) + 1e-05)
    return center * scale, scale


def layer_norm_back(grad, normed, scale, gain):
    inner = grad * gain
    mean_one = jnp.mean(inner, axis=0, keepdims=True)
    mean_two = jnp.mean(inner * normed, axis=0, keepdims=True)
    return scale * (inner - mean_one - normed * mean_two)


def lane_fold(values):
    total = values[:, :128]
    for start in range(128, values.shape[1], 128):
        total = total + values[:, start : start + 128]
    return total


def group_barrier(plan, half, me):
    barrier = pltpu.get_barrier_semaphore()

    def signal(off, carry):
        pl.semaphore_signal(
            barrier,
            inc=1,
            device_id=plan.member(half, (me + off) % plan.members),
            device_id_type=MESH,
        )
        return carry

    lax.fori_loop(1, plan.members, signal, 0)
    pl.semaphore_wait(barrier, plan.members - 1)


def swap_copy(plan, half, me, off, src, dst, send, recv):
    to = (me + off) % plan.members
    return pltpu.make_async_remote_copy(
        src_ref=src.at[to],
        dst_ref=dst.at[me],
        send_sem=send.at[off],
        recv_sem=recv.at[off],
        device_id=plan.member(half, to),
        device_id_type=MESH,
    )


def swap_start(plan, half, me, src, dst, send, recv, local):
    def start(off, carry):
        swap_copy(plan, half, me, off, src, dst, send, recv).start()
        return carry

    lax.fori_loop(1, plan.members, start, 0)
    pltpu.make_async_copy(src.at[me], dst.at[me], local).start()


def swap_wait(plan, half, me, src, dst, send, recv, local):
    def wait(off, carry):
        swap_copy(plan, half, me, off, src, dst, send, recv).wait()
        return carry

    lax.fori_loop(1, plan.members, wait, 0)
    pltpu.make_async_copy(src.at[me], dst.at[me], local).wait()


def enter_kernel(
    plan, pair, near, mats, pair_out, near_out, mats_out, sends, recvs, near_sends, near_recvs, mat_sems
):
    row, col, half, me = plan.here()
    own, cols, pieces, width = plan.own_rows, plan.cols, plan.pieces, plan.block_cols
    source = me // pieces
    other = (1 - half) * plan.half_rows + row % plan.half_rows
    barrier = pltpu.get_barrier_semaphore()

    def greet(off, carry):
        index = (row * cols + col + off) % (plan.rows * cols)
        pl.semaphore_signal(
            barrier, inc=1, device_id=(index // cols, index % cols), device_id_type=MESH
        )
        return carry

    lax.fori_loop(1, plan.rows * cols, greet, 0)
    pl.semaphore_wait(barrier, plan.rows * cols - 1)

    first = pl.ds(col * plan.group_mats, plan.group_mats)
    cross = pltpu.make_async_remote_copy(
        src_ref=mats.at[first],
        dst_ref=mats_out.at[row, first],
        send_sem=mat_sems.at[0],
        recv_sem=mat_sems.at[1],
        device_id=(other, col),
        device_id_type=MESH,
    )
    cross.start()
    mine = pltpu.make_async_copy(mats.at[first], mats_out.at[row, first], mat_sems.at[2])
    mine.start()

    def targets():
        for crop in range(plan.crops):
            for piece in range(pieces):
                index = row * pieces + piece
                yield crop, piece, (crop * plan.half_rows + index // cols, index % cols)

    def block(crop, piece, to):
        slot = crop * pieces + piece
        there = pl.ds(pl.multiple_of(col * width, width), width)
        return (
            pltpu.make_async_remote_copy(
                src_ref=pair.at[crop, pl.ds(piece * own, own)],
                dst_ref=pair_out.at[:, there],
                send_sem=sends.at[slot],
                recv_sem=recvs.at[col],
                device_id=to,
                device_id_type=MESH,
            ),
            pltpu.make_async_remote_copy(
                src_ref=near.at[crop, piece],
                dst_ref=near_out.at[col],
                send_sem=near_sends.at[slot],
                recv_sem=near_recvs.at[col],
                device_id=to,
                device_id_type=MESH,
            ),
        )

    def local(crop, piece):
        slot = crop * pieces + piece
        there = pl.ds(pl.multiple_of(col * width, width), width)
        return (
            pltpu.make_async_copy(
                pair.at[crop, pl.ds(piece * own, own)], pair_out.at[:, there], sends.at[slot]
            ),
            pltpu.make_async_copy(near.at[crop, piece], near_out.at[col], near_sends.at[slot]),
        )

    for crop, piece, to in targets():
        stays = jnp.logical_and(to[0] == row, to[1] == col)

        @pl.when(stays)
        def _():
            for copy in local(crop, piece):
                copy.start()

        @pl.when(jnp.logical_not(stays))
        def _():
            for copy in block(crop, piece, to):
                copy.start()

    cross.wait()
    mine.wait()

    def share(off, slot):
        to = (me + off) % plan.members
        shard = slot * plan.half_rows + row % plan.half_rows
        return pltpu.make_async_remote_copy(
            src_ref=mats_out.at[shard, first],
            dst_ref=mats_out.at[shard, first],
            send_sem=mat_sems.at[3 + slot * plan.members + off],
            recv_sem=mat_sems.at[3 + (2 + slot) * plan.members + off],
            device_id=plan.member(half, to),
            device_id_type=MESH,
        )

    def taken(off, slot):
        origin = (me - off + plan.members) % plan.members
        shard = slot * plan.half_rows + origin // cols
        part = pl.ds((origin % cols) * plan.group_mats, plan.group_mats)
        return pltpu.make_async_remote_copy(
            src_ref=mats_out.at[shard, part],
            dst_ref=mats_out.at[shard, part],
            send_sem=mat_sems.at[3 + slot * plan.members + off],
            recv_sem=mat_sems.at[3 + (2 + slot) * plan.members + off],
            device_id=plan.member(half, origin),
            device_id_type=MESH,
        )

    def pass_on(off, carry):
        for slot in range(2):
            share(off, slot).start()
        return carry

    lax.fori_loop(1, plan.members, pass_on, 0)

    def settle(off, carry):
        for slot in range(2):
            share(off, slot).wait_send()
            taken(off, slot).wait_recv()
        return carry

    lax.fori_loop(1, plan.members, settle, 0)

    for crop, piece, to in targets():
        stays = jnp.logical_and(to[0] == row, to[1] == col)

        @pl.when(stays)
        def _():
            for copy in local(crop, piece):
                copy.wait()

        @pl.when(jnp.logical_not(stays))
        def _():
            for copy in block(crop, piece, to):
                copy.wait_send()

    for origin in range(cols):
        there = pl.ds(origin * width, width)

        @pl.when(jnp.logical_not(jnp.logical_and(source == row, col == origin)))
        def _():
            pltpu.make_async_remote_copy(
                src_ref=pair_out.at[:, there],
                dst_ref=pair_out.at[:, there],
                send_sem=sends.at[0],
                recv_sem=recvs.at[origin],
                device_id=(source, origin),
                device_id_type=MESH,
            ).wait_recv()
            pltpu.make_async_remote_copy(
                src_ref=near_out.at[origin],
                dst_ref=near_out.at[origin],
                send_sem=near_sends.at[0],
                recv_sem=near_recvs.at[origin],
                device_id=(source, origin),
                device_id_type=MESH,
            ).wait_recv()


def enter(plan, pair, near, mats):
    anywhere = pl.BlockSpec(memory_space=pl.ANY)
    slots = plan.crops * plan.pieces
    dma = pltpu.SemaphoreType.DMA
    return pl.pallas_call(
        functools.partial(enter_kernel, plan),
        out_shape=(
            jax.ShapeDtypeStruct((plan.own_rows, plan.length, plan.channels), BF16),
            jax.ShapeDtypeStruct((plan.cols,) + near.shape[2:], near.dtype),
            jax.ShapeDtypeStruct((plan.rows,) + mats.shape, BF16),
        ),
        in_specs=[anywhere] * 3,
        out_specs=(anywhere,) * 3,
        scratch_shapes=[
            dma((slots,)),
            dma((plan.cols,)),
            dma((slots,)),
            dma((plan.cols,)),
            dma((3 + 4 * plan.members,)),
        ],
        compiler_params=pltpu.CompilerParams(collective_id=0, has_side_effects=True),
    )(pair, near, mats)


def square(plan, ref, index):
    return ref[index].reshape(plan.length, plan.length)


def product_kernel(plan, outgoing, parts, full, result, staged, *sems):
    _, _, half, me = plan.here()
    group_barrier(plan, half, me)
    swap_start(plan, half, me, parts, full, *sems[:3])
    swap_wait(plan, half, me, parts, full, *sems[:3])

    def channel(h, carry):
        left = full[:, 0, h].reshape(plan.length, plan.length)
        right = full[:, 1, h].reshape(plan.length, plan.length)
        value = dot(left, right, NT if outgoing else TN)
        staged[:, h] = value.astype(BF16).reshape(plan.members, plan.own_rows, plan.length)
        return carry

    lax.fori_loop(0, plan.own_channels, channel, 0)
    swap_start(plan, half, me, staged, result, *sems[3:])
    swap_wait(plan, half, me, staged, result, *sems[3:])


def product_back_kernel(plan, outgoing, parts, full, result, gathered, staged, *sems):
    _, _, half, me = plan.here()
    group_barrier(plan, half, me)
    swap_start(plan, half, me, parts, gathered, *sems[:3])
    swap_wait(plan, half, me, parts, gathered, *sems[:3])
    blocks = (plan.members, plan.own_rows, plan.length)

    def channel(h, carry):
        left = full[:, 0, h].reshape(plan.length, plan.length)
        right = full[:, 1, h].reshape(plan.length, plan.length)
        grad = gathered[:, h].reshape(plan.length, plan.length)
        if outgoing:
            grad_left, grad_right = dot(grad, right), dot(grad, left, TN)
        else:
            grad_left, grad_right = dot(right, grad, NT), dot(left, grad)
        staged[:, 0, h] = grad_left.astype(BF16).reshape(blocks)
        staged[:, 1, h] = grad_right.astype(BF16).reshape(blocks)
        return carry

    lax.fori_loop(0, plan.own_channels, channel, 0)
    swap_start(plan, half, me, staged, result, *sems[3:])
    swap_wait(plan, half, me, staged, result, *sems[3:])


def swap_sems(plan):
    dma = pltpu.SemaphoreType.DMA
    return [dma((plan.members,)), dma((plan.members,)), dma] * 2


def vmem(count):
    return [pl.BlockSpec(memory_space=pltpu.VMEM)] * count


def product(plan, parts, outgoing, collective_id):
    one = (plan.members, plan.own_channels, plan.own_rows, plan.length)
    return pl.pallas_call(
        functools.partial(product_kernel, plan, outgoing),
        out_shape=(jax.ShapeDtypeStruct(parts.shape, BF16), jax.ShapeDtypeStruct(one, BF16)),
        in_specs=vmem(1),
        out_specs=tuple(vmem(2)),
        scratch_shapes=[pltpu.VMEM(one, BF16)] + swap_sems(plan),
        compiler_params=pltpu.CompilerParams(
            collective_id=collective_id, has_side_effects=True, vmem_limit_bytes=VMEM_LIMIT
        ),
    )(parts)


def product_back(plan, parts, full, outgoing, collective_id):
    return pl.pallas_call(
        functools.partial(product_back_kernel, plan, outgoing),
        out_shape=jax.ShapeDtypeStruct(full.shape, BF16),
        in_specs=vmem(2),
        out_specs=vmem(1)[0],
        scratch_shapes=[pltpu.VMEM(parts.shape, BF16), pltpu.VMEM(full.shape, BF16)]
        + swap_sems(plan),
        compiler_params=pltpu.CompilerParams(
            collective_id=collective_id, has_side_effects=True, vmem_limit_bytes=VMEM_LIMIT
        ),
    )(parts, full)


def reduce_kernel(plan, grads, total, got, crossed, sent, *sems):
    row, col, half, me = plan.here()
    other = (1 - half) * plan.half_rows + row % plan.half_rows
    barrier = pltpu.get_barrier_semaphore()
    pl.semaphore_signal(barrier, inc=1, device_id=(other, col), device_id_type=MESH)

    def greet(off, carry):
        pl.semaphore_signal(
            barrier,
            inc=1,
            device_id=plan.member(half, (me + off) % plan.members),
            device_id_type=MESH,
        )
        return carry

    lax.fori_loop(1, plan.members, greet, 0)
    pl.semaphore_wait(barrier, plan.members)

    swap_start(plan, half, me, grads, got, *sems[:3])
    swap_wait(plan, half, me, grads, got, *sems[:3])
    sums = jnp.sum(got[...].astype(F32), axis=0)
    sent[...] = sums
    across, mine, theirs = sems[3], sems[4], sems[5]
    cross = pltpu.make_async_remote_copy(
        src_ref=sent.at[1 - half],
        dst_ref=crossed,
        send_sem=across.at[0],
        recv_sem=across.at[1],
        device_id=(other, col),
        device_id_type=MESH,
    )
    cross.start()
    cross.wait()
    total[col] = sent[half] + crossed[...]

    def gather(off, slot, to):
        return pltpu.make_async_remote_copy(
            src_ref=total.at[slot],
            dst_ref=total.at[slot],
            send_sem=mine.at[off],
            recv_sem=theirs.at[off],
            device_id=(row, to),
            device_id_type=MESH,
        )

    for off in range(1, plan.cols):
        gather(off, col, (col + off) % plan.cols).start()
    for off in range(1, plan.cols):
        origin = (col - off + plan.cols) % plan.cols
        gather(off, col, (col + off) % plan.cols).wait_send()
        gather(off, origin, origin).wait_recv()


def reduce_grads(plan, grads):
    dma = pltpu.SemaphoreType.DMA
    part = grads.shape[2:]
    return pl.pallas_call(
        functools.partial(reduce_kernel, plan),
        out_shape=jax.ShapeDtypeStruct((plan.cols,) + part, F32),
        in_specs=vmem(1),
        out_specs=vmem(1)[0],
        scratch_shapes=[
            pltpu.VMEM(grads.shape, BF16),
            pltpu.VMEM(part, F32),
            pltpu.VMEM((2,) + part, F32),
            dma((plan.members,)),
            dma((plan.members,)),
            dma,
            dma((2,)),
            dma((plan.cols,)),
            dma((plan.cols,)),
        ],
        compiler_params=pltpu.CompilerParams(
            collective_id=5, has_side_effects=True, vmem_limit_bytes=VMEM_LIMIT
        ),
    )(grads)


def whole_mat(plan, mats, index):
    return mats[:, index].astype(F32).reshape(plan.channels, plan.channels)


def fill_columns(plan, mats, numbers, into):
    for place, number in enumerate(numbers):
        into[place * plan.channels : (place + 1) * plan.channels, :] = whole_mat(
            plan, mats, number
        ).T.astype(BF16)


def fill_rows(plan, mats, numbers, into):
    for place, number in enumerate(numbers):
        into[:, place * plan.channels : (place + 1) * plan.channels] = whole_mat(
            plan, mats, number
        ).astype(BF16)


def fill_gains(plan, mats, numbers, into):
    extra = whole_mat(plan, mats, N_MATS)
    for place, number in enumerate(numbers):
        into[place] = jnp.broadcast_to(
            extra[:, number : number + 1], (plan.channels, plan.length)
        )


def pair_mask(plan, limits, i):
    _, _, half, me = plan.here()
    limit = limits[half]
    places = lax.broadcasted_iota(jnp.int32, (1, plan.length), 1)
    row_place = me * plan.own_rows + i
    return jnp.where(jnp.logical_and(places < limit, row_place < limit), 1.0, 0.0).astype(F32)


def to_channels(plan, rows):
    return jnp.swapaxes(rows, 0, 1).reshape(
        plan.members, plan.own_channels, plan.own_rows, plan.length
    )


def to_rows(plan, channels):
    return jnp.swapaxes(
        channels.reshape(plan.channels, plan.own_rows, plan.length), 0, 1
    )


def gated_sides(plan, low, into_side, mask):
    c = plan.channels
    projected = dot(into_side[: 4 * c, :], low)
    left = mask * jax.nn.sigmoid(projected[:c]) * projected[c : 2 * c]
    right = mask * jax.nn.sigmoid(projected[2 * c : 3 * c]) * projected[3 * c :]
    return left.astype(BF16), right.astype(BF16)


def first_kernel(plan, pair, mats, limits, state, parts, into_side, gain, left_rows, right_rows):
    fill_columns(plan, mats, range(4), into_side)
    fill_gains(plan, mats, (0,), gain)

    def body(i, carry):
        value = pair[i].astype(F32).T
        state[i] = value.astype(BF16)
        normed, _ = layer_norm(value)
        left, right = gated_sides(
            plan, (normed * gain[0]).astype(BF16), into_side, pair_mask(plan, limits, i)
        )
        left_rows[i] = left
        right_rows[i] = right
        return carry

    lax.fori_loop(0, plan.own_rows, body, 0)
    parts[:, 0] = to_channels(plan, left_rows[...])
    parts[:, 1] = to_channels(plan, right_rows[...])


def close_triangle(low, mixed_low, gate_side, out_side):
    gating = jax.nn.sigmoid(dot(gate_side[...], low))
    return gating, dot(out_side[...], mixed_low)


def middle_kernel(
    plan, product_in, state, mats, limits, state_out, product_rows, parts, gate_side, out_side,
    into_side, gains, left_rows, right_rows,
):
    fill_columns(plan, mats, (4,), gate_side)
    fill_columns(plan, mats, (5,), out_side)
    fill_columns(plan, mats, range(6, 10), into_side)
    fill_gains(plan, mats, (0, 1, 2), gains)
    product_rows[...] = to_rows(plan, product_in[...])

    def body(i, carry):
        before = state[i].astype(F32)
        normed, _ = layer_norm(before)
        mixed, _ = layer_norm(product_rows[i].astype(F32))
        gating, branch = close_triangle(
            (normed * gains[0]).astype(BF16), (mixed * gains[1]).astype(BF16), gate_side, out_side
        )
        after = before + gating * branch
        state_out[i] = after
        normed, _ = layer_norm(after)
        left, right = gated_sides(
            plan, (normed * gains[2]).astype(BF16), into_side, pair_mask(plan, limits, i)
        )
        left_rows[i] = left
        right_rows[i] = right
        return carry

    lax.fori_loop(0, plan.own_rows, body, 0)
    parts[:, 0] = to_channels(plan, left_rows[...])
    parts[:, 1] = to_channels(plan, right_rows[...])


def close_triangle_back(grad, gating, branch, mixed, scale, mixed_low, out_rows, gain, grad_out, grad_gain):
    grad_gate = (grad * branch * gating * (1.0 - gating)).astype(BF16)
    grad_branch = (grad * gating).astype(BF16)
    grad_out[...] += dot(mixed_low, grad_branch, NT)
    grad_mixed = dot(out_rows[...], grad_branch)
    grad_gain[...] += lane_fold(grad_mixed * mixed)
    return grad_gate, layer_norm_back(grad_mixed, mixed, scale, gain).astype(BF16)


def open_triangle_back(plan, grads, low, into_side, in_rows, mask, grad_in, grad_sides):
    c = plan.channels
    grad_left, grad_right, grad_gate = grads
    projected = dot(into_side[: 4 * c, :], low)
    left_gate = jax.nn.sigmoid(projected[:c])
    right_gate = jax.nn.sigmoid(projected[2 * c : 3 * c])
    grad_left = mask * grad_left.astype(F32)
    grad_right = mask * grad_right.astype(F32)
    shared = grad_left * left_gate
    grad_sides[:c, :] = (shared * projected[c : 2 * c] * (1.0 - left_gate)).astype(BF16)
    grad_sides[c : 2 * c, :] = shared.astype(BF16)
    shared = grad_right * right_gate
    grad_sides[2 * c : 3 * c, :] = (shared * projected[3 * c :] * (1.0 - right_gate)).astype(BF16)
    grad_sides[3 * c : 4 * c, :] = shared.astype(BF16)
    grad_sides[4 * c :, :] = grad_gate
    grad_in[...] += dot(low, grad_sides[...], NT)
    return dot(in_rows[...], grad_sides[...])


def attend_kernel(
    plan, product_in, state, mats, limits, near, frames, target, motif,
    grad_state, grad_gate, parts, grad_attend, grad_attend_out, grad_out, grad_gains, grad_struct, losses,
    product_rows, grad_rows, gate_side, out_side, out_rows, attend_side, attend_rows, last_side, last_rows,
    struct, gains, counts, places_bias, query, keys, values, probs, attended, grad_sides,
):
    c, length, depth = plan.channels, plan.length, plan.channels // NH
    _, _, half, me = plan.here()
    fill_columns(plan, mats, (10,), gate_side)
    fill_columns(plan, mats, (11,), out_side)
    fill_rows(plan, mats, (11,), out_rows)
    fill_columns(plan, mats, range(12, 16), attend_side)
    fill_rows(plan, mats, range(12, 16), attend_rows)
    fill_columns(plan, mats, (16,), last_side)
    fill_rows(plan, mats, (16,), last_rows)
    fill_gains(plan, mats, (2, 3, 4, 5), gains)
    struct[...] = whole_mat(plan, mats, N_MATS).T[STRUCT_LANE : STRUCT_LANE + 16].astype(BF16)
    product_rows[...] = to_rows(plan, product_in[...])

    limit = limits[half]
    key_places = lax.broadcasted_iota(jnp.int32, (length, 128), 0)
    places_bias[...] = jnp.where(key_places < limit, 0.0, -1e9).astype(F32)
    lists = near[0]
    row_places = lax.broadcasted_iota(jnp.int32, (plan.own_rows, length), 1)
    total = jnp.zeros((plan.own_rows, length), F32)
    for entry in range(lists.shape[1]):
        total += jnp.where(lists[:, entry : entry + 1] == row_places, 1.0, 0.0).astype(F32)
    counts[...] = total

    places = lax.broadcasted_iota(jnp.int32, (1, length), 1)
    counted = jnp.zeros((1, length), F32)
    for crop in range(plan.crops):
        counted += jnp.where(places < limits[crop], 1.0, 0.0).astype(F32) * (
            1 - motif[crop : crop + 1, :]
        ).astype(F32)
    loss_count = jnp.sum(counted, axis=1, keepdims=True)
    weight_row = jnp.where(places < limit, 1.0, 0.0).astype(F32) * (
        1 - motif[pl.ds(half, 1), :]
    ).astype(F32)
    spare = jnp.zeros((16 - frames.shape[1], length), F32)
    frames_all = jnp.concatenate([frames[half], spare], axis=0)
    target_all = jnp.concatenate([target[half], spare], axis=0)

    for ref in (grad_attend, grad_attend_out, grad_out, grad_gains, grad_struct, losses):
        ref[...] = jnp.zeros_like(ref)

    def body(i, carry):
        before = state[i]
        normed, _ = layer_norm(before)
        mixed, mixed_scale = layer_norm(product_rows[i].astype(F32))
        mixed_low = (mixed * gains[1]).astype(BF16)
        gating, branch = close_triangle(
            (normed * gains[0]).astype(BF16), mixed_low, gate_side, out_side
        )
        held = before + gating * branch

        held_normed, held_scale = layer_norm(held)
        held_low = (held_normed * gains[2]).astype(BF16)
        projected = dot(attend_side[...], held_low)
        query[...] = (projected[:c] * depth ** (-0.5)).astype(BF16)
        keys[...] = projected[c : 2 * c].astype(BF16)
        values[...] = projected[2 * c : 3 * c].astype(BF16)
        attend_gate = jax.nn.sigmoid(projected[3 * c :])
        bias = jnp.concatenate([places_bias[...]] * (length // 128), axis=1)
        for head in range(NH):
            part = slice(head * depth, (head + 1) * depth)
            scores = dot(keys[part, :], query[part, :], TN) + bias
            powers = jnp.exp(scores - jnp.max(scores, axis=0, keepdims=True))
            share = powers * (1.0 / jnp.sum(powers, axis=0, keepdims=True))
            probs[head] = share
            attended[part, :] = dot(values[part, :], share.astype(BF16))
        gated_low = (attended[...] * attend_gate).astype(BF16)
        last = held + dot(last_side[...], gated_low)

        last_normed, last_scale = layer_norm(last)
        last_low = (last_normed * gains[3]).astype(BF16)
        edges = dot(struct[...], last_low)
        here = places == me * plan.own_rows + i
        frame_here = jnp.sum(jnp.where(here, frames_all, 0.0), axis=1, keepdims=True)
        target_here = jnp.sum(jnp.where(here, target_all, 0.0), axis=1, keepdims=True)
        weight_here = jnp.sum(jnp.where(here, weight_row, 0.0), axis=1, keepdims=True)
        weighted = counts[pl.ds(i, 1), :] * (frames_all - frame_here)
        residual = frame_here + jnp.sum(weighted * edges, axis=1, keepdims=True) - target_here
        lost = weight_here * residual * residual
        losses[0:1, :] += jnp.broadcast_to(jnp.sum(lost, axis=0, keepdims=True), (1, 128))
        grad_update = 2.0 * residual * (weight_here * (1.0 / loss_count))
        grad_edges = (grad_update * weighted).astype(BF16)
        grad_struct[...] += dot(grad_edges, last_low, NT)
        grad_low = dot(struct[...], grad_edges, TN)
        grad_gains[2] += lane_fold(grad_low * last_normed)
        grad_last = layer_norm_back(grad_low, last_normed, last_scale, gains[3])

        grad_branch = grad_last.astype(BF16)
        grad_attend_out[...] += dot(gated_low, grad_branch, NT)
        grad_gated = dot(last_rows[...], grad_branch)
        grad_sides[3 * c :, :] = (
            grad_gated * attended[...] * attend_gate * (1.0 - attend_gate)
        ).astype(BF16)
        grad_att = (grad_gated * attend_gate).astype(BF16)
        for head in range(NH):
            part = slice(head * depth, (head + 1) * depth)
            share = probs[head]
            grad_share = dot(values[part, :], grad_att[part, :], TN)
            weighed = share * grad_share
            grad_scores = (weighed - share * jnp.sum(weighed, axis=0, keepdims=True)).astype(BF16)
            grad_sides[part, :] = (dot(keys[part, :], grad_scores) * depth ** (-0.5)).astype(BF16)
            grad_sides[c + head * depth : c + (head + 1) * depth, :] = dot(
                query[part, :], grad_scores, NT
            ).astype(BF16)
            grad_sides[2 * c + head * depth : 2 * c + (head + 1) * depth, :] = dot(
                grad_att[part, :], share.astype(BF16), NT
            ).astype(BF16)
        grad_attend[...] += dot(held_low, grad_sides[...], NT)
        grad_low = dot(attend_rows[...], grad_sides[...])
        grad_gains[1] += lane_fold(grad_low * held_normed)
        grad_held = grad_last + layer_norm_back(grad_low, held_normed, held_scale, gains[2])
        grad_state[i] = grad_held

        grad_gate[i], grad_rows[i] = close_triangle_back(
            grad_held, gating, branch, mixed, mixed_scale, mixed_low, out_rows, gains[1],
            grad_out, grad_gains.at[0],
        )
        return carry

    lax.fori_loop(0, plan.own_rows, body, 0)
    losses[1:2, :] = jnp.broadcast_to(loss_count, (1, 128))
    parts[...] = to_channels(plan, grad_rows[...])


def turn_kernel(
    plan, grad_parts, grad_after, grad_gate, state, first_state, product_rows, mats, limits,
    grad_gate_out, parts, grad_in, grad_out, grad_gains,
    left_rows, right_rows, grad_rows, into_side, in_rows, gate_side, out_side, out_rows, gains, grad_sides,
):
    fill_columns(plan, mats, range(6, 10), into_side)
    fill_rows(plan, mats, range(6, 11), in_rows)
    fill_columns(plan, mats, (4,), gate_side)
    fill_columns(plan, mats, (5,), out_side)
    fill_rows(plan, mats, (5,), out_rows)
    fill_gains(plan, mats, (0, 1, 2), gains)
    left_rows[...] = to_rows(plan, grad_parts[:, 0])
    right_rows[...] = to_rows(plan, grad_parts[:, 1])
    for ref in (grad_in, grad_out, grad_gains):
        ref[...] = jnp.zeros_like(ref)

    def body(i, carry):
        normed, scale = layer_norm(state[i])
        low = (normed * gains[2]).astype(BF16)
        grad_low = open_triangle_back(
            plan, (left_rows[i], right_rows[i], grad_gate[i]), low, into_side, in_rows,
            pair_mask(plan, limits, i), grad_in, grad_sides,
        )
        grad_gains[1] += lane_fold(grad_low * normed)
        grad = grad_after[i] + layer_norm_back(grad_low, normed, scale, gains[2])

        normed, _ = layer_norm(first_state[i].astype(F32))
        mixed, mixed_scale = layer_norm(product_rows[i].astype(F32))
        mixed_low = (mixed * gains[1]).astype(BF16)
        gating, branch = close_triangle(
            (normed * gains[0]).astype(BF16), mixed_low, gate_side, out_side
        )
        grad_gate_out[i], grad_rows[i] = close_triangle_back(
            grad, gating, branch, mixed, mixed_scale, mixed_low, out_rows, gains[1],
            grad_out, grad_gains.at[0],
        )
        return carry

    lax.fori_loop(0, plan.own_rows, body, 0)
    parts[...] = to_channels(plan, grad_rows[...])


def last_kernel(
    plan, grad_parts, grad_gate, first_state, mats, limits,
    attend_in, attend_out, second_out, gains_late, grad_struct, losses,
    second_in, first_out, gains_mid,
    packed,
    left_rows, right_rows, into_side, in_rows, gain, grad_sides, grad_in, grad_gain,
):
    c = plan.channels
    fill_columns(plan, mats, range(4), into_side)
    fill_rows(plan, mats, range(5), in_rows)
    fill_gains(plan, mats, (0,), gain)
    left_rows[...] = to_rows(plan, grad_parts[:, 0])
    right_rows[...] = to_rows(plan, grad_parts[:, 1])
    for ref in (grad_in, grad_gain):
        ref[...] = jnp.zeros_like(ref)

    def body(i, carry):
        normed, _ = layer_norm(first_state[i].astype(F32))
        grad_low = open_triangle_back(
            plan, (left_rows[i], right_rows[i], grad_gate[i]), (normed * gain[0]).astype(BF16),
            into_side, in_rows, pair_mask(plan, limits, i), grad_in, grad_sides,
        )
        grad_gain[...] += lane_fold(grad_low * normed)
        return carry

    lax.fori_loop(0, plan.own_rows, body, 0)

    def put(number, value):
        group, place = number // plan.group_mats, number % plan.group_mats
        blocks = value.reshape(2, plan.half_rows, plan.shard, c)
        for near_half in range(2):
            for row in range(plan.half_rows):
                packed[row * plan.cols + group, near_half, place] = blocks[near_half, row].astype(BF16)

    for m in range(5):
        put(m, grad_in[:, m * c : (m + 1) * c])
        put(6 + m, second_in[:, m * c : (m + 1) * c])
    put(5, first_out[...])
    put(11, second_out[...])
    for m in range(4):
        put(12 + m, attend_in[:, m * c : (m + 1) * c])
    put(16, attend_out[...])

    lanes = lax.broadcasted_iota(jnp.int32, (c, 128), 1)
    extra = jnp.zeros((c, 128), F32)
    by_gain = (grad_gain[...], gains_mid[0], gains_mid[1], gains_late[0], gains_late[1], gains_late[2])
    for m, value in enumerate(by_gain):
        extra += jnp.where(lanes == m, jnp.sum(value, axis=1, keepdims=True), 0.0)
    padded = jnp.concatenate(
        [jnp.zeros((STRUCT_LANE, c), F32), grad_struct[...], jnp.zeros((128 - STRUCT_LANE - 16, c), F32)],
        axis=0,
    )
    extra += padded.T
    extra += jnp.where(lanes == LOSS_LANE, losses[0:1, :], 0.0)
    high = extra.astype(BF16)
    put(N_MATS, high.astype(F32))
    put(N_MATS + 1, extra - high.astype(F32))
    for number in range(N_MATS + 2, plan.mats):
        put(number, jnp.zeros((c, c), F32))


def local_call(kernel, plan, args, outs, scratch, flops):
    specs = [
        pl.BlockSpec(memory_space=pltpu.SMEM if value.ndim == 1 else pltpu.VMEM) for value in args
    ]
    many = isinstance(outs, (list, tuple)) and not isinstance(outs, jax.ShapeDtypeStruct)
    return pl.pallas_call(
        functools.partial(kernel, plan),
        out_shape=tuple(outs) if many else outs,
        in_specs=specs,
        out_specs=tuple(vmem(len(outs))) if many else vmem(1)[0],
        scratch_shapes=scratch,
        compiler_params=pltpu.CompilerParams(vmem_limit_bytes=VMEM_LIMIT),
    )(*args)


def adam_update(param, first, second, gradient, rate, decay):
    first_new = BETA_ONE * first + (1.0 - BETA_ONE) * gradient
    second_new = BETA_TWO * second + (1.0 - BETA_TWO) * gradient * gradient
    first_hat = first_new / (1.0 - BETA_ONE**STEP)
    second_hat = second_new / (1.0 - BETA_TWO**STEP)
    return (
        first_new,
        second_new,
        param - rate * (first_hat / (jnp.sqrt(second_hat) + ADAM_EPS) + decay * param),
    )


def per_device(
    plan, pair, frames, target, lengths, motif, neighbours, weights, weights_m, weights_v,
    struct_w, struct_m, struct_v, gains, gains_m, gains_v,
):
    rows, c, length, shard = plan.own_rows, plan.channels, plan.length, plan.shard
    sds = jax.ShapeDtypeStruct
    extra = jnp.zeros((plan.mats - N_MATS, shard, c), F32)
    extra = extra.at[0, :, :N_GAINS].set(gains.T)
    extra = extra.at[0, :, STRUCT_LANE : STRUCT_LANE + struct_w.shape[0]].set(struct_w.T)
    mats_own = jnp.concatenate([weights.astype(BF16), extra.astype(BF16)], axis=0)
    near = neighbours.reshape(plan.crops, plan.pieces, rows, neighbours.shape[-1])
    pair_rows, near_rows, mats = enter(plan, pair, near, mats_own)

    by_row = (rows, c, length)
    parts_shape = (plan.members, 2, plan.own_channels, rows, length)
    part_shape = (plan.members, plan.own_channels, rows, length)
    low_rows = pltpu.VMEM(by_row, BF16)

    def mat_buffer(tall, wide=1):
        return pltpu.VMEM((tall * c, wide * c), BF16)

    def gain_buffer(count):
        return pltpu.VMEM((count, c, length), F32)

    state_zero, parts = local_call(
        first_kernel, plan, (pair_rows, mats, lengths),
        [sds(by_row, BF16), sds(parts_shape, BF16)],
        [mat_buffer(4), gain_buffer(1), low_rows, low_rows], 0,
    )
    full_one, product_one = product(plan, parts, True, 1)
    state_one, product_rows, parts = local_call(
        middle_kernel, plan, (product_one, state_zero, mats, lengths),
        [sds(by_row, F32), sds(by_row, BF16), sds(parts_shape, BF16)],
        [mat_buffer(1), mat_buffer(1), mat_buffer(4), gain_buffer(3), low_rows, low_rows], 0,
    )
    full_two, product_two = product(plan, parts, False, 2)
    (
        grad_two, grad_gate, parts, attend_in, attend_out, second_out, gains_late, grad_struct, losses,
    ) = local_call(
        attend_kernel, plan,
        (product_two, state_one, mats, lengths, near_rows, frames, target, motif),
        [
            sds(by_row, F32), sds(by_row, BF16), sds(part_shape, BF16),
            sds((c, 4 * c), F32), sds((c, c), F32), sds((c, c), F32),
            sds((3, c, 128), F32), sds((16, c), F32), sds((8, 128), F32),
        ],
        [
            low_rows, low_rows, mat_buffer(1), mat_buffer(1), mat_buffer(1), mat_buffer(4),
            mat_buffer(1, 4), mat_buffer(1), mat_buffer(1), pltpu.VMEM((16, c), BF16), gain_buffer(4),
            pltpu.VMEM((rows, length), F32), pltpu.VMEM((length, 128), F32),
            pltpu.VMEM((c, length), BF16), pltpu.VMEM((c, length), BF16), pltpu.VMEM((c, length), BF16),
            pltpu.VMEM((NH, length, length), F32), pltpu.VMEM((c, length), F32),
            pltpu.VMEM((4 * c, length), BF16),
        ],
        0,
    )
    grad_parts = product_back(plan, parts, full_two, False, 3)
    grad_gate, parts, second_in, first_out, gains_mid = local_call(
        turn_kernel, plan,
        (grad_parts, grad_two, grad_gate, state_one, state_zero, product_rows, mats, lengths),
        [
            sds(by_row, BF16), sds(part_shape, BF16), sds((c, 5 * c), F32), sds((c, c), F32),
            sds((2, c, 128), F32),
        ],
        [
            low_rows, low_rows, low_rows, mat_buffer(4), mat_buffer(1, 5), mat_buffer(1), mat_buffer(1),
            mat_buffer(1), gain_buffer(3), pltpu.VMEM((5 * c, length), BF16),
        ],
        0,
    )
    grad_parts = product_back(plan, parts, full_one, True, 4)
    packed = local_call(
        last_kernel, plan,
        (
            grad_parts, grad_gate, state_zero, mats, lengths, attend_in, attend_out, second_out,
            gains_late, grad_struct, losses, second_in, first_out, gains_mid,
        ),
        sds((plan.members, 2, plan.group_mats, shard, c), BF16),
        [
            low_rows, low_rows, mat_buffer(4), mat_buffer(1, 5), gain_buffer(1),
            pltpu.VMEM((5 * c, length), BF16), pltpu.VMEM((c, 5 * c), F32), pltpu.VMEM((c, 128), F32),
        ],
        0,
    )
    summed = reduce_grads(plan, packed).reshape(plan.mats, shard, c)
    small = summed[N_MATS] + summed[N_MATS + 1]
    own_gains = small[:, :N_GAINS].T
    own_struct = small[:, STRUCT_LANE : STRUCT_LANE + struct_w.shape[0]].T
    weight_new = adam_update(weights, weights_m, weights_v, summed[:N_MATS], 0.1, 0.01)
    struct_new = adam_update(struct_w, struct_m, struct_v, own_struct, 0.1, 0.01)
    gain_new = adam_update(gains, gains_m, gains_v, own_gains, 0.4, 0.0)
    return (small[0, LOSS_LANE], losses[1, 0]) + weight_new + struct_new + gain_new


def solution(mesh):
    in_specs = (
        P(None, "row", "col", None), P(), P(), P(), P(), P(None, "row", None),
        P(None, "row", None), P(None, "row", None), P(None, "row", None),
    ) + (P(None, "row"),) * 6
    out_specs = (P(), P()) + (P(None, "row", None),) * 3 + (P(None, "row"),) * 6

    def step(pair, *rest):
        plan = Plan(mesh, pair.shape, rest[5].shape)
        return jax.shard_map(
            functools.partial(per_device, plan),
            mesh=mesh, in_specs=in_specs, out_specs=out_specs, check_vma=False,
        )(pair, *rest)

    return step
```

time: 1490 us -> 422 us (0.28)
  waiting for transfers between devices: 785 us -> 0 us
  Pallas kernels: 0 us -> 404 us
  local copies, waits for them, and re-layouts: 222 us -> 7.56 us
  matrix products: 187 us -> 0 us
  blocking collectives: 159 us -> 0 us
  other arithmetic: 109 us -> 8.62 us
  between operations: 16.6 us -> 0.87 us
    pallas_call x0 -> x11, Pallas kernels: none -> 404 us  [the longest x5 132 us: local_call(): pl.pallas_call(functools.partial(kernel, plan), out_shape=tuple(outs) if...]
    all_gather x5 -> x0, waiting for transfers between devices: 333 us -> none  [the longest x2 246 us: row_panels(): return lax.all_gather(values, 'row', axis=1, tiled=True)]
    reduce_scatter x4 -> x0, waiting for transfers between devices: 275 us -> none  [the longest x1 148 us: row_sums(): lax.psum_scatter(partial_term(jnp.int32(0), row_total * lax.axis_size('ro...]
    dot_general x32 -> x0, matrix products: 176 us -> none  [the longest x1 13.2 us: tri_back(): jnp.einsum('bkih,bijh->bkjh', panels, grad_rows, preferred_element_type=j...]
    unnamed x12 -> x0, waiting for transfers between devices: 92 us -> none
    psum x1 -> x0, waiting for transfers between devices: 85.5 us -> none  [per_device(): lax.psum((grad_mats, grad_struct, grad_gains), ('row', 'col'))]
    all_gather x3 -> x0, blocking collectives: 85.1 us -> none  [the longest x1 31.3 us: per_device(): lax.all_gather(weights.astype(jnp.bfloat16), 'row', axis=1, tiled=True)]
    psum x3 -> x0, blocking collectives: 73.5 us -> none  [the longest x1 39.4 us: per_device(): lax.psum((grad_mats, grad_struct, grad_gains), ('row', 'col'))]
  transfers between devices with their start and end apart: 11 -> 0, of which waited for: 11 -> 0; matrix products, arithmetic and copies ran while one was open for 6% -> 0% of each run, Pallas kernels for 0% -> 0%
where the time goes in v1:
time: 422 us; the launch traced here: 421 us
  Pallas kernels  404 us (96%)
  other arithmetic  8.62 us (2%)
  local copies, waits for them, and re-layouts  7.56 us (2%)
    pallas_call x5, Pallas kernels, local_call(): pl.pallas_call(functools.partial(kernel, plan), out_shape=tuple(outs) if...  132 us
    pallas_call x2, Pallas kernels, product(): pl.pallas_call(functools.partial(product_kernel, plan, outgoing), out_sha...  112 us
    pallas_call x2, Pallas kernels, product_back(): pl.pallas_call(functools.partial(product_back_kernel, plan, outgoing), ou...  100 us
    pallas_call x1, Pallas kernels, reduce_grads(): pl.pallas_call(functools.partial(reduce_kernel, plan), out_shape=jax.Shap...  30.9 us
    pallas_call x1, Pallas kernels, enter(): pl.pallas_call(functools.partial(enter_kernel, plan), out_shape=(jax.Shap...  29.3 us

profile of v1, /device:TPU:0, one launch (start us, length us, event | category | flops | bytes accessed | tf_op | source)
XLA Modules:
  0.0 420.7 jit_solution(14247162618113694169)
XLA Ops:
  1.2 2.7 and_reduce_fusion
  3.9 0.8 copy.26
  4.7 0.8 copy.27
  5.4 2.0 dynamic-slice_select_fusion
  7.5 1.5 scatter.9
  9.0 0.9 convert_element_type.6
  9.9 0.6 pad_maximum_fusion.mats
  10.6 29.3 %shard_map.230 = (bf16[16,256,128]{2,1,0:T(8,128)(2,1)}, s32[4,16,32]{2,1,0:T(8,128)}, bf16[8,20,16,128]{3,2,1,0:T(8,128)(2,1)}) custom-call(bf16[2,32,64,128]{3,2,1,0:T(8,128)(2,1)} %pair.1, s32[2,2,16,32]{3,2,1,0:T(8,128)} %bitcast.32, bf16[20,16,128]{2,1,0:T(8,128)(2,1)} %pad_maximum_fusion.mats), custom_call_target="tpu_custom_call" | custom-call | tf_op jit(solution)/shard_map/pallas_call | solution.py:289
  39.9 9.1 %shard_map.231 = (bf16[16,128,256]{2,1,0:T(8,128)(2,1)}, bf16[16,2,8,16,256]{4,3,2,1,0:T(8,128)(2,1)}) custom-call(bf16[16,256,128]{2,1,0:T(8,128)(2,1)} %get-tuple-element.61.pair, bf16[8,20,16,128]{3,2,1,0:T(8,128)(2,1)} %get-tuple-element.62.mats, s32[2]{0:T(128)} %limits.9), custom_call_target="tpu_custom_call" | custom-call | tf_op jit(solution)/shard_map/pallas_call | solution.py:846
  49.1 55.8 %shard_map.232 = (bf16[16,2,8,16,256]{4,3,2,1,0:T(8,128)(2,1)}, bf16[16,8,16,256]{3,2,1,0:T(8,128)(2,1)}) custom-call(bf16[16,2,8,16,256]{4,3,2,1,0:T(8,128)(2,1)} %get-tuple-element.63.parts), custom_call_target="tpu_custom_call" | custom-call | tf_op jit(solution)/shard_map/pallas_call | solution.py:366
  104.9 12.6 %shard_map.233 = (f32[16,128,256]{2,1,0:T(8,128)}, bf16[16,128,256]{2,1,0:T(8,128)(2,1)}, bf16[16,2,8,16,256]{4,3,2,1,0:T(8,128)(2,1)}) custom-call(bf16[16,8,16,256]{3,2,1,0:T(8,128)(2,1)} %get-tuple-element.64.product_in, bf16[16,128,256]{2,1,0:T(8,128)(2,1)} %get-tuple-element.65.state.first_state, bf16[8,20,16,128]{3,2,1,0:T(8,128)(2,1)} %get-tuple-element.62.mats, ...), custom_call_target="tpu_custom_call" | custom-call | tf_op jit(solution)/shard_map/pallas_call | solution.py:846
  117.5 56.0 %shard_map.234 = (bf16[16,2,8,16,256]{4,3,2,1,0:T(8,128)(2,1)}, bf16[16,8,16,256]{3,2,1,0:T(8,128)(2,1)}) custom-call(bf16[16,2,8,16,256]{4,3,2,1,0:T(8,128)(2,1)} %get-tuple-element.66.parts), custom_call_target="tpu_custom_call" | custom-call | tf_op jit(solution)/shard_map/pallas_call | solution.py:366
  173.5 0.6 copy.28.frames
  174.1 0.6 copy.29.target
  174.7 74.3 %shard_map.235 = (f32[16,128,256]{2,1,0:T(8,128)}, bf16[16,128,256]{2,1,0:T(8,128)(2,1)}, bf16[16,8,16,256]{3,2,1,0:T(8,128)(2,1)}, f32[128,512]{1,0:T(8,128)}, ...) custom-call(bf16[16,8,16,256]{3,2,1,0:T(8,128)(2,1)} %get-tuple-elem, ...), custom_call_target="tpu_custom_call" | custom-call | tf_op jit(solution)/shard_map/pallas_call | solution.py:846
  249.1 46.4 %shard_map.236.grad_parts = bf16[16,2,8,16,256]{4,3,2,1,0:T(8,128)(2,1)} custom-call(bf16[16,8,16,256]{3,2,1,0:T(8,128)(2,1)} %get-tuple-element.70.parts, bf16[16,2,8,16,256]{4,3,2,1,0:T(8,128)(2,1)} %get-tuple-element.71.full), custom_call_target="tpu_custom_call" | custom-call | tf_op jit(solution)/shard_map/pallas_call | solution.py:379
  295.5 20.9 %shard_map.237 = (bf16[16,128,256]{2,1,0:T(8,128)(2,1)}, bf16[16,8,16,256]{3,2,1,0:T(8,128)(2,1)}, f32[128,640]{1,0:T(8,128)}, f32[128,128]{1,0:T(8,128)}, f32[2,128,128]{2,1,0:T(8,128)}) custom-call(bf16[16,2,8,16,256]{4,3,2,1,0:T(8,128)(2,1)} %shard_map.236.grad_parts, f32[16,128,256]{2,1,0:T(8,128)} %get-tuple-element.72.grad_after, ...), custom_call_target="tpu_custom_call" | custom-call | tf_op jit(solution)/shard_map/pallas_call | solution.py:846
  316.4 53.5 %shard_map.238.grad_parts = bf16[16,2,8,16,256]{4,3,2,1,0:T(8,128)(2,1)} custom-call(bf16[16,8,16,256]{3,2,1,0:T(8,128)(2,1)} %get-tuple-element.75.parts, bf16[16,2,8,16,256]{4,3,2,1,0:T(8,128)(2,1)} %get-tuple-element.76.full), custom_call_target="tpu_custom_call" | custom-call | tf_op jit(solution)/shard_map/pallas_call | solution.py:379
  370.0 14.7 %shard_map.239.grads = bf16[16,2,5,16,128]{4,3,2,1,0:T(8,128)(2,1)} custom-call(bf16[16,2,8,16,256]{4,3,2,1,0:T(8,128)(2,1)} %shard_map.238.grad_parts, bf16[16,128,256]{2,1,0:T(8,128)(2,1)} %get-tuple-element.77.grad_gate, bf16[16,128,256]{2,1,0:T(8,128)(2,1)} %get-tuple-element.65.state.first_state, bf16[8,20,16,128]{3,2,1,0:T(8,128)(2,1)} %get-tuple-element.62.mats, ...), custom_call_target="tpu_custom_call" | custom-call | tf_op jit(solution)/shard_map/pallas_call | solution.py:846
  384.7 30.9 %shard_map.240 = f32[4,5,16,128]{3,2,1,0:T(8,128)} custom-call(bf16[16,2,5,16,128]{4,3,2,1,0:T(8,128)(2,1)} %shard_map.239.grads), custom_call_target="tpu_custom_call" | custom-call | tf_op jit(solution)/shard_map/pallas_call | solution.py:448
  415.6 1.7 multiply_subtract_fusion
  417.4 0.7 fusion.6
  418.4 0.6 multiply_subtract_fusion.1
  419.5 1.2 slice.81
  (29 shorter events, 1.4 us)
Async XLA Ops:
  104.9 68.6 %copy-start.5 = (f32[2,6,256]{2,0,1:T(2,128)S(1)}, f32[2,6,256]{2,0,1:T(2,128)}, u32[]{:S(2)}) copy-start(f32[2,6,256]{2,0,1:T(2,128)} %param.20) | copy-start | bytes 36868
  104.9 69.2 %copy-start.6 = (f32[2,6,256]{2,0,1:T(2,128)S(1)}, f32[2,6,256]{2,0,1:T(2,128)}, u32[]{:S(2)}) copy-start(f32[2,6,256]{2,0,1:T(2,128)} %param.21) | copy-start | bytes 36868
  370.0 45.6 %copy-start = (f32[17,16,128]{2,1,0:T(8,128)S(1)}, f32[17,16,128]{2,1,0:T(8,128)}, u32[]{:S(2)}) copy-start(f32[17,16,128]{2,1,0:T(8,128)} %param.25) | copy-start | bytes 417796
  370.0 45.6 %copy-start.1 = (f32[17,16,128]{2,1,0:T(8,128)S(1)}, f32[17,16,128]{2,1,0:T(8,128)}, u32[]{:S(2)}) copy-start(f32[17,16,128]{2,1,0:T(8,128)} %param.27) | copy-start | bytes 417796
  370.0 45.6 %copy-start.2 = (f32[17,16,128]{2,1,0:T(8,128)S(1)}, f32[17,16,128]{2,1,0:T(8,128)}, u32[]{:S(2)}) copy-start(f32[17,16,128]{2,1,0:T(8,128)} %param.26) | copy-start | bytes 417796
  384.7 33.6 %copy-start.3 = (f32[6,16]{1,0:T(8,128)S(1)}, f32[6,16]{1,0:T(8,128)}, u32[]{:S(2)}) copy-start(f32[6,16]{1,0:T(8,128)} %param.31) | copy-start | bytes 1156
  384.7 33.6 %copy-start.4 = (f32[6,16]{1,0:T(8,128)S(1)}, f32[6,16]{1,0:T(8,128)}, u32[]{:S(2)}) copy-start(f32[6,16]{1,0:T(8,128)} %param.28) | copy-start | bytes 1156
  384.7 33.6 %copy-start.7 = (f32[6,16]{1,0:T(8,128)S(1)}, f32[6,16]{1,0:T(8,128)}, u32[]{:S(2)}) copy-start(f32[6,16]{1,0:T(8,128)} %param.33) | copy-start | bytes 1156
  384.7 33.6 %copy-start.8 = (f32[6,16]{1,0:T(8,128)S(1)}, f32[6,16]{1,0:T(8,128)}, u32[]{:S(2)}) copy-start(f32[6,16]{1,0:T(8,128)} %param.32) | copy-start | bytes 1156
  384.7 33.6 %copy-start.9 = (f32[6,16]{1,0:T(8,128)S(1)}, f32[6,16]{1,0:T(8,128)}, u32[]{:S(2)}) copy-start(f32[6,16]{1,0:T(8,128)} %param.30) | copy-start | bytes 1156
  384.7 33.6 %copy-start.10 = (f32[6,16]{1,0:T(8,128)S(1)}, f32[6,16]{1,0:T(8,128)}, u32[]{:S(2)}) copy-start(f32[6,16]{1,0:T(8,128)} %param.29) | copy-start | bytes 1156

commit v2 on v1

--- a/solution.py
+++ b/solution.py
@@ -44,6 +44,8 @@
         self.shard = self.channels // self.rows
         self.group_mats = -(-(N_MATS + 2) // self.cols)
         self.mats = self.group_mats * self.cols
+        self.blocks = min(4, self.own_rows)
+        self.block_own = self.own_rows // self.blocks
 
     def here(self):
         row, col = lax.axis_index("row"), lax.axis_index("col")
@@ -74,7 +76,7 @@
     return total
 
 
-def group_barrier(plan, half, me):
+def barrier_signal(plan, half, me):
     barrier = pltpu.get_barrier_semaphore()
 
     def signal(off, carry):
@@ -87,41 +89,104 @@
         return carry
 
     lax.fori_loop(1, plan.members, signal, 0)
-    pl.semaphore_wait(barrier, plan.members - 1)
-
-
-def swap_copy(plan, half, me, off, src, dst, send, recv):
-    to = (me + off) % plan.members
-    return pltpu.make_async_remote_copy(
-        src_ref=src.at[to],
-        dst_ref=dst.at[me],
-        send_sem=send.at[off],
-        recv_sem=recv.at[off],
-        device_id=plan.member(half, to),
-        device_id_type=MESH,
-    )
-
-
-def swap_start(plan, half, me, src, dst, send, recv, local):
-    def start(off, carry):
-        swap_copy(plan, half, me, off, src, dst, send, recv).start()
+
+
+def barrier_wait(plan):
+    pl.semaphore_wait(pltpu.get_barrier_semaphore(), plan.members - 1)
+
+
+class Swap:
+    def __init__(self, plan, half, me, src, dst, sems):
+        self.plan, self.half, self.me, self.src, self.dst = plan, half, me, src, dst
+        self.send, self.recv, self.local = sems
+
+    def start(self, block):
+        plan, half, me = self.plan, self.half, self.me
+
+        def one(off, carry):
+            to = (me + off) % plan.members
+            pltpu.make_async_remote_copy(
+                src_ref=self.src.at[to, block],
+                dst_ref=self.dst.at[me, block],
+                send_sem=self.send.at[block],
+                recv_sem=self.recv.at[block],
+                device_id=plan.member(half, to),
+                device_id_type=MESH,
+            ).start()
+            return carry
+
+        lax.fori_loop(1, plan.members, one, 0)
+        self.own(block).start()
+
+    def own(self, block):
+        me = self.me
+        return pltpu.make_async_copy(
+            self.src.at[me, block], self.dst.at[me, block], self.local.at[block]
+        )
+
+    def whole(self, block):
+        others = pl.ds(0, self.plan.members - 1)
+        return pltpu.make_async_remote_copy(
+            src_ref=self.src.at[others, block],
+            dst_ref=self.dst.at[others, block],
+            send_sem=self.send.at[block],
+            recv_sem=self.recv.at[block],
+            device_id=self.plan.member(self.half, (self.me + 1) % self.plan.members),
+            device_id_type=MESH,
+        )
+
+    def arrive(self, block):
+        self.whole(block).wait_recv()
+        self.own(block).wait()
+
+    def arrive_all(self):
+        def one(block, carry):
+            self.arrive(block)
+            return carry
+
+        lax.fori_loop(0, self.plan.blocks, one, 0)
+
+    def start_all(self):
+        def one(block, carry):
+            self.start(block)
+            return carry
+
+        lax.fori_loop(0, self.plan.blocks, one, 0)
+
+    def finish(self):
+        def one(block, carry):
+            self.whole(block).wait_send()
+            return carry
+
+        lax.fori_loop(0, self.plan.blocks, one, 0)
+
+
+def swap_sems(plan, count):
+    return [pltpu.SemaphoreType.DMA((plan.blocks,))] * (3 * count)
+
+
+def each_row(plan, before, body, after):
+    def one(block, carry):
+        before(block)
+
+        def row(r, carry):
+            body(block, r, block * plan.block_own + r)
+            return carry
+
+        lax.fori_loop(0, plan.block_own, row, 0)
+        after(block)
         return carry
 
-    lax.fori_loop(1, plan.members, start, 0)
-    pltpu.make_async_copy(src.at[me], dst.at[me], local).start()
-
-
-def swap_wait(plan, half, me, src, dst, send, recv, local):
-    def wait(off, carry):
-        swap_copy(plan, half, me, off, src, dst, send, recv).wait()
-        return carry
-
-    lax.fori_loop(1, plan.members, wait, 0)
-    pltpu.make_async_copy(src.at[me], dst.at[me], local).wait()
+    lax.fori_loop(0, plan.blocks, one, 0)
+
+
+def vmem(count):
+    return [pl.BlockSpec(memory_space=pltpu.VMEM)] * count
 
 
 def enter_kernel(
-    plan, pair, near, mats, pair_out, near_out, mats_out, sends, recvs, near_sends, near_recvs, mat_sems
+    plan, pair, near, weights, extra, pair_out, near_out, mats_out,
+    mats, sends, recvs, near_sends, near_recvs, mat_sems,
 ):
     row, col, half, me = plan.here()
     own, cols, pieces, width = plan.own_rows, plan.cols, plan.pieces, plan.block_cols
@@ -137,6 +202,9 @@
         return carry
 
     lax.fori_loop(1, plan.rows * cols, greet, 0)
+    mats[:N_MATS] = weights[...].astype(BF16)
+    mats[N_MATS] = extra[...].astype(BF16)
+    mats[N_MATS + 1 :] = jnp.zeros((plan.mats - N_MATS - 1,) + extra.shape, BF16)
     pl.semaphore_wait(barrier, plan.rows * cols - 1)
 
     first = pl.ds(col * plan.group_mats, plan.group_mats)
@@ -282,20 +350,22 @@
             ).wait_recv()
 
 
-def enter(plan, pair, near, mats):
+def enter(plan, pair, near, weights, extra):
     anywhere = pl.BlockSpec(memory_space=pl.ANY)
     slots = plan.crops * plan.pieces
     dma = pltpu.SemaphoreType.DMA
+    mats = (plan.mats,) + weights.shape[1:]
     return pl.pallas_call(
         functools.partial(enter_kernel, plan),
         out_shape=(
             jax.ShapeDtypeStruct((plan.own_rows, plan.length, plan.channels), BF16),
             jax.ShapeDtypeStruct((plan.cols,) + near.shape[2:], near.dtype),
-            jax.ShapeDtypeStruct((plan.rows,) + mats.shape, BF16),
+            jax.ShapeDtypeStruct((plan.rows,) + mats, BF16),
         ),
-        in_specs=[anywhere] * 3,
+        in_specs=[anywhere] * 2 + vmem(2),
         out_specs=(anywhere,) * 3,
         scratch_shapes=[
+            pltpu.VMEM(mats, BF16),
             dma((slots,)),
             dma((plan.cols,)),
             dma((slots,)),
@@ -303,90 +373,7 @@
             dma((3 + 4 * plan.members,)),
         ],
         compiler_params=pltpu.CompilerParams(collective_id=0, has_side_effects=True),
-    )(pair, near, mats)
-
-
-def square(plan, ref, index):
-    return ref[index].reshape(plan.length, plan.length)
-
-
-def product_kernel(plan, outgoing, parts, full, result, staged, *sems):
-    _, _, half, me = plan.here()
-    group_barrier(plan, half, me)
-    swap_start(plan, half, me, parts, full, *sems[:3])
-    swap_wait(plan, half, me, parts, full, *sems[:3])
-
-    def channel(h, carry):
-        left = full[:, 0, h].reshape(plan.length, plan.length)
-        right = full[:, 1, h].reshape(plan.length, plan.length)
-        value = dot(left, right, NT if outgoing else TN)
-        staged[:, h] = value.astype(BF16).reshape(plan.members, plan.own_rows, plan.length)
-        return carry
-
-    lax.fori_loop(0, plan.own_channels, channel, 0)
-    swap_start(plan, half, me, staged, result, *sems[3:])
-    swap_wait(plan, half, me, staged, result, *sems[3:])
-
-
-def product_back_kernel(plan, outgoing, parts, full, result, gathered, staged, *sems):
-    _, _, half, me = plan.here()
-    group_barrier(plan, half, me)
-    swap_start(plan, half, me, parts, gathered, *sems[:3])
-    swap_wait(plan, half, me, parts, gathered, *sems[:3])
-    blocks = (plan.members, plan.own_rows, plan.length)
-
-    def channel(h, carry):
-        left = full[:, 0, h].reshape(plan.length, plan.length)
-        right = full[:, 1, h].reshape(plan.length, plan.length)
-        grad = gathered[:, h].reshape(plan.length, plan.length)
-        if outgoing:
-            grad_left, grad_right = dot(grad, right), dot(grad, left, TN)
-        else:
-            grad_left, grad_right = dot(right, grad, NT), dot(left, grad)
-        staged[:, 0, h] = grad_left.astype(BF16).reshape(blocks)
-        staged[:, 1, h] = grad_right.astype(BF16).reshape(blocks)
-        return carry
-
-    lax.fori_loop(0, plan.own_channels, channel, 0)
-    swap_start(plan, half, me, staged, result, *sems[3:])
-    swap_wait(plan, half, me, staged, result, *sems[3:])
-
-
-def swap_sems(plan):
-    dma = pltpu.SemaphoreType.DMA
-    return [dma((plan.members,)), dma((plan.members,)), dma] * 2
-
-
-def vmem(count):
-    return [pl.BlockSpec(memory_space=pltpu.VMEM)] * count
-
-
-def product(plan, parts, outgoing, collective_id):
-    one = (plan.members, plan.own_channels, plan.own_rows, plan.length)
-    return pl.pallas_call(
-        functools.partial(product_kernel, plan, outgoing),
-        out_shape=(jax.ShapeDtypeStruct(parts.shape, BF16), jax.ShapeDtypeStruct(one, BF16)),
-        in_specs=vmem(1),
-        out_specs=tuple(vmem(2)),
-        scratch_shapes=[pltpu.VMEM(one, BF16)] + swap_sems(plan),
-        compiler_params=pltpu.CompilerParams(
-            collective_id=collective_id, has_side_effects=True, vmem_limit_bytes=VMEM_LIMIT
-        ),
-    )(parts)
-
-
-def product_back(plan, parts, full, outgoing, collective_id):
-    return pl.pallas_call(
-        functools.partial(product_back_kernel, plan, outgoing),
-        out_shape=jax.ShapeDtypeStruct(full.shape, BF16),
-        in_specs=vmem(2),
-        out_specs=vmem(1)[0],
-        scratch_shapes=[pltpu.VMEM(parts.shape, BF16), pltpu.VMEM(full.shape, BF16)]
-        + swap_sems(plan),
-        compiler_params=pltpu.CompilerParams(
-            collective_id=collective_id, has_side_effects=True, vmem_limit_bytes=VMEM_LIMIT
-        ),
-    )(parts, full)
+    )(pair, near, weights, extra)
 
 
 def reduce_kernel(plan, grads, total, got, crossed, sent, *sems):
@@ -407,9 +394,11 @@
     lax.fori_loop(1, plan.members, greet, 0)
     pl.semaphore_wait(barrier, plan.members)
 
-    swap_start(plan, half, me, grads, got, *sems[:3])
-    swap_wait(plan, half, me, grads, got, *sems[:3])
-    sums = jnp.sum(got[...].astype(F32), axis=0)
+    swap = Swap(plan, half, me, grads, got, sems[:3])
+    swap.start(0)
+    swap.arrive(0)
+    swap.whole(0).wait_send()
+    sums = jnp.sum(got[:, 0].astype(F32), axis=0)
     sent[...] = sums
     across, mine, theirs = sems[3], sems[4], sems[5]
     cross = pltpu.make_async_remote_copy(
@@ -444,7 +433,7 @@
 
 def reduce_grads(plan, grads):
     dma = pltpu.SemaphoreType.DMA
-    part = grads.shape[2:]
+    part = grads.shape[3:]
     return pl.pallas_call(
         functools.partial(reduce_kernel, plan),
         out_shape=jax.ShapeDtypeStruct((plan.cols,) + part, F32),
@@ -454,15 +443,15 @@
             pltpu.VMEM(grads.shape, BF16),
             pltpu.VMEM(part, F32),
             pltpu.VMEM((2,) + part, F32),
-            dma((plan.members,)),
-            dma((plan.members,)),
-            dma,
+            dma((1,)),
+            dma((1,)),
+            dma((1,)),
             dma((2,)),
             dma((plan.cols,)),
             dma((plan.cols,)),
         ],
         compiler_params=pltpu.CompilerParams(
-            collective_id=5, has_side_effects=True, vmem_limit_bytes=VMEM_LIMIT
+            collective_id=6, has_side_effects=True, vmem_limit_bytes=VMEM_LIMIT
         ),
     )(grads)
 
@@ -491,6 +480,24 @@
         into[place] = jnp.broadcast_to(
             extra[:, number : number + 1], (plan.channels, plan.length)
         )
+
+
+def mixing(plan):
+    c, own = plan.channels, plan.own_channels
+    row = lax.broadcasted_iota(jnp.int32, (2 * c, 2 * c), 0)
+    there = (row // own) % 2 * c + row // (2 * own) * own + row % own
+    return jnp.where(lax.broadcasted_iota(jnp.int32, (2 * c, 2 * c), 1) == there, 1.0, 0.0).astype(BF16)
+
+
+def fill_sides(plan, mats, first, side, rows=None):
+    c = plan.channels
+    mix = mixing(plan)
+    for place in range(2):
+        columns = [whole_mat(plan, mats, first + place + 2 * k).T.astype(BF16) for k in range(2)]
+        mixed = dot(mix, jnp.concatenate(columns, axis=0))
+        side[2 * c * place : 2 * c * (place + 1), :] = mixed.astype(BF16)
+        if rows is not None:
+            rows[:, 2 * c * place : 2 * c * (place + 1)] = mixed.T.astype(BF16)
 
 
 def pair_mask(plan, limits, i):
@@ -501,44 +508,79 @@
     return jnp.where(jnp.logical_and(places < limit, row_place < limit), 1.0, 0.0).astype(F32)
 
 
-def to_channels(plan, rows):
-    return jnp.swapaxes(rows, 0, 1).reshape(
-        plan.members, plan.own_channels, plan.own_rows, plan.length
+def to_members(plan, values):
+    return values.reshape(plan.members, values.shape[0] // plan.members, plan.length).astype(BF16)
+
+
+def from_members(plan, blocks):
+    return blocks.astype(F32).reshape(-1, plan.length)
+
+
+def gated_sides(plan, low, side, mask):
+    projected = dot(side[...], low)
+    count = 2 * plan.channels
+    return mask * jax.nn.sigmoid(projected[:count]) * projected[count:]
+
+
+def turned(plan, rows):
+    return jnp.swapaxes(rows.reshape(plan.length, rows.shape[3], plan.length), 0, 1)
+
+
+def turned_back(plan, channels):
+    count = channels.shape[0]
+    return jnp.swapaxes(channels, 0, 1).reshape(
+        plan.members, plan.blocks, plan.block_own, count, plan.length
     )
 
 
-def to_rows(plan, channels):
-    return jnp.swapaxes(
-        channels.reshape(plan.channels, plan.own_rows, plan.length), 0, 1
-    )
-
-
-def gated_sides(plan, low, into_side, mask):
-    c = plan.channels
-    projected = dot(into_side[: 4 * c, :], low)
-    left = mask * jax.nn.sigmoid(projected[:c]) * projected[c : 2 * c]
-    right = mask * jax.nn.sigmoid(projected[2 * c : 3 * c]) * projected[3 * c :]
-    return left.astype(BF16), right.astype(BF16)
-
-
-def first_kernel(plan, pair, mats, limits, state, parts, into_side, gain, left_rows, right_rows):
-    fill_columns(plan, mats, range(4), into_side)
+def make_product(plan, outgoing, full, sides, turned_out, staged):
+    sides[...] = turned(plan, full[...])
+    own = plan.own_channels
+
+    def channel(h, carry):
+        turned_out[h] = dot(sides[h], sides[own + h], NT if outgoing else TN).astype(BF16)
+        return carry
+
+    lax.fori_loop(0, own, channel, 0)
+    staged[...] = turned_back(plan, turned_out[...])
+
+
+def make_product_back(plan, outgoing, grads, sides, grad_turned, turned_out, staged):
+    grad_turned[...] = turned(plan, grads[...])
+    own = plan.own_channels
+
+    def channel(h, carry):
+        left, right, grad = sides[h], sides[own + h], grad_turned[h]
+        if outgoing:
+            grad_left, grad_right = dot(grad, right), dot(grad, left, TN)
+        else:
+            grad_left, grad_right = dot(right, grad, NT), dot(left, grad)
+        turned_out[h] = grad_left.astype(BF16)
+        turned_out[own + h] = grad_right.astype(BF16)
+        return carry
+
+    lax.fori_loop(0, own, channel, 0)
+    staged[...] = turned_back(plan, turned_out[...])
+
+
+def first_kernel(plan, pair, mats, limits, state, full, parts, side, gain, *sems):
+    _, _, half, me = plan.here()
+    barrier_signal(plan, half, me)
+    fill_sides(plan, mats, 0, side)
     fill_gains(plan, mats, (0,), gain)
-
-    def body(i, carry):
+    out = Swap(plan, half, me, parts, full, sems)
+    barrier_wait(plan)
+
+    def body(block, r, i):
         value = pair[i].astype(F32).T
         state[i] = value.astype(BF16)
         normed, _ = layer_norm(value)
-        left, right = gated_sides(
-            plan, (normed * gain[0]).astype(BF16), into_side, pair_mask(plan, limits, i)
-        )
-        left_rows[i] = left
-        right_rows[i] = right
-        return carry
-
-    lax.fori_loop(0, plan.own_rows, body, 0)
-    parts[:, 0] = to_channels(plan, left_rows[...])
-    parts[:, 1] = to_channels(plan, right_rows[...])
+        low = (normed * gain[0]).astype(BF16)
+        parts[:, block, r] = to_members(plan, gated_sides(plan, low, side, pair_mask(plan, limits, i)))
+
+    each_row(plan, lambda block: None, body, out.start)
+    out.arrive_all()
+    out.finish()
 
 
 def close_triangle(low, mixed_low, gate_side, out_side):
@@ -547,35 +589,38 @@
 
 
 def middle_kernel(
-    plan, product_in, state, mats, limits, state_out, product_rows, parts, gate_side, out_side,
-    into_side, gains, left_rows, right_rows,
+    plan, full_in, state, mats, limits, state_out, sides, product, full,
+    turned_out, staged, parts, gate_side, out_side, side, gains, *sems,
 ):
+    _, _, half, me = plan.here()
+    barrier_signal(plan, half, me)
+    make_product(plan, True, full_in, sides, turned_out, staged)
+    into = Swap(plan, half, me, staged, product, sems[:3])
+    out = Swap(plan, half, me, parts, full, sems[3:])
+    barrier_wait(plan)
+    into.start_all()
     fill_columns(plan, mats, (4,), gate_side)
     fill_columns(plan, mats, (5,), out_side)
-    fill_columns(plan, mats, range(6, 10), into_side)
+    fill_sides(plan, mats, 6, side)
     fill_gains(plan, mats, (0, 1, 2), gains)
-    product_rows[...] = to_rows(plan, product_in[...])
-
-    def body(i, carry):
+
+    def body(block, r, i):
         before = state[i].astype(F32)
         normed, _ = layer_norm(before)
-        mixed, _ = layer_norm(product_rows[i].astype(F32))
+        mixed, _ = layer_norm(from_members(plan, product[:, block, r]))
         gating, branch = close_triangle(
             (normed * gains[0]).astype(BF16), (mixed * gains[1]).astype(BF16), gate_side, out_side
         )
         after = before + gating * branch
         state_out[i] = after
         normed, _ = layer_norm(after)
-        left, right = gated_sides(
-            plan, (normed * gains[2]).astype(BF16), into_side, pair_mask(plan, limits, i)
-        )
-        left_rows[i] = left
-        right_rows[i] = right
-        return carry
-
-    lax.fori_loop(0, plan.own_rows, body, 0)
-    parts[:, 0] = to_channels(plan, left_rows[...])
-    parts[:, 1] = to_channels(plan, right_rows[...])
+        low = (normed * gains[2]).astype(BF16)
+        parts[:, block, r] = to_members(plan, gated_sides(plan, low, side, pair_mask(plan, limits, i)))
+
+    each_row(plan, into.arrive, body, out.start)
+    out.arrive_all()
+    into.finish()
+    out.finish()
 
 
 def close_triangle_back(grad, gating, branch, mixed, scale, mixed_low, out_rows, gain, grad_out, grad_gain):
@@ -584,36 +629,36 @@
     grad_out[...] += dot(mixed_low, grad_branch, NT)
     grad_mixed = dot(out_rows[...], grad_branch)
     grad_gain[...] += lane_fold(grad_mixed * mixed)
-    return grad_gate, layer_norm_back(grad_mixed, mixed, scale, gain).astype(BF16)
-
-
-def open_triangle_back(plan, grads, low, into_side, in_rows, mask, grad_in, grad_sides):
-    c = plan.channels
-    grad_left, grad_right, grad_gate = grads
-    projected = dot(into_side[: 4 * c, :], low)
-    left_gate = jax.nn.sigmoid(projected[:c])
-    right_gate = jax.nn.sigmoid(projected[2 * c : 3 * c])
-    grad_left = mask * grad_left.astype(F32)
-    grad_right = mask * grad_right.astype(F32)
-    shared = grad_left * left_gate
-    grad_sides[:c, :] = (shared * projected[c : 2 * c] * (1.0 - left_gate)).astype(BF16)
-    grad_sides[c : 2 * c, :] = shared.astype(BF16)
-    shared = grad_right * right_gate
-    grad_sides[2 * c : 3 * c, :] = (shared * projected[3 * c :] * (1.0 - right_gate)).astype(BF16)
-    grad_sides[3 * c : 4 * c, :] = shared.astype(BF16)
-    grad_sides[4 * c :, :] = grad_gate
-    grad_in[...] += dot(low, grad_sides[...], NT)
+    return grad_gate, layer_norm_back(grad_mixed, mixed, scale, gain)
+
+
+def open_triangle_back(plan, grad, grad_gate, low, side, in_rows, mask, grad_in, grad_sides):
+    count = 2 * plan.channels
+    projected = dot(side[...], low)
+    gate = jax.nn.sigmoid(projected[:count])
+    shared = mask * grad * gate
+    grad_sides[:count, :] = (shared * projected[count:] * (1.0 - gate)).astype(BF16)
+    grad_sides[count : 2 * count, :] = shared.astype(BF16)
+    grad_sides[2 * count :, :] = grad_gate
+    grad_in[...] += dot(grad_sides[...], low, NT)
     return dot(in_rows[...], grad_sides[...])
 
 
 def attend_kernel(
-    plan, product_in, state, mats, limits, near, frames, target, motif,
-    grad_state, grad_gate, parts, grad_attend, grad_attend_out, grad_out, grad_gains, grad_struct, losses,
-    product_rows, grad_rows, gate_side, out_side, out_rows, attend_side, attend_rows, last_side, last_rows,
+    plan, full_in, state, mats, limits, near, frames, target, motif,
+    grad_state, grad_gate, sides, full, grad_attend, grad_attend_out, grad_out, grad_gains, grad_struct, losses,
+    turned_out, staged, product, parts, gate_side, out_side, out_rows, attend_side, attend_rows, last_side, last_rows,
     struct, gains, counts, places_bias, query, keys, values, probs, attended, grad_sides,
+    *sems,
 ):
     c, length, depth = plan.channels, plan.length, plan.channels // NH
     _, _, half, me = plan.here()
+    barrier_signal(plan, half, me)
+    make_product(plan, False, full_in, sides, turned_out, staged)
+    into = Swap(plan, half, me, staged, product, sems[:3])
+    out = Swap(plan, half, me, parts, full, sems[3:])
+    barrier_wait(plan)
+    into.start_all()
     fill_columns(plan, mats, (10,), gate_side)
     fill_columns(plan, mats, (11,), out_side)
     fill_rows(plan, mats, (11,), out_rows)
@@ -623,7 +668,6 @@
     fill_rows(plan, mats, (16,), last_rows)
     fill_gains(plan, mats, (2, 3, 4, 5), gains)
     struct[...] = whole_mat(plan, mats, N_MATS).T[STRUCT_LANE : STRUCT_LANE + 16].astype(BF16)
-    product_rows[...] = to_rows(plan, product_in[...])
 
     limit = limits[half]
     key_places = lax.broadcasted_iota(jnp.int32, (length, 128), 0)
@@ -652,10 +696,10 @@
     for ref in (grad_attend, grad_attend_out, grad_out, grad_gains, grad_struct, losses):
         ref[...] = jnp.zeros_like(ref)
 
-    def body(i, carry):
+    def body(block, r, i):
         before = state[i]
         normed, _ = layer_norm(before)
-        mixed, mixed_scale = layer_norm(product_rows[i].astype(F32))
+        mixed, mixed_scale = layer_norm(from_members(plan, product[:, block, r]))
         mixed_low = (mixed * gains[1]).astype(BF16)
         gating, branch = close_triangle(
             (normed * gains[0]).astype(BF16), mixed_low, gate_side, out_side
@@ -718,106 +762,125 @@
             grad_sides[2 * c + head * depth : 2 * c + (head + 1) * depth, :] = dot(
                 grad_att[part, :], share.astype(BF16), NT
             ).astype(BF16)
-        grad_attend[...] += dot(held_low, grad_sides[...], NT)
+        grad_attend[...] += dot(grad_sides[...], held_low, NT)
         grad_low = dot(attend_rows[...], grad_sides[...])
         grad_gains[1] += lane_fold(grad_low * held_normed)
         grad_held = grad_last + layer_norm_back(grad_low, held_normed, held_scale, gains[2])
         grad_state[i] = grad_held
 
-        grad_gate[i], grad_rows[i] = close_triangle_back(
+        grad_gate[i], grad_product = close_triangle_back(
             grad_held, gating, branch, mixed, mixed_scale, mixed_low, out_rows, gains[1],
             grad_out, grad_gains.at[0],
         )
-        return carry
-
-    lax.fori_loop(0, plan.own_rows, body, 0)
+        parts[:, block, r] = to_members(plan, grad_product)
+
+    each_row(plan, into.arrive, body, out.start)
     losses[1:2, :] = jnp.broadcast_to(loss_count, (1, 128))
-    parts[...] = to_channels(plan, grad_rows[...])
+    out.arrive_all()
+    into.finish()
+    out.finish()
 
 
 def turn_kernel(
-    plan, grad_parts, grad_after, grad_gate, state, first_state, product_rows, mats, limits,
-    grad_gate_out, parts, grad_in, grad_out, grad_gains,
-    left_rows, right_rows, grad_rows, into_side, in_rows, gate_side, out_side, out_rows, gains, grad_sides,
+    plan, full_in, sides, grad_after, grad_gate, state, first_state, product_one, mats, limits,
+    grad_gate_out, full, grad_in, grad_out, grad_gains,
+    grad_turned, turned_out, staged, grad_parts, parts,
+    side, in_rows, gate_side, out_side, out_rows, gains, grad_sides, *sems,
 ):
-    fill_columns(plan, mats, range(6, 10), into_side)
-    fill_rows(plan, mats, range(6, 11), in_rows)
+    c = plan.channels
+    _, _, half, me = plan.here()
+    barrier_signal(plan, half, me)
+    make_product_back(plan, False, full_in, sides, grad_turned, turned_out, staged)
+    into = Swap(plan, half, me, staged, grad_parts, sems[:3])
+    out = Swap(plan, half, me, parts, full, sems[3:])
+    barrier_wait(plan)
+    into.start_all()
+    fill_sides(plan, mats, 6, side, in_rows)
+    in_rows[:, 4 * c :] = whole_mat(plan, mats, 10).astype(BF16)
     fill_columns(plan, mats, (4,), gate_side)
     fill_columns(plan, mats, (5,), out_side)
     fill_rows(plan, mats, (5,), out_rows)
     fill_gains(plan, mats, (0, 1, 2), gains)
-    left_rows[...] = to_rows(plan, grad_parts[:, 0])
-    right_rows[...] = to_rows(plan, grad_parts[:, 1])
     for ref in (grad_in, grad_out, grad_gains):
         ref[...] = jnp.zeros_like(ref)
 
-    def body(i, carry):
+    def body(block, r, i):
         normed, scale = layer_norm(state[i])
         low = (normed * gains[2]).astype(BF16)
         grad_low = open_triangle_back(
-            plan, (left_rows[i], right_rows[i], grad_gate[i]), low, into_side, in_rows,
+            plan, from_members(plan, grad_parts[:, block, r]), grad_gate[i], low, side, in_rows,
             pair_mask(plan, limits, i), grad_in, grad_sides,
         )
         grad_gains[1] += lane_fold(grad_low * normed)
         grad = grad_after[i] + layer_norm_back(grad_low, normed, scale, gains[2])
 
         normed, _ = layer_norm(first_state[i].astype(F32))
-        mixed, mixed_scale = layer_norm(product_rows[i].astype(F32))
+        mixed, mixed_scale = layer_norm(from_members(plan, product_one[:, block, r]))
         mixed_low = (mixed * gains[1]).astype(BF16)
         gating, branch = close_triangle(
             (normed * gains[0]).astype(BF16), mixed_low, gate_side, out_side
         )
-        grad_gate_out[i], grad_rows[i] = close_triangle_back(
+        grad_gate_out[i], grad_product = close_triangle_back(
             grad, gating, branch, mixed, mixed_scale, mixed_low, out_rows, gains[1],
             grad_out, grad_gains.at[0],
         )
-        return carry
-
-    lax.fori_loop(0, plan.own_rows, body, 0)
-    parts[...] = to_channels(plan, grad_rows[...])
+        parts[:, block, r] = to_members(plan, grad_product)
+
+    each_row(plan, into.arrive, body, out.start)
+    out.arrive_all()
+    into.finish()
+    out.finish()
 
 
 def last_kernel(
-    plan, grad_parts, grad_gate, first_state, mats, limits,
+    plan, full_in, sides, grad_gate, first_state, mats, limits,
     attend_in, attend_out, second_out, gains_late, grad_struct, losses,
     second_in, first_out, gains_mid,
     packed,
-    left_rows, right_rows, into_side, in_rows, gain, grad_sides, grad_in, grad_gain,
+    grad_turned, turned_out, staged, grad_parts, side, in_rows, gain, grad_sides, grad_in, grad_gain, *sems,
 ):
     c = plan.channels
-    fill_columns(plan, mats, range(4), into_side)
-    fill_rows(plan, mats, range(5), in_rows)
+    _, _, half, me = plan.here()
+    barrier_signal(plan, half, me)
+    make_product_back(plan, True, full_in, sides, grad_turned, turned_out, staged)
+    into = Swap(plan, half, me, staged, grad_parts, sems)
+    barrier_wait(plan)
+    into.start_all()
+    fill_sides(plan, mats, 0, side, in_rows)
+    in_rows[:, 4 * c :] = whole_mat(plan, mats, 4).astype(BF16)
     fill_gains(plan, mats, (0,), gain)
-    left_rows[...] = to_rows(plan, grad_parts[:, 0])
-    right_rows[...] = to_rows(plan, grad_parts[:, 1])
     for ref in (grad_in, grad_gain):
         ref[...] = jnp.zeros_like(ref)
 
-    def body(i, carry):
+    def body(block, r, i):
         normed, _ = layer_norm(first_state[i].astype(F32))
         grad_low = open_triangle_back(
-            plan, (left_rows[i], right_rows[i], grad_gate[i]), (normed * gain[0]).astype(BF16),
-            into_side, in_rows, pair_mask(plan, limits, i), grad_in, grad_sides,
+            plan, from_members(plan, grad_parts[:, block, r]), grad_gate[i],
+            (normed * gain[0]).astype(BF16), side, in_rows, pair_mask(plan, limits, i), grad_in, grad_sides,
         )
         grad_gain[...] += lane_fold(grad_low * normed)
-        return carry
-
-    lax.fori_loop(0, plan.own_rows, body, 0)
+
+    each_row(plan, into.arrive, body, lambda block: None)
 
     def put(number, value):
         group, place = number // plan.group_mats, number % plan.group_mats
         blocks = value.reshape(2, plan.half_rows, plan.shard, c)
         for near_half in range(2):
             for row in range(plan.half_rows):
-                packed[row * plan.cols + group, near_half, place] = blocks[near_half, row].astype(BF16)
-
-    for m in range(5):
-        put(m, grad_in[:, m * c : (m + 1) * c])
-        put(6 + m, second_in[:, m * c : (m + 1) * c])
+                packed[row * plan.cols + group, 0, near_half, place] = blocks[near_half, row].astype(BF16)
+
+    mix = mixing(plan)
+    for first, ref in ((0, grad_in), (6, second_in)):
+        for place in range(2):
+            mixed = ref[2 * c * place : 2 * c * (place + 1), :].astype(BF16)
+            columns = dot(mix, mixed, TN)
+            put(first + place, columns[:c].T)
+            put(first + place + 2, columns[c:].T)
+        put(first + 4, ref[4 * c :, :].T)
     put(5, first_out[...])
     put(11, second_out[...])
     for m in range(4):
-        put(12 + m, attend_in[:, m * c : (m + 1) * c])
+        put(12 + m, attend_in[m * c : (m + 1) * c, :].T)
     put(16, attend_out[...])
 
     lanes = lax.broadcasted_iota(jnp.int32, (c, 128), 1)
@@ -836,20 +899,22 @@
     put(N_MATS + 1, extra - high.astype(F32))
     for number in range(N_MATS + 2, plan.mats):
         put(number, jnp.zeros((c, c), F32))
-
-
-def local_call(kernel, plan, args, outs, scratch, flops):
+    into.finish()
+
+
+def call(kernel, plan, args, outs, scratch, collective_id, swaps):
     specs = [
         pl.BlockSpec(memory_space=pltpu.SMEM if value.ndim == 1 else pltpu.VMEM) for value in args
     ]
-    many = isinstance(outs, (list, tuple)) and not isinstance(outs, jax.ShapeDtypeStruct)
     return pl.pallas_call(
         functools.partial(kernel, plan),
-        out_shape=tuple(outs) if many else outs,
+        out_shape=tuple(outs),
         in_specs=specs,
-        out_specs=tuple(vmem(len(outs))) if many else vmem(1)[0],
-        scratch_shapes=scratch,
-        compiler_params=pltpu.CompilerParams(vmem_limit_bytes=VMEM_LIMIT),
+        out_specs=tuple(vmem(len(outs))),
+        scratch_shapes=scratch + swap_sems(plan, swaps),
+        compiler_params=pltpu.CompilerParams(
+            collective_id=collective_id, has_side_effects=True, vmem_limit_bytes=VMEM_LIMIT
+        ),
     )(*args)
 
 
@@ -869,90 +934,98 @@
     plan, pair, frames, target, lengths, motif, neighbours, weights, weights_m, weights_v,
     struct_w, struct_m, struct_v, gains, gains_m, gains_v,
 ):
-    rows, c, length, shard = plan.own_rows, plan.channels, plan.length, plan.shard
+    rows, c, length, shard, own = plan.own_rows, plan.channels, plan.length, plan.shard, plan.own_channels
     sds = jax.ShapeDtypeStruct
-    extra = jnp.zeros((plan.mats - N_MATS, shard, c), F32)
-    extra = extra.at[0, :, :N_GAINS].set(gains.T)
-    extra = extra.at[0, :, STRUCT_LANE : STRUCT_LANE + struct_w.shape[0]].set(struct_w.T)
-    mats_own = jnp.concatenate([weights.astype(BF16), extra.astype(BF16)], axis=0)
+    comps = struct_w.shape[0]
+    extra = jnp.concatenate(
+        [
+            gains.T,
+            jnp.zeros((shard, STRUCT_LANE - N_GAINS), F32),
+            struct_w.T,
+            jnp.zeros((shard, c - STRUCT_LANE - comps), F32),
+        ],
+        axis=1,
+    )
     near = neighbours.reshape(plan.crops, plan.pieces, rows, neighbours.shape[-1])
-    pair_rows, near_rows, mats = enter(plan, pair, near, mats_own)
+    pair_rows, near_rows, mats = enter(plan, pair, near, weights, extra)
 
     by_row = (rows, c, length)
-    parts_shape = (plan.members, 2, plan.own_channels, rows, length)
-    part_shape = (plan.members, plan.own_channels, rows, length)
-    low_rows = pltpu.VMEM(by_row, BF16)
-
-    def mat_buffer(tall, wide=1):
-        return pltpu.VMEM((tall * c, wide * c), BF16)
-
-    def gain_buffer(count):
-        return pltpu.VMEM((count, c, length), F32)
-
-    state_zero, parts = local_call(
+    two = (plan.members, plan.blocks, plan.block_own, 2 * own, length)
+    one = (plan.members, plan.blocks, plan.block_own, own, length)
+    two_turned, one_turned = (2 * own, length, length), (own, length, length)
+
+    def low(*shape):
+        return pltpu.VMEM(shape, BF16)
+
+    def wide(*shape):
+        return pltpu.VMEM(shape, F32)
+
+    state_zero, full_one = call(
         first_kernel, plan, (pair_rows, mats, lengths),
-        [sds(by_row, BF16), sds(parts_shape, BF16)],
-        [mat_buffer(4), gain_buffer(1), low_rows, low_rows], 0,
+        [sds(by_row, BF16), sds(two, BF16)],
+        [low(*two), low(4 * c, c), wide(1, c, length)], 1, 1,
     )
-    full_one, product_one = product(plan, parts, True, 1)
-    state_one, product_rows, parts = local_call(
-        middle_kernel, plan, (product_one, state_zero, mats, lengths),
-        [sds(by_row, F32), sds(by_row, BF16), sds(parts_shape, BF16)],
-        [mat_buffer(1), mat_buffer(1), mat_buffer(4), gain_buffer(3), low_rows, low_rows], 0,
+    state_one, sides_one, product_one, full_two = call(
+        middle_kernel, plan, (full_one, state_zero, mats, lengths),
+        [sds(by_row, F32), sds(two_turned, BF16), sds(one, BF16), sds(two, BF16)],
+        [
+            low(*one_turned), low(*one), low(*two), low(c, c), low(c, c), low(4 * c, c),
+            wide(3, c, length),
+        ],
+        2, 2,
     )
-    full_two, product_two = product(plan, parts, False, 2)
     (
-        grad_two, grad_gate, parts, attend_in, attend_out, second_out, gains_late, grad_struct, losses,
-    ) = local_call(
+        grad_two, grad_gate, sides_two, full_grad, attend_in, attend_out, second_out, gains_late,
+        grad_struct, losses,
+    ) = call(
         attend_kernel, plan,
-        (product_two, state_one, mats, lengths, near_rows, frames, target, motif),
+        (full_two, state_one, mats, lengths, near_rows, frames, target, motif),
         [
-            sds(by_row, F32), sds(by_row, BF16), sds(part_shape, BF16),
-            sds((c, 4 * c), F32), sds((c, c), F32), sds((c, c), F32),
+            sds(by_row, F32), sds(by_row, BF16), sds(two_turned, BF16), sds(one, BF16),
+            sds((4 * c, c), F32), sds((c, c), F32), sds((c, c), F32),
             sds((3, c, 128), F32), sds((16, c), F32), sds((8, 128), F32),
         ],
         [
-            low_rows, low_rows, mat_buffer(1), mat_buffer(1), mat_buffer(1), mat_buffer(4),
-            mat_buffer(1, 4), mat_buffer(1), mat_buffer(1), pltpu.VMEM((16, c), BF16), gain_buffer(4),
-            pltpu.VMEM((rows, length), F32), pltpu.VMEM((length, 128), F32),
-            pltpu.VMEM((c, length), BF16), pltpu.VMEM((c, length), BF16), pltpu.VMEM((c, length), BF16),
-            pltpu.VMEM((NH, length, length), F32), pltpu.VMEM((c, length), F32),
-            pltpu.VMEM((4 * c, length), BF16),
+            low(*one_turned), low(*one), low(*one), low(*one),
+            low(c, c), low(c, c), low(c, c), low(4 * c, c), low(c, 4 * c), low(c, c), low(c, c),
+            low(16, c), wide(4, c, length), wide(rows, length), wide(length, 128),
+            low(c, length), low(c, length), low(c, length),
+            wide(NH, length, length), wide(c, length), low(4 * c, length),
         ],
-        0,
+        3, 2,
     )
-    grad_parts = product_back(plan, parts, full_two, False, 3)
-    grad_gate, parts, second_in, first_out, gains_mid = local_call(
+    grad_gate, full_grad, second_in, first_out, gains_mid = call(
         turn_kernel, plan,
-        (grad_parts, grad_two, grad_gate, state_one, state_zero, product_rows, mats, lengths),
+        (full_grad, sides_two, grad_two, grad_gate, state_one, state_zero, product_one, mats, lengths),
         [
-            sds(by_row, BF16), sds(part_shape, BF16), sds((c, 5 * c), F32), sds((c, c), F32),
+            sds(by_row, BF16), sds(one, BF16), sds((5 * c, c), F32), sds((c, c), F32),
             sds((2, c, 128), F32),
         ],
         [
-            low_rows, low_rows, low_rows, mat_buffer(4), mat_buffer(1, 5), mat_buffer(1), mat_buffer(1),
-            mat_buffer(1), gain_buffer(3), pltpu.VMEM((5 * c, length), BF16),
+            low(*one_turned), low(*two_turned), low(*two), low(*two), low(*one),
+            low(4 * c, c), low(c, 5 * c), low(c, c), low(c, c), low(c, c), wide(3, c, length),
+            low(5 * c, length),
         ],
-        0,
+        4, 2,
     )
-    grad_parts = product_back(plan, parts, full_one, True, 4)
-    packed = local_call(
+    (packed,) = call(
         last_kernel, plan,
         (
-            grad_parts, grad_gate, state_zero, mats, lengths, attend_in, attend_out, second_out,
-            gains_late, grad_struct, losses, second_in, first_out, gains_mid,
+            full_grad, sides_one, grad_gate, state_zero, mats, lengths, attend_in, attend_out,
+            second_out, gains_late, grad_struct, losses, second_in, first_out, gains_mid,
         ),
-        sds((plan.members, 2, plan.group_mats, shard, c), BF16),
+        [sds((plan.members, 1, 2, plan.group_mats, shard, c), BF16)],
         [
-            low_rows, low_rows, mat_buffer(4), mat_buffer(1, 5), gain_buffer(1),
-            pltpu.VMEM((5 * c, length), BF16), pltpu.VMEM((c, 5 * c), F32), pltpu.VMEM((c, 128), F32),
+            low(*one_turned), low(*two_turned), low(*two), low(*two),
+            low(4 * c, c), low(c, 5 * c), wide(1, c, length), low(5 * c, length),
+            wide(5 * c, c), wide(c, 128),
         ],
-        0,
+        5, 1,
     )
     summed = reduce_grads(plan, packed).reshape(plan.mats, shard, c)
     small = summed[N_MATS] + summed[N_MATS + 1]
     own_gains = small[:, :N_GAINS].T
-    own_struct = small[:, STRUCT_LANE : STRUCT_LANE + struct_w.shape[0]].T
+    own_struct = small[:, STRUCT_LANE : STRUCT_LANE + comps].T
     weight_new = adam_update(weights, weights_m, weights_v, summed[:N_MATS], 0.1, 0.01)
     struct_new = adam_update(struct_w, struct_m, struct_v, own_struct, 0.1, 0.01)
     gain_new = adam_update(gains, gains_m, gains_v, own_gains, 0.4, 0.0)

time: 422 us -> 318 us (0.75)
  Pallas kernels: 404 us -> 308 us
  other arithmetic: 8.62 us -> 3.03 us
    pallas_call x9 -> x5, Pallas kernels: 343 us -> 254 us  [call(): pl.pallas_call(functools.partial(kernel, plan), out_shape=tuple(outs), in...]
    pallas_call x1, Pallas kernels: 30.9 us -> 23.6 us  [reduce_grads(): pl.pallas_call(functools.partial(reduce_kernel, plan), out_shape=jax.Shap...]
    another operation x3 -> x0, other arithmetic: 4.69 us -> none  [step(): jax.shard_map(functools.partial(per_device, plan), mesh=mesh, in_specs=in...]
where the time goes in v2:
time: 318 us
  Pallas kernels  308 us (97%)
  local copies, waits for them, and re-layouts  5.58 us (2%)
    pallas_call x5, Pallas kernels, call(): pl.pallas_call(functools.partial(kernel, plan), out_shape=tuple(outs), in...  254 us
    pallas_call x1, Pallas kernels, enter(): pl.pallas_call(functools.partial(enter_kernel, plan), out_shape=(jax.Shap...  30.2 us
    pallas_call x1, Pallas kernels, reduce_grads(): pl.pallas_call(functools.partial(reduce_kernel, plan), out_shape=jax.Shap...  23.6 us

profile of v2, /device:TPU:0, one launch (start us, length us, event | category | flops | bytes accessed | tf_op | source)
XLA Modules:
  0.0 317.6 jit_solution(3617425233195415864)
XLA Ops:
  0.6 0.8 copy.26
  1.4 0.8 copy.27
  2.2 0.1 pad.1.clone
  2.3 0.1 pad.3.clone
  2.3 0.7 maximum_maximum_fusion.extra
  3.0 30.2 %shard_map.230 = (bf16[16,256,128]{2,1,0:T(8,128)(2,1)}, s32[4,16,32]{2,1,0:T(8,128)}, bf16[8,20,16,128]{3,2,1,0:T(8,128)(2,1)}) custom-call(bf16[2,32,64,128]{3,2,1,0:T(8,128)(2,1)} %pair.1, s32[2,2,16,32]{3,2,1,0:T(8,128)} %bitcast.26, f32[17,16,128]{2,1,0:T(8,128)} %weights.1, f32[16,128]{1,0:T(8,128)} %maximum_maximum_fusion.extra), custom_call_target="tpu_custom_call" | custom-call | tf_op jit(solution)/shard_map/pallas_call | solution.py:358
  33.2 37.6 %shard_map.231 = (bf16[16,128,256]{2,1,0:T(8,128)(2,1)}, bf16[16,4,4,16,256]{4,3,2,1,0:T(8,128)(2,1)}) custom-call(bf16[16,256,128]{2,1,0:T(8,128)(2,1)} %get-tuple-element.35.pair, bf16[8,20,16,128]{3,2,1,0:T(8,128)(2,1)} %get-tuple-element.36.mats, s32[2]{0:T(128)} %limits.9), custom_call_target="tpu_custom_call" | custom-call | tf_op jit(solution)/shard_map/pallas_call | solution.py:909
  70.9 45.7 %shard_map.232 = (f32[16,128,256]{2,1,0:T(8,128)}, bf16[16,256,256]{2,1,0:T(8,128)(2,1)}, bf16[16,4,4,8,256]{4,3,2,1,0:T(8,128)(2,1)}, bf16[16,4,4,16,256]{4,3,2,1,0:T(8,128)(2,1)}) custom-call(bf16[16,4,4,16,256]{4,3,2,1,0:T(8,128)(2,1)} %get-tuple-element.37.full_in, bf16[16,128,256]{2,1,0:T(8,128)(2,1)} %get-tuple-element.38.state.first_state, ...), custom_call_target="tpu_custom_call" | custom-call | tf_op jit(solution)/shard_map/pallas_call | solution.py:909
  116.6 0.6 copy.28.frames
  117.2 0.6 copy.29.target
  117.8 90.1 %shard_map.233 = (f32[16,128,256]{2,1,0:T(8,128)}, bf16[16,128,256]{2,1,0:T(8,128)(2,1)}, bf16[16,256,256]{2,1,0:T(8,128)(2,1)}, bf16[16,4,4,8,256]{4,3,2,1,0:T(...) custom-call(bf16[16,4,4,16,256]{4,3,2,1,0:T(8,128)(2,1)} %get-tuple-, ...), custom_call_target="tpu_custom_call" | custom-call | tf_op jit(solution)/shard_map/pallas_call | solution.py:909
  207.9 46.3 %shard_map.234 = (bf16[16,128,256]{2,1,0:T(8,128)(2,1)}, bf16[16,4,4,8,256]{4,3,2,1,0:T(8,128)(2,1)}, f32[640,128]{1,0:T(8,128)}, f32[128,128]{1,0:T(8,128)}, f32[2,128,128]{2,1,0:T(8,128)}) custom-call(bf16[16,4,4,8,256]{4,3,2,1,0:T(8,128)(2,1)} %get-tuple-element.42.full_in, bf16[16,256,256]{2,1,0:T(8,128)(2,1)} %get-tuple-element.43.sides, ...), custom_call_target="tpu_custom_call" | custom-call | tf_op jit(solution)/shard_map/pallas_call | solution.py:909
  254.3 0.0 copy-start.2
  254.3 34.7 %shard_map.235.grads = bf16[16,1,2,5,16,128]{5,4,3,2,1,0:T(8,128)(2,1)} custom-call(bf16[16,4,4,8,256]{4,3,2,1,0:T(8,128)(2,1)} %get-tuple-element.47.full_in, bf16[16,256,256]{2,1,0:T(8,128)(2,1)} %get-tuple-element.48.sides, bf16[16,128,256]{2,1,0:T(8,128)(2,1)} %get-tuple-element.49.grad_gate, bf16[16,128,256]{2,1,0:T(8,128)(2,1)} %get-tuple-element.38.state.first_state, ...), custom_call_target="tpu_custom_call" | custom-call | tf_op jit(solution)/shard_map/pallas_call | solution.py:909
  288.9 0.0 copy-start.4
  288.9 0.0 copy-start.7
  289.0 23.6 %shard_map.236 = f32[4,5,16,128]{3,2,1,0:T(8,128)} custom-call(bf16[16,1,2,5,16,128]{5,4,3,2,1,0:T(8,128)(2,1)} %shard_map.235.grads), custom_call_target="tpu_custom_call" | custom-call | tf_op jit(solution)/shard_map/pallas_call | solution.py:437
  312.6 1.7 multiply_subtract_fusion
  314.3 0.7 fusion.6
  315.0 0.1 copy.32
  315.1 0.1 copy.33
  315.3 0.6 multiply_subtract_fusion.1
  315.9 0.5 slice.30
  316.4 1.2 slice.24
  (22 shorter events, 0.1 us)
Async XLA Ops:
  70.9 45.7 %copy-start.5 = (f32[2,6,256]{2,0,1:T(2,128)S(1)}, f32[2,6,256]{2,0,1:T(2,128)}, u32[]{:S(2)}) copy-start(f32[2,6,256]{2,0,1:T(2,128)} %param.16) | copy-start | bytes 36868
  70.9 46.3 %copy-start.6 = (f32[2,6,256]{2,0,1:T(2,128)S(1)}, f32[2,6,256]{2,0,1:T(2,128)}, u32[]{:S(2)}) copy-start(f32[2,6,256]{2,0,1:T(2,128)} %param.17) | copy-start | bytes 36868
  254.2 58.3 %copy-start = (f32[17,16,128]{2,1,0:T(8,128)S(1)}, f32[17,16,128]{2,1,0:T(8,128)}, u32[]{:S(2)}) copy-start(f32[17,16,128]{2,1,0:T(8,128)} %weights.1) | copy-start | bytes 417796
  254.2 58.3 %copy-start.1 = (f32[17,16,128]{2,1,0:T(8,128)S(1)}, f32[17,16,128]{2,1,0:T(8,128)}, u32[]{:S(2)}) copy-start(f32[17,16,128]{2,1,0:T(8,128)} %param.23) | copy-start | bytes 417796
  254.3 58.3 %copy-start.2 = (f32[17,16,128]{2,1,0:T(8,128)S(1)}, f32[17,16,128]{2,1,0:T(8,128)}, u32[]{:S(2)}) copy-start(f32[17,16,128]{2,1,0:T(8,128)} %param.22) | copy-start | bytes 417796
  288.9 26.3 %copy-start.3 = (f32[6,16]{1,0:T(8,128)S(1)}, f32[6,16]{1,0:T(8,128)}, u32[]{:S(2)}) copy-start(f32[6,16]{1,0:T(8,128)} %param.24) | copy-start | bytes 1156
  288.9 26.3 %copy-start.4 = (f32[6,16]{1,0:T(8,128)S(1)}, f32[6,16]{1,0:T(8,128)}, u32[]{:S(2)}) copy-start(f32[6,16]{1,0:T(8,128)} %param.27) | copy-start | bytes 1156
  288.9 26.3 %copy-start.7 = (f32[6,16]{1,0:T(8,128)S(1)}, f32[6,16]{1,0:T(8,128)}, u32[]{:S(2)}) copy-start(f32[6,16]{1,0:T(8,128)} %param.29) | copy-start | bytes 1156
  289.0 26.3 %copy-start.8 = (f32[6,16]{1,0:T(8,128)S(1)}, f32[6,16]{1,0:T(8,128)}, u32[]{:S(2)}) copy-start(f32[6,16]{1,0:T(8,128)} %param.28) | copy-start | bytes 1156
  289.0 26.3 %copy-start.9 = (f32[6,16]{1,0:T(8,128)S(1)}, f32[6,16]{1,0:T(8,128)}, u32[]{:S(2)}) copy-start(f32[6,16]{1,0:T(8,128)} %param.26) | copy-start | bytes 1156
  289.0 26.3 %copy-start.10 = (f32[6,16]{1,0:T(8,128)S(1)}, f32[6,16]{1,0:T(8,128)}, u32[]{:S(2)}) copy-start(f32[6,16]{1,0:T(8,128)} %param.25) | copy-start | bytes 1156

commit v3 on v2

--- a/solution.py
+++ b/solution.py
@@ -21,6 +21,8 @@
 BF16 = jnp.bfloat16
 MESH = pl.DeviceIdType.MESH
 VMEM_LIMIT = 60 * 2**20
+WIDTH = 2
+ATTEND_WIDTH = 4
 NN = ((1,), (0,))
 NT = ((1,), (1,))
 TN = ((0,), (0,))
@@ -165,19 +167,34 @@
     return [pltpu.SemaphoreType.DMA((plan.blocks,))] * (3 * count)
 
 
-def each_row(plan, before, body, after):
+def each_group(plan, width, before, body, after):
+    width = min(width, plan.block_own)
+
     def one(block, carry):
         before(block)
 
-        def row(r, carry):
-            body(block, r, block * plan.block_own + r)
+        def group(g, carry):
+            inner = [g * width + k for k in range(width)]
+            body(block, inner, [block * plan.block_own + r for r in inner])
             return carry
 
-        lax.fori_loop(0, plan.block_own, row, 0)
+        lax.fori_loop(0, plan.block_own // width, group, 0)
         after(block)
         return carry
 
     lax.fori_loop(0, plan.blocks, one, 0)
+
+
+def beside(parts):
+    return jnp.concatenate(parts, axis=1)
+
+
+def split_rows(plan, values, count):
+    return [values[:, k * plan.length : (k + 1) * plan.length] for k in range(count)]
+
+
+def wide_gain(gain, count):
+    return beside([gain] * count)
 
 
 def vmem(count):
@@ -522,6 +539,25 @@
     return mask * jax.nn.sigmoid(projected[:count]) * projected[count:]
 
 
+def row_masks(plan, limits, rows):
+    return beside([pair_mask(plan, limits, i) for i in rows])
+
+
+def send_sides(plan, parts, block, inner, values):
+    for r, value in zip(inner, split_rows(plan, values, len(inner))):
+        parts[:, block, r] = to_members(plan, value)
+
+
+def keep_rows(plan, rows, pairs):
+    for ref, values in pairs:
+        for i, value in zip(rows, split_rows(plan, values, len(rows))):
+            ref[i] = value
+
+
+def take_rows(plan, product, block, inner):
+    return beside([from_members(plan, product[:, block, r]) for r in inner])
+
+
 def turned(plan, rows):
     return jnp.swapaxes(rows.reshape(plan.length, rows.shape[3], plan.length), 0, 1)
 
@@ -571,14 +607,17 @@
     out = Swap(plan, half, me, parts, full, sems)
     barrier_wait(plan)
 
-    def body(block, r, i):
-        value = pair[i].astype(F32).T
-        state[i] = value.astype(BF16)
-        normed, _ = layer_norm(value)
-        low = (normed * gain[0]).astype(BF16)
-        parts[:, block, r] = to_members(plan, gated_sides(plan, low, side, pair_mask(plan, limits, i)))
-
-    each_row(plan, lambda block: None, body, out.start)
+    def body(block, inner, rows):
+        values = []
+        for i in rows:
+            value = pair[i].astype(F32).T
+            state[i] = value.astype(BF16)
+            values.append(value)
+        normed, _ = layer_norm(beside(values))
+        low = (normed * wide_gain(gain[0], len(rows))).astype(BF16)
+        send_sides(plan, parts, block, inner, gated_sides(plan, low, side, row_masks(plan, limits, rows)))
+
+    each_group(plan, WIDTH, lambda block: None, body, out.start)
     out.arrive_all()
     out.finish()
 
@@ -604,20 +643,24 @@
     fill_sides(plan, mats, 6, side)
     fill_gains(plan, mats, (0, 1, 2), gains)
 
-    def body(block, r, i):
-        before = state[i].astype(F32)
+    def body(block, inner, rows):
+        count = len(rows)
+        before = beside([state[i].astype(F32) for i in rows])
         normed, _ = layer_norm(before)
-        mixed, _ = layer_norm(from_members(plan, product[:, block, r]))
+        mixed, _ = layer_norm(take_rows(plan, product, block, inner))
         gating, branch = close_triangle(
-            (normed * gains[0]).astype(BF16), (mixed * gains[1]).astype(BF16), gate_side, out_side
+            (normed * wide_gain(gains[0], count)).astype(BF16),
+            (mixed * wide_gain(gains[1], count)).astype(BF16),
+            gate_side, out_side,
         )
         after = before + gating * branch
-        state_out[i] = after
+        for i, value in zip(rows, split_rows(plan, after, count)):
+            state_out[i] = value
         normed, _ = layer_norm(after)
-        low = (normed * gains[2]).astype(BF16)
-        parts[:, block, r] = to_members(plan, gated_sides(plan, low, side, pair_mask(plan, limits, i)))
-
-    each_row(plan, into.arrive, body, out.start)
+        low = (normed * wide_gain(gains[2], count)).astype(BF16)
+        send_sides(plan, parts, block, inner, gated_sides(plan, low, side, row_masks(plan, limits, rows)))
+
+    each_group(plan, WIDTH, into.arrive, body, out.start)
     out.arrive_all()
     into.finish()
     out.finish()
@@ -648,8 +691,8 @@
     plan, full_in, state, mats, limits, near, frames, target, motif,
     grad_state, grad_gate, sides, full, grad_attend, grad_attend_out, grad_out, grad_gains, grad_struct, losses,
     turned_out, staged, product, parts, gate_side, out_side, out_rows, attend_side, attend_rows, last_side, last_rows,
-    struct, gains, counts, places_bias, query, keys, values, probs, attended, grad_sides,
-    *sems,
+    struct, gains, counts, places_bias, query, keys, values, probs, probs_low, grad_probs, grad_scores,
+    attended, grad_att, grad_sides, *sems,
 ):
     c, length, depth = plan.channels, plan.length, plan.channels // NH
     _, _, half, me = plan.here()
@@ -696,51 +739,62 @@
     for ref in (grad_attend, grad_attend_out, grad_out, grad_gains, grad_struct, losses):
         ref[...] = jnp.zeros_like(ref)
 
-    def body(block, r, i):
-        before = state[i]
+    def body(block, inner, rows):
+        count = len(rows)
+        gain = [wide_gain(gains[k], count) for k in range(4)]
+        before = beside([state[i] for i in rows])
         normed, _ = layer_norm(before)
-        mixed, mixed_scale = layer_norm(from_members(plan, product[:, block, r]))
-        mixed_low = (mixed * gains[1]).astype(BF16)
-        gating, branch = close_triangle(
-            (normed * gains[0]).astype(BF16), mixed_low, gate_side, out_side
-        )
+        mixed, mixed_scale = layer_norm(take_rows(plan, product, block, inner))
+        mixed_low = (mixed * gain[1]).astype(BF16)
+        gating, branch = close_triangle((normed * gain[0]).astype(BF16), mixed_low, gate_side, out_side)
         held = before + gating * branch
 
         held_normed, held_scale = layer_norm(held)
-        held_low = (held_normed * gains[2]).astype(BF16)
+        held_low = (held_normed * gain[2]).astype(BF16)
         projected = dot(attend_side[...], held_low)
         query[...] = (projected[:c] * depth ** (-0.5)).astype(BF16)
         keys[...] = projected[c : 2 * c].astype(BF16)
         values[...] = projected[2 * c : 3 * c].astype(BF16)
         attend_gate = jax.nn.sigmoid(projected[3 * c :])
-        bias = jnp.concatenate([places_bias[...]] * (length // 128), axis=1)
-        for head in range(NH):
-            part = slice(head * depth, (head + 1) * depth)
-            scores = dot(keys[part, :], query[part, :], TN) + bias
+        bias = beside([places_bias[...]] * (length // 128))
+        parts_of = [
+            (slice(head * depth, (head + 1) * depth), slice(k * length, (k + 1) * length), k * NH + head)
+            for k in range(count)
+            for head in range(NH)
+        ]
+        for part, lanes, slot in parts_of:
+            probs[slot] = dot(keys[part, lanes], query[part, lanes], TN)
+        for part, lanes, slot in parts_of:
+            scores = probs[slot] + bias
             powers = jnp.exp(scores - jnp.max(scores, axis=0, keepdims=True))
             share = powers * (1.0 / jnp.sum(powers, axis=0, keepdims=True))
-            probs[head] = share
-            attended[part, :] = dot(values[part, :], share.astype(BF16))
+            probs[slot] = share
+            probs_low[slot] = share.astype(BF16)
+        for part, lanes, slot in parts_of:
+            attended[part, lanes] = dot(values[part, lanes], probs_low[slot])
         gated_low = (attended[...] * attend_gate).astype(BF16)
         last = held + dot(last_side[...], gated_low)
 
         last_normed, last_scale = layer_norm(last)
-        last_low = (last_normed * gains[3]).astype(BF16)
-        edges = dot(struct[...], last_low)
-        here = places == me * plan.own_rows + i
-        frame_here = jnp.sum(jnp.where(here, frames_all, 0.0), axis=1, keepdims=True)
-        target_here = jnp.sum(jnp.where(here, target_all, 0.0), axis=1, keepdims=True)
-        weight_here = jnp.sum(jnp.where(here, weight_row, 0.0), axis=1, keepdims=True)
-        weighted = counts[pl.ds(i, 1), :] * (frames_all - frame_here)
-        residual = frame_here + jnp.sum(weighted * edges, axis=1, keepdims=True) - target_here
-        lost = weight_here * residual * residual
-        losses[0:1, :] += jnp.broadcast_to(jnp.sum(lost, axis=0, keepdims=True), (1, 128))
-        grad_update = 2.0 * residual * (weight_here * (1.0 / loss_count))
-        grad_edges = (grad_update * weighted).astype(BF16)
+        last_low = (last_normed * gain[3]).astype(BF16)
+        edges = split_rows(plan, dot(struct[...], last_low), count)
+        grad_edges = []
+        for k, i in enumerate(rows):
+            here = places == me * plan.own_rows + i
+            frame_here = jnp.sum(jnp.where(here, frames_all, 0.0), axis=1, keepdims=True)
+            target_here = jnp.sum(jnp.where(here, target_all, 0.0), axis=1, keepdims=True)
+            weight_here = jnp.sum(jnp.where(here, weight_row, 0.0), axis=1, keepdims=True)
+            weighted = counts[pl.ds(i, 1), :] * (frames_all - frame_here)
+            residual = frame_here + jnp.sum(weighted * edges[k], axis=1, keepdims=True) - target_here
+            lost = weight_here * residual * residual
+            losses[0:1, :] += jnp.broadcast_to(jnp.sum(lost, axis=0, keepdims=True), (1, 128))
+            grad_update = 2.0 * residual * (weight_here * (1.0 / loss_count))
+            grad_edges.append((grad_update * weighted).astype(BF16))
+        grad_edges = beside(grad_edges)
         grad_struct[...] += dot(grad_edges, last_low, NT)
         grad_low = dot(struct[...], grad_edges, TN)
         grad_gains[2] += lane_fold(grad_low * last_normed)
-        grad_last = layer_norm_back(grad_low, last_normed, last_scale, gains[3])
+        grad_last = layer_norm_back(grad_low, last_normed, last_scale, gain[3])
 
         grad_branch = grad_last.astype(BF16)
         grad_attend_out[...] += dot(gated_low, grad_branch, NT)
@@ -748,33 +802,36 @@
         grad_sides[3 * c :, :] = (
             grad_gated * attended[...] * attend_gate * (1.0 - attend_gate)
         ).astype(BF16)
-        grad_att = (grad_gated * attend_gate).astype(BF16)
-        for head in range(NH):
-            part = slice(head * depth, (head + 1) * depth)
-            share = probs[head]
-            grad_share = dot(values[part, :], grad_att[part, :], TN)
-            weighed = share * grad_share
-            grad_scores = (weighed - share * jnp.sum(weighed, axis=0, keepdims=True)).astype(BF16)
-            grad_sides[part, :] = (dot(keys[part, :], grad_scores) * depth ** (-0.5)).astype(BF16)
-            grad_sides[c + head * depth : c + (head + 1) * depth, :] = dot(
-                query[part, :], grad_scores, NT
+        grad_att[...] = (grad_gated * attend_gate).astype(BF16)
+        for part, lanes, slot in parts_of:
+            grad_probs[slot] = dot(values[part, lanes], grad_att[part, lanes], TN)
+        for part, lanes, slot in parts_of:
+            share = probs[slot]
+            weighed = share * grad_probs[slot]
+            grad_scores[slot] = (weighed - share * jnp.sum(weighed, axis=0, keepdims=True)).astype(BF16)
+        for part, lanes, slot in parts_of:
+            first = part.start
+            grad_sides[first : first + depth, lanes] = (
+                dot(keys[part, lanes], grad_scores[slot]) * depth ** (-0.5)
             ).astype(BF16)
-            grad_sides[2 * c + head * depth : 2 * c + (head + 1) * depth, :] = dot(
-                grad_att[part, :], share.astype(BF16), NT
+            grad_sides[c + first : c + first + depth, lanes] = dot(
+                query[part, lanes], grad_scores[slot], NT
+            ).astype(BF16)
+            grad_sides[2 * c + first : 2 * c + first + depth, lanes] = dot(
+                grad_att[part, lanes], probs_low[slot], NT
             ).astype(BF16)
         grad_attend[...] += dot(grad_sides[...], held_low, NT)
         grad_low = dot(attend_rows[...], grad_sides[...])
         grad_gains[1] += lane_fold(grad_low * held_normed)
-        grad_held = grad_last + layer_norm_back(grad_low, held_normed, held_scale, gains[2])
-        grad_state[i] = grad_held
-
-        grad_gate[i], grad_product = close_triangle_back(
-            grad_held, gating, branch, mixed, mixed_scale, mixed_low, out_rows, gains[1],
+        grad_held = grad_last + layer_norm_back(grad_low, held_normed, held_scale, gain[2])
+        gate_back, grad_product = close_triangle_back(
+            grad_held, gating, branch, mixed, mixed_scale, mixed_low, out_rows, gain[1],
             grad_out, grad_gains.at[0],
         )
-        parts[:, block, r] = to_members(plan, grad_product)
-
-    each_row(plan, into.arrive, body, out.start)
+        keep_rows(plan, rows, ((grad_state, grad_held), (grad_gate, gate_back)))
+        send_sides(plan, parts, block, inner, grad_product)
+
+    each_group(plan, ATTEND_WIDTH, into.arrive, body, out.start)
     losses[1:2, :] = jnp.broadcast_to(loss_count, (1, 128))
     out.arrive_all()
     into.finish()
@@ -804,29 +861,30 @@
     for ref in (grad_in, grad_out, grad_gains):
         ref[...] = jnp.zeros_like(ref)
 
-    def body(block, r, i):
-        normed, scale = layer_norm(state[i])
-        low = (normed * gains[2]).astype(BF16)
+    def body(block, inner, rows):
+        count = len(rows)
+        gain = [wide_gain(gains[k], count) for k in range(3)]
+        normed, scale = layer_norm(beside([state[i] for i in rows]))
+        low = (normed * gain[2]).astype(BF16)
         grad_low = open_triangle_back(
-            plan, from_members(plan, grad_parts[:, block, r]), grad_gate[i], low, side, in_rows,
-            pair_mask(plan, limits, i), grad_in, grad_sides,
+            plan, take_rows(plan, grad_parts, block, inner), beside([grad_gate[i] for i in rows]), low,
+            side, in_rows, row_masks(plan, limits, rows), grad_in, grad_sides,
         )
         grad_gains[1] += lane_fold(grad_low * normed)
-        grad = grad_after[i] + layer_norm_back(grad_low, normed, scale, gains[2])
-
-        normed, _ = layer_norm(first_state[i].astype(F32))
-        mixed, mixed_scale = layer_norm(from_members(plan, product_one[:, block, r]))
-        mixed_low = (mixed * gains[1]).astype(BF16)
-        gating, branch = close_triangle(
-            (normed * gains[0]).astype(BF16), mixed_low, gate_side, out_side
-        )
-        grad_gate_out[i], grad_product = close_triangle_back(
-            grad, gating, branch, mixed, mixed_scale, mixed_low, out_rows, gains[1],
+        grad = beside([grad_after[i] for i in rows]) + layer_norm_back(grad_low, normed, scale, gain[2])
+
+        normed, _ = layer_norm(beside([first_state[i].astype(F32) for i in rows]))
+        mixed, mixed_scale = layer_norm(take_rows(plan, product_one, block, inner))
+        mixed_low = (mixed * gain[1]).astype(BF16)
+        gating, branch = close_triangle((normed * gain[0]).astype(BF16), mixed_low, gate_side, out_side)
+        gate_back, grad_product = close_triangle_back(
+            grad, gating, branch, mixed, mixed_scale, mixed_low, out_rows, gain[1],
             grad_out, grad_gains.at[0],
         )
-        parts[:, block, r] = to_members(plan, grad_product)
-
-    each_row(plan, into.arrive, body, out.start)
+        keep_rows(plan, rows, ((grad_gate_out, gate_back),))
+        send_sides(plan, parts, block, inner, grad_product)
+
+    each_group(plan, WIDTH, into.arrive, body, out.start)
     out.arrive_all()
     into.finish()
     out.finish()
@@ -852,15 +910,16 @@
     for ref in (grad_in, grad_gain):
         ref[...] = jnp.zeros_like(ref)
 
-    def body(block, r, i):
-        normed, _ = layer_norm(first_state[i].astype(F32))
+    def body(block, inner, rows):
+        normed, _ = layer_norm(beside([first_state[i].astype(F32) for i in rows]))
         grad_low = open_triangle_back(
-            plan, from_members(plan, grad_parts[:, block, r]), grad_gate[i],
-            (normed * gain[0]).astype(BF16), side, in_rows, pair_mask(plan, limits, i), grad_in, grad_sides,
+            plan, take_rows(plan, grad_parts, block, inner), beside([grad_gate[i] for i in rows]),
+            (normed * wide_gain(gain[0], len(rows))).astype(BF16), side, in_rows,
+            row_masks(plan, limits, rows), grad_in, grad_sides,
         )
         grad_gain[...] += lane_fold(grad_low * normed)
 
-    each_row(plan, into.arrive, body, lambda block: None)
+    each_group(plan, WIDTH, into.arrive, body, lambda block: None)
 
     def put(number, value):
         group, place = number // plan.group_mats, number % plan.group_mats
@@ -950,6 +1009,9 @@
     pair_rows, near_rows, mats = enter(plan, pair, near, weights, extra)
 
     by_row = (rows, c, length)
+    wide_lanes = min(WIDTH, plan.block_own) * length
+    many = min(ATTEND_WIDTH, plan.block_own) * length
+    slots = NH * many // length
     two = (plan.members, plan.blocks, plan.block_own, 2 * own, length)
     one = (plan.members, plan.blocks, plan.block_own, own, length)
     two_turned, one_turned = (2 * own, length, length), (own, length, length)
@@ -989,8 +1051,9 @@
             low(*one_turned), low(*one), low(*one), low(*one),
             low(c, c), low(c, c), low(c, c), low(4 * c, c), low(c, 4 * c), low(c, c), low(c, c),
             low(16, c), wide(4, c, length), wide(rows, length), wide(length, 128),
-            low(c, length), low(c, length), low(c, length),
-            wide(NH, length, length), wide(c, length), low(4 * c, length),
+            low(c, many), low(c, many), low(c, many),
+            wide(slots, length, length), low(slots, length, length), wide(slots, length, length),
+            low(slots, length, length), wide(c, many), low(c, many), low(4 * c, many),
         ],
         3, 2,
     )
@@ -1004,7 +1067,7 @@
         [
             low(*one_turned), low(*two_turned), low(*two), low(*two), low(*one),
             low(4 * c, c), low(c, 5 * c), low(c, c), low(c, c), low(c, c), wide(3, c, length),
-            low(5 * c, length),
+            low(5 * c, wide_lanes),
         ],
         4, 2,
     )
@@ -1017,7 +1080,7 @@
         [sds((plan.members, 1, 2, plan.group_mats, shard, c), BF16)],
         [
             low(*one_turned), low(*two_turned), low(*two), low(*two),
-            low(4 * c, c), low(c, 5 * c), wide(1, c, length), low(5 * c, length),
+            low(4 * c, c), low(c, 5 * c), wide(1, c, length), low(5 * c, wide_lanes),
             wide(5 * c, c), wide(c, 128),
         ],
         5, 1,

time: 318 us -> 275 us (0.86)
  Pallas kernels: 308 us -> 265 us
    pallas_call x5, Pallas kernels: 254 us -> 211 us  [call(): pl.pallas_call(functools.partial(kernel, plan), out_shape=tuple(outs), in...]
where the time goes in v3:
time: 275 us; the launch traced here: 274 us
  Pallas kernels  265 us (96%)
  local copies, waits for them, and re-layouts  5.58 us (2%)
  other arithmetic  3.03 us (1%)
    pallas_call x5, Pallas kernels, call(): pl.pallas_call(functools.partial(kernel, plan), out_shape=tuple(outs), in...  211 us
    pallas_call x1, Pallas kernels, enter(): pl.pallas_call(functools.partial(enter_kernel, plan), out_shape=(jax.Shap...  30.2 us
    pallas_call x1, Pallas kernels, reduce_grads(): pl.pallas_call(functools.partial(reduce_kernel, plan), out_shape=jax.Shap...  23.5 us

profile of v3, /device:TPU:0, one launch (start us, length us, event | category | flops | bytes accessed | tf_op | source)
XLA Modules:
  0.0 274.4 jit_solution(17784886609516513582)
XLA Ops:
  0.6 0.8 copy.26
  1.4 0.8 copy.27
  2.2 0.1 pad.1.clone
  2.3 0.1 pad.3.clone
  2.3 0.7 maximum_maximum_fusion.extra
  3.0 30.2 %shard_map.230 = (bf16[16,256,128]{2,1,0:T(8,128)(2,1)}, s32[4,16,32]{2,1,0:T(8,128)}, bf16[8,20,16,128]{3,2,1,0:T(8,128)(2,1)}) custom-call(bf16[2,32,64,128]{3,2,1,0:T(8,128)(2,1)} %pair.1, s32[2,2,16,32]{3,2,1,0:T(8,128)} %bitcast.26, f32[17,16,128]{2,1,0:T(8,128)} %weights.1, f32[16,128]{1,0:T(8,128)} %maximum_maximum_fusion.extra), custom_call_target="tpu_custom_call" | custom-call | tf_op jit(solution)/shard_map/pallas_call | solution.py:375
  33.2 37.1 %shard_map.231 = (bf16[16,128,256]{2,1,0:T(8,128)(2,1)}, bf16[16,4,4,16,256]{4,3,2,1,0:T(8,128)(2,1)}) custom-call(bf16[16,256,128]{2,1,0:T(8,128)(2,1)} %get-tuple-element.35.pair, bf16[8,20,16,128]{3,2,1,0:T(8,128)(2,1)} %get-tuple-element.36.mats, s32[2]{0:T(128)} %limits.9), custom_call_target="tpu_custom_call" | custom-call | tf_op jit(solution)/shard_map/pallas_call | solution.py:968
  70.3 0.0 copy-start.6
  70.3 44.7 %shard_map.232 = (f32[16,128,256]{2,1,0:T(8,128)}, bf16[16,256,256]{2,1,0:T(8,128)(2,1)}, bf16[16,4,4,8,256]{4,3,2,1,0:T(8,128)(2,1)}, bf16[16,4,4,16,256]{4,3,2,1,0:T(8,128)(2,1)}) custom-call(bf16[16,4,4,16,256]{4,3,2,1,0:T(8,128)(2,1)} %get-tuple-element.37.full_in, bf16[16,128,256]{2,1,0:T(8,128)(2,1)} %get-tuple-element.38.state.first_state, ...), custom_call_target="tpu_custom_call" | custom-call | tf_op jit(solution)/shard_map/pallas_call | solution.py:968
  115.0 0.6 copy.28.frames
  115.6 0.6 copy.29.target
  116.3 49.2 %shard_map.233 = (f32[16,128,256]{2,1,0:T(8,128)}, bf16[16,128,256]{2,1,0:T(8,128)(2,1)}, bf16[16,256,256]{2,1,0:T(8,128)(2,1)}, bf16[16,4,4,8,256]{4,3,2,1,0:T(...) custom-call(bf16[16,4,4,16,256]{4,3,2,1,0:T(8,128)(2,1)} %get-tuple-, ...), custom_call_target="tpu_custom_call" | custom-call | tf_op jit(solution)/shard_map/pallas_call | solution.py:968
  165.5 46.6 %shard_map.234 = (bf16[16,128,256]{2,1,0:T(8,128)(2,1)}, bf16[16,4,4,8,256]{4,3,2,1,0:T(8,128)(2,1)}, f32[640,128]{1,0:T(8,128)}, f32[128,128]{1,0:T(8,128)}, f32[2,128,128]{2,1,0:T(8,128)}) custom-call(bf16[16,4,4,8,256]{4,3,2,1,0:T(8,128)(2,1)} %get-tuple-element.42.full_in, bf16[16,256,256]{2,1,0:T(8,128)(2,1)} %get-tuple-element.43.sides, ...), custom_call_target="tpu_custom_call" | custom-call | tf_op jit(solution)/shard_map/pallas_call | solution.py:968
  212.1 0.0 copy-start
  212.1 0.0 copy-start.1
  212.1 33.5 %shard_map.235.grads = bf16[16,1,2,5,16,128]{5,4,3,2,1,0:T(8,128)(2,1)} custom-call(bf16[16,4,4,8,256]{4,3,2,1,0:T(8,128)(2,1)} %get-tuple-element.47.full_in, bf16[16,256,256]{2,1,0:T(8,128)(2,1)} %get-tuple-element.48.sides, bf16[16,128,256]{2,1,0:T(8,128)(2,1)} %get-tuple-element.49.grad_gate, bf16[16,128,256]{2,1,0:T(8,128)(2,1)} %get-tuple-element.38.state.first_state, ...), custom_call_target="tpu_custom_call" | custom-call | tf_op jit(solution)/shard_map/pallas_call | solution.py:968
  245.7 23.5 %shard_map.236 = f32[4,5,16,128]{3,2,1,0:T(8,128)} custom-call(bf16[16,1,2,5,16,128]{5,4,3,2,1,0:T(8,128)(2,1)} %shard_map.235.grads), custom_call_target="tpu_custom_call" | custom-call | tf_op jit(solution)/shard_map/pallas_call | solution.py:454
  269.3 1.7 multiply_subtract_fusion
  271.0 0.7 fusion.6
  271.8 0.1 copy.32
  271.9 0.1 copy.33
  272.0 0.6 multiply_subtract_fusion.1
  272.7 0.5 slice.30
  273.2 1.2 slice.24
  (22 shorter events, 0.1 us)
Async XLA Ops:
  70.3 44.7 %copy-start.5 = (f32[2,6,256]{2,0,1:T(2,128)S(1)}, f32[2,6,256]{2,0,1:T(2,128)}, u32[]{:S(2)}) copy-start(f32[2,6,256]{2,0,1:T(2,128)} %param.16) | copy-start | bytes 36868
  70.3 45.3 %copy-start.6 = (f32[2,6,256]{2,0,1:T(2,128)S(1)}, f32[2,6,256]{2,0,1:T(2,128)}, u32[]{:S(2)}) copy-start(f32[2,6,256]{2,0,1:T(2,128)} %param.17) | copy-start | bytes 36868
  212.1 57.2 %copy-start = (f32[17,16,128]{2,1,0:T(8,128)S(1)}, f32[17,16,128]{2,1,0:T(8,128)}, u32[]{:S(2)}) copy-start(f32[17,16,128]{2,1,0:T(8,128)} %weights.1) | copy-start | bytes 417796
  212.1 57.2 %copy-start.1 = (f32[17,16,128]{2,1,0:T(8,128)S(1)}, f32[17,16,128]{2,1,0:T(8,128)}, u32[]{:S(2)}) copy-start(f32[17,16,128]{2,1,0:T(8,128)} %param.23) | copy-start | bytes 417796
  212.1 57.2 %copy-start.2 = (f32[17,16,128]{2,1,0:T(8,128)S(1)}, f32[17,16,128]{2,1,0:T(8,128)}, u32[]{:S(2)}) copy-start(f32[17,16,128]{2,1,0:T(8,128)} %param.22) | copy-start | bytes 417796
  245.7 26.3 %copy-start.3 = (f32[6,16]{1,0:T(8,128)S(1)}, f32[6,16]{1,0:T(8,128)}, u32[]{:S(2)}) copy-start(f32[6,16]{1,0:T(8,128)} %param.24) | copy-start | bytes 1156
  245.7 26.3 %copy-start.4 = (f32[6,16]{1,0:T(8,128)S(1)}, f32[6,16]{1,0:T(8,128)}, u32[]{:S(2)}) copy-start(f32[6,16]{1,0:T(8,128)} %param.27) | copy-start | bytes 1156
  245.7 26.3 %copy-start.7 = (f32[6,16]{1,0:T(8,128)S(1)}, f32[6,16]{1,0:T(8,128)}, u32[]{:S(2)}) copy-start(f32[6,16]{1,0:T(8,128)} %param.29) | copy-start | bytes 1156
  245.7 26.3 %copy-start.8 = (f32[6,16]{1,0:T(8,128)S(1)}, f32[6,16]{1,0:T(8,128)}, u32[]{:S(2)}) copy-start(f32[6,16]{1,0:T(8,128)} %param.28) | copy-start | bytes 1156
  245.7 26.3 %copy-start.9 = (f32[6,16]{1,0:T(8,128)S(1)}, f32[6,16]{1,0:T(8,128)}, u32[]{:S(2)}) copy-start(f32[6,16]{1,0:T(8,128)} %param.26) | copy-start | bytes 1156
  245.7 26.3 %copy-start.10 = (f32[6,16]{1,0:T(8,128)S(1)}, f32[6,16]{1,0:T(8,128)}, u32[]{:S(2)}) copy-start(f32[6,16]{1,0:T(8,128)} %param.25) | copy-start | bytes 1156

commit v4 on v3

v4 whole, which is shorter than its diff:
```python
import functools
import types

import jax
import jax.numpy as jnp
from jax import lax
from jax.experimental import pallas as pl
from jax.experimental.pallas import tpu as pltpu
from jax.sharding import PartitionSpec as P

NH = 4
STEP = 5
BETA_ONE = 0.5
BETA_TWO = 0.5
ADAM_EPS = 1e-08
N_MATS = 17
N_GAINS = 6
HIGH, LOW = N_MATS, N_MATS + 1
STRUCT_LANE = 8
LOSS_LANE = 32
EARLY = tuple(range(5, N_MATS))
LATE = tuple(range(5)) + (HIGH, LOW)

F32 = jnp.float32
BF16 = jnp.bfloat16
MESH = pl.DeviceIdType.MESH
VMEM_LIMIT = 62 * 2**20
WIDTH = 2
ATTEND_WIDTH = 4
NN = ((1,), (0,))
NT = ((1,), (1,))
TN = ((0,), (0,))


def dot(left, right, contract=NN):
    return lax.dot_general(left, right, (contract, ((), ())), preferred_element_type=F32)


class Plan:
    def __init__(self, mesh, pair):
        self.rows, self.cols = mesh.shape["row"], mesh.shape["col"]
        self.half_rows = self.rows // 2
        self.members = self.half_rows * self.cols
        self.crops, self.length, _, self.channels = pair
        self.middle = self.length // 2
        self.own_rows = self.length // self.members
        self.own_channels = self.channels // self.members
        self.block_rows = self.length // self.rows
        self.block_cols = self.length // self.cols
        self.side_rows = self.own_rows // 2
        self.shard = self.channels // self.rows
        self.early_slots = -(-len(EARLY) // self.cols)
        self.late_slots = -(-len(LATE) // self.cols)
        self.slots = self.early_slots + self.late_slots
        self.blocks = min(4, self.own_rows)
        self.side_blocks = self.blocks // 2
        self.block_own = self.own_rows // self.blocks

    def here(self):
        row, col = lax.axis_index("row"), lax.axis_index("col")
        half = row // self.half_rows
        return row, col, half, (row % self.half_rows) * self.cols + col

    def member(self, half, index):
        return (half * self.half_rows + index // self.cols, index % self.cols)

    def place(self, number):
        if number in EARLY:
            index, first = EARLY.index(number), 0
        else:
            index, first = LATE.index(number), self.early_slots
        return index % self.cols, first + index // self.cols

    def position(self, i):
        row, col, _, _ = self.here()
        side, r = i // self.side_rows, i % self.side_rows
        return side * self.middle + (row % self.half_rows) * self.block_rows + col * self.side_rows + r

    def natural(self, position):
        _, _, half, _ = self.here()
        return (position + half * self.middle) % self.length

    def pieces(self):
        for side in range(2):
            for member in range(self.members):
                row, col = member // self.cols, member % self.cols
                first = side * self.middle + row * self.block_rows + col * self.side_rows
                yield first, member, side * self.side_blocks


def layer_norm(values):
    center = values - jnp.mean(values, axis=0, keepdims=True)
    scale = lax.rsqrt(jnp.mean(center * center, axis=0, keepdims=True) + 1e-05)
    return center * scale, scale


def layer_norm_back(grad, normed, scale, gain):
    inner = grad * gain
    mean_one = jnp.mean(inner, axis=0, keepdims=True)
    mean_two = jnp.mean(inner * normed, axis=0, keepdims=True)
    return scale * (inner - mean_one - normed * mean_two)


def lane_fold(values):
    total = values[:, :128]
    for start in range(128, values.shape[1], 128):
        total = total + values[:, start : start + 128]
    return total


def remote(src, dst, send, recv, to):
    return pltpu.make_async_remote_copy(
        src_ref=src, dst_ref=dst, send_sem=send, recv_sem=recv, device_id=to, device_id_type=MESH
    )


class Swap:
    def __init__(self, plan, half, me, src, dst, sems):
        self.plan, self.half, self.me, self.src, self.dst = plan, half, me, src, dst
        self.send, self.recv, self.local = sems

    def start(self, block):
        plan, half, me = self.plan, self.half, self.me

        def one(off, carry):
            to = (me + off) % plan.members
            pltpu.make_async_remote_copy(
                src_ref=self.src.at[to, block],
                dst_ref=self.dst.at[me, block],
                send_sem=self.send.at[block],
                recv_sem=self.recv.at[block],
                device_id=plan.member(half, to),
                device_id_type=MESH,
            ).start()
            return carry

        lax.fori_loop(1, plan.members, one, 0)
        self.own(block).start()

    def own(self, block):
        me = self.me
        return pltpu.make_async_copy(
            self.src.at[me, block], self.dst.at[me, block], self.local.at[block]
        )

    def whole(self, block):
        others = pl.ds(0, self.plan.members - 1)
        return pltpu.make_async_remote_copy(
            src_ref=self.src.at[others, block],
            dst_ref=self.dst.at[others, block],
            send_sem=self.send.at[block],
            recv_sem=self.recv.at[block],
            device_id=self.plan.member(self.half, (self.me + 1) % self.plan.members),
            device_id_type=MESH,
        )

    def arrive(self, block):
        self.whole(block).wait_recv()
        self.own(block).wait()

    def arrive_all(self):
        def one(block, carry):
            self.arrive(block)
            return carry

        lax.fori_loop(0, self.plan.blocks, one, 0)

    def start_all(self):
        def one(block, carry):
            self.start(block)
            return carry

        lax.fori_loop(0, self.plan.blocks, one, 0)

    def finish(self):
        def one(block, carry):
            self.whole(block).wait_send()
            return carry

        lax.fori_loop(0, self.plan.blocks, one, 0)


def each_group(plan, width, before, body, after):
    width = min(width, plan.block_own)

    def one(block, carry):
        before(block)

        def group(g, carry):
            inner = [g * width + k for k in range(width)]
            body(block, inner, [block * plan.block_own + r for r in inner])
            return carry

        lax.fori_loop(0, plan.block_own // width, group, 0)
        after(block)
        return carry

    lax.fori_loop(0, plan.blocks, one, 0)


def beside(parts):
    return jnp.concatenate(parts, axis=1)


def split_rows(plan, values, count):
    return [values[:, k * plan.length : (k + 1) * plan.length] for k in range(count)]


def wide_gain(gain, count):
    return beside([gain] * count)


def greet(plan):
    row, _, half, me = plan.here()
    other = (1 - half) * plan.half_rows + row % plan.half_rows
    barrier = pltpu.get_barrier_semaphore()

    def member(off, carry):
        to = plan.member(half, (me + off) % plan.members)
        pl.semaphore_signal(barrier, inc=1, device_id=to, device_id_type=MESH)
        return carry

    lax.fori_loop(1, plan.members, member, 0)
    for col in range(plan.cols):
        pl.semaphore_signal(barrier, inc=1, device_id=(other, col), device_id_type=MESH)
    pl.semaphore_wait(barrier, plan.members - 1 + plan.cols)


def pair_copies(plan, b, far, off, k):
    row, col, half, _ = plan.here()
    other = (1 - half) * plan.half_rows + row % plan.half_rows
    crop = 1 - half if far else half
    to = (col + off) % plan.cols
    width = plan.block_cols
    there = (col * width + crop * plan.middle) % plan.length
    slot = plan.side_blocks * (1 if far else 0) + k
    return (
        b.pair.at[crop, pl.ds(to * plan.side_rows + k * plan.block_own, plan.block_own)],
        b.pair_in.at[slot, :, pl.ds(pl.multiple_of(there, width), width)],
        slot,
        (other if far else row, to),
    )


def enter_start(plan, b):
    row, col, half, _ = plan.here()
    other = (1 - half) * plan.half_rows + row % plan.half_rows
    b.mats_own[...] = jnp.zeros_like(b.mats_own)
    for m in range(N_MATS):
        b.mats_own[plan.place(m)] = b.weights[m].astype(BF16)
    b.mats_own[plan.place(HIGH)] = b.extra[...].astype(BF16)
    greet(plan)
    spot = row * plan.cols + col
    remote(b.mats_own.at[col], b.mats_in.at[spot], b.cross_sems.at[0], b.cross_sems.at[1], (other, col)).start()
    for k in range(plan.side_blocks):
        for off in range(plan.cols):
            src, dst, slot, to = pair_copies(plan, b, True, off, k)
            remote(src, dst, b.pair_sends.at[0], b.pair_recvs.at[slot], to).start()
        for off in range(1, plan.cols):
            src, dst, slot, to = pair_copies(plan, b, False, off, k)
            remote(src, dst, b.pair_sends.at[1], b.pair_recvs.at[slot], to).start()
        src, dst, slot, _ = pair_copies(plan, b, False, 0, k)
        pltpu.make_async_copy(src, dst, b.pair_local.at[slot]).start()
    remote(b.near.at[1 - half, col], b.near_far, b.near_sems.at[0], b.near_sems.at[1], (other, col)).start()
    b.mats_in[spot] = b.mats_own[col]


def share_mats(plan, b):
    row, col, half, me = plan.here()
    other = (1 - half) * plan.half_rows + row % plan.half_rows
    spot = other * plan.cols + col
    cross = remote(b.mats_own.at[col], b.mats_in.at[spot], b.cross_sems.at[0], b.cross_sems.at[1], (other, col))
    cross.wait_recv()

    def share(off, carry):
        to = plan.member(half, (me + off) % plan.members)
        for shard in (row, other):
            block = b.mats_in.at[shard * plan.cols + col]
            remote(block, block, b.share_sems.at[0], b.share_sems.at[1], to).start()
        return carry

    lax.fori_loop(1, plan.members, share, 0)
    blocks = b.mats_in.at[pl.ds(0, 2 * plan.members - 2)]
    whole = remote(blocks, blocks, b.share_sems.at[0], b.share_sems.at[1], plan.member(half, (me + 1) % plan.members))
    cross.wait_send()
    whole.wait_recv()
    whole.wait_send()


def pair_arrive(plan, b, block):
    row, _, half, me = plan.here()
    away = plan.member(half, (me + 1) % plan.members)

    @pl.when(block < plan.side_blocks)
    def _():
        part = b.pair_in.at[block, :, pl.ds(0, (plan.cols - 1) * plan.block_cols)]
        remote(part, part, b.pair_sends.at[1], b.pair_recvs.at[block], away).wait_recv()
        row, col, half, _ = plan.here()
        width = plan.block_cols
        there = (col * width + half * plan.middle) % plan.length
        pltpu.make_async_copy(
            b.pair.at[half, pl.ds(col * plan.side_rows + block * plan.block_own, plan.block_own)],
            b.pair_in.at[block, :, pl.ds(pl.multiple_of(there, width), width)],
            b.pair_local.at[block],
        ).wait()

    @pl.when(block >= plan.side_blocks)
    def _():
        part = b.pair_in.at[block]
        remote(part, part, b.pair_sends.at[0], b.pair_recvs.at[block], away).wait_recv()


def enter_finish(plan, b):
    row, col, half, _ = plan.here()
    other = (1 - half) * plan.half_rows + row % plan.half_rows
    part = b.pair.at[0]
    remote(part, part, b.pair_sends.at[0], b.pair_recvs.at[0], (other, col)).wait_send()
    part = b.pair.at[0, pl.ds(0, (plan.cols - 1) * plan.side_rows)]
    remote(part, part, b.pair_sends.at[1], b.pair_recvs.at[0], (other, col)).wait_send()
    near = remote(b.near.at[1 - half, col], b.near_far, b.near_sems.at[0], b.near_sems.at[1], (other, col))
    near.wait_send()
    near.wait_recv()


def add_grads(plan, b):
    row, col, half, _ = plan.here()
    other = (1 - half) * plan.half_rows + row % plan.half_rows
    cross = remote(b.sums.at[1 - half], b.crossed, b.add_sems.at[0], b.add_sems.at[1], (other, col))
    cross.start()
    cross.wait()
    b.total[col] = b.sums[half] + b.crossed[...]
    for off in range(1, plan.cols):
        to = (col + off) % plan.cols
        remote(b.total.at[col], b.total.at[col], b.add_sems.at[2], b.add_sems.at[3], (row, to)).start()
    blocks = b.total.at[pl.ds(0, plan.cols - 1)]
    whole = remote(blocks, blocks, b.add_sems.at[2], b.add_sems.at[3], (row, (col + 1) % plan.cols))
    whole.wait_send()
    whole.wait_recv()
    for m in range(N_MATS):
        b.summed[m] = b.total[plan.place(m)]
    b.summed[N_MATS] = b.total[plan.place(HIGH)] + b.total[plan.place(LOW)]


def whole_mat(plan, b, number):
    group, slot = plan.place(number)
    shards = [b.mats_in[row * plan.cols + group, slot].astype(F32) for row in range(plan.rows)]
    return jnp.concatenate(shards, axis=0)


def fill_columns(plan, b, numbers, into):
    for place, number in enumerate(numbers):
        into[place * plan.channels : (place + 1) * plan.channels, :] = whole_mat(
            plan, b, number
        ).T.astype(BF16)


def fill_rows(plan, b, numbers, into):
    for place, number in enumerate(numbers):
        into[:, place * plan.channels : (place + 1) * plan.channels] = whole_mat(
            plan, b, number
        ).astype(BF16)


def fill_gains(plan, b, into):
    extra = whole_mat(plan, b, HIGH)
    for number in range(N_GAINS):
        into[number] = jnp.broadcast_to(
            extra[:, number : number + 1], (plan.channels, plan.length)
        )


def mixing(plan):
    c, own = plan.channels, plan.own_channels
    row = lax.broadcasted_iota(jnp.int32, (2 * c, 2 * c), 0)
    there = (row // own) % 2 * c + row // (2 * own) * own + row % own
    return jnp.where(lax.broadcasted_iota(jnp.int32, (2 * c, 2 * c), 1) == there, 1.0, 0.0).astype(BF16)


def fill_sides(plan, b, first, side, rows=None):
    c = plan.channels
    mix = mixing(plan)
    for place in range(2):
        columns = [whole_mat(plan, b, first + place + 2 * k).T.astype(BF16) for k in range(2)]
        mixed = dot(mix, jnp.concatenate(columns, axis=0))
        side[2 * c * place : 2 * c * (place + 1), :] = mixed.astype(BF16)
        if rows is not None:
            rows[:, 2 * c * place : 2 * c * (place + 1)] = mixed.T.astype(BF16)


def pair_mask(plan, limits, i):
    _, _, half, _ = plan.here()
    limit = limits[half]
    places = plan.natural(lax.broadcasted_iota(jnp.int32, (1, plan.length), 1))
    row_place = plan.natural(plan.position(i))
    return jnp.where(jnp.logical_and(places < limit, row_place < limit), 1.0, 0.0).astype(F32)


def from_middle(plan, values):
    _, _, half, _ = plan.here()
    turned_values = beside([values[:, plan.middle :], values[:, : plan.middle]])
    return jnp.where(jnp.full(values.shape, half) == 1, turned_values, values)


def to_members(plan, values):
    return values.reshape(plan.members, values.shape[0] // plan.members, plan.length).astype(BF16)


def from_members(plan, blocks):
    return blocks.astype(F32).reshape(-1, plan.length)


def gated_sides(plan, low, side, mask):
    projected = dot(side[...], low)
    count = 2 * plan.channels
    return mask * jax.nn.sigmoid(projected[:count]) * projected[count:]


def row_masks(plan, limits, rows):
    return beside([pair_mask(plan, limits, i) for i in rows])


def send_sides(plan, parts, block, inner, values):
    for r, value in zip(inner, split_rows(plan, values, len(inner))):
        parts[:, block, r] = to_members(plan, value)


def keep_rows(plan, rows, pairs):
    for ref, values in pairs:
        for i, value in zip(rows, split_rows(plan, values, len(rows))):
            ref[i] = value


def take_rows(plan, product, block, inner):
    return beside([from_members(plan, product[:, block, r]) for r in inner])


def turned(plan, ref):
    count = ref.shape[3]
    pieces = [
        ref[member, first : first + plan.side_blocks].reshape(plan.side_rows, count, plan.length)
        for _, member, first in plan.pieces()
    ]
    return jnp.swapaxes(jnp.concatenate(pieces, axis=0), 0, 1)


def turned_back(plan, channels, into):
    values = jnp.swapaxes(channels, 0, 1)
    shape = (plan.side_blocks, plan.block_own) + values.shape[1:]
    for place, member, first in plan.pieces():
        into[member, first : first + plan.side_blocks] = values[place : place + plan.side_rows].reshape(shape)


def make_product(plan, outgoing, full, sides, turned_out, staged):
    sides[...] = turned(plan, full)
    own = plan.own_channels

    def channel(h, carry):
        turned_out[h] = dot(sides[h], sides[own + h], NT if outgoing else TN).astype(BF16)
        return carry

    lax.fori_loop(0, own, channel, 0)
    turned_back(plan, turned_out[:own], staged)


def make_product_back(plan, outgoing, grads, sides, grad_turned, turned_out, staged):
    grad_turned[...] = turned(plan, grads)
    own = plan.own_channels

    def channel(h, carry):
        left, right, grad = sides[h], sides[own + h], grad_turned[h]
        if outgoing:
            grad_left, grad_right = dot(grad, right), dot(grad, left, TN)
        else:
            grad_left, grad_right = dot(right, grad, NT), dot(left, grad)
        turned_out[h] = grad_left.astype(BF16)
        turned_out[own + h] = grad_right.astype(BF16)
        return carry

    lax.fori_loop(0, own, channel, 0)
    turned_back(plan, turned_out[...], staged)


def first_phase(plan, b, out):
    def body(block, inner, rows):
        values = []
        for r, i in zip(inner, rows):
            value = b.pair_in[block, r].astype(F32).T
            b.state_zero[i] = value.astype(BF16)
            values.append(value)
        normed, _ = layer_norm(beside(values))
        low = (normed * wide_gain(b.gains[0], len(rows))).astype(BF16)
        masks = row_masks(plan, b.limits, rows)
        send_sides(plan, b.parts_two, block, inner, gated_sides(plan, low, b.side_one, masks))

    each_group(plan, WIDTH, lambda block: pair_arrive(plan, b, block), body, out.start)


def close_triangle(low, mixed_low, gate_side, out_side):
    gating = jax.nn.sigmoid(dot(gate_side[...], low))
    return gating, dot(out_side[...], mixed_low)


def middle_phase(plan, b, into, out):
    def body(block, inner, rows):
        count = len(rows)
        before = beside([b.state_zero[i].astype(F32) for i in rows])
        normed, _ = layer_norm(before)
        mixed, _ = layer_norm(take_rows(plan, b.product_one, block, inner))
        gating, branch = close_triangle(
            (normed * wide_gain(b.gains[0], count)).astype(BF16),
            (mixed * wide_gain(b.gains[1], count)).astype(BF16),
            b.gate_side_one, b.out_side_one,
        )
        after = before + gating * branch
        keep_rows(plan, rows, ((b.state_one, after),))
        normed, _ = layer_norm(after)
        low = (normed * wide_gain(b.gains[2], count)).astype(BF16)
        masks = row_masks(plan, b.limits, rows)
        send_sides(plan, b.parts_two, block, inner, gated_sides(plan, low, b.side_two, masks))

    each_group(plan, WIDTH, into.arrive, body, out.start)


def close_triangle_back(grad, gating, branch, mixed, scale, mixed_low, out_rows, gain, grad_out, grad_gain):
    grad_gate = (grad * branch * gating * (1.0 - gating)).astype(BF16)
    grad_branch = (grad * gating).astype(BF16)
    grad_out[...] += dot(mixed_low, grad_branch, NT)
    grad_mixed = dot(out_rows[...], grad_branch)
    grad_gain[...] += lane_fold(grad_mixed * mixed)
    return grad_gate, layer_norm_back(grad_mixed, mixed, scale, gain)


def open_triangle_back(plan, grad, grad_gate, low, side, in_rows, mask, grad_in, grad_sides):
    count = 2 * plan.channels
    projected = dot(side[...], low)
    gate = jax.nn.sigmoid(projected[:count])
    shared = mask * grad * gate
    grad_sides[:count, :] = (shared * projected[count:] * (1.0 - gate)).astype(BF16)
    grad_sides[count : 2 * count, :] = shared.astype(BF16)
    grad_sides[2 * count :, :] = grad_gate
    grad_in[...] += dot(grad_sides[...], low, NT)
    return dot(in_rows[...], grad_sides[...])


def attend_phase(plan, b, into, out):
    c, length, depth = plan.channels, plan.length, plan.channels // NH
    _, _, half, _ = plan.here()
    limit = b.limits[half]
    key_places = plan.natural(lax.broadcasted_iota(jnp.int32, (length, 128), 0))
    b.places_bias[...] = jnp.where(key_places < limit, 0.0, -1e9).astype(F32)
    col = lax.axis_index("col")
    lists = jnp.concatenate([b.near[half, col], b.near_far[...]], axis=0)
    row_places = plan.natural(lax.broadcasted_iota(jnp.int32, (plan.own_rows, length), 1))
    total = jnp.zeros((plan.own_rows, length), F32)
    for entry in range(lists.shape[1]):
        total += jnp.where(lists[:, entry : entry + 1] == row_places, 1.0, 0.0).astype(F32)
    b.counts[...] = total

    places = lax.broadcasted_iota(jnp.int32, (1, length), 1)
    counted = jnp.zeros((1, length), F32)
    for crop in range(plan.crops):
        counted += jnp.where(places < b.limits[crop], 1.0, 0.0).astype(F32) * (
            1 - b.motif[crop : crop + 1, :]
        ).astype(F32)
    loss_count = jnp.sum(counted, axis=1, keepdims=True)
    weight_row = jnp.where(places < limit, 1.0, 0.0).astype(F32) * (
        1 - b.motif[pl.ds(half, 1), :]
    ).astype(F32)
    spare = jnp.zeros((16 - b.frames.shape[1], length), F32)
    frames_all = from_middle(plan, jnp.concatenate([b.frames[half], spare], axis=0))
    target_all = from_middle(plan, jnp.concatenate([b.target[half], spare], axis=0))
    weight_row = from_middle(plan, weight_row)


    def body(block, inner, rows):
        count = len(rows)
        gain = [wide_gain(b.gains[k], count) for k in range(2, 6)]
        before = beside([b.state_one[i] for i in rows])
        normed, _ = layer_norm(before)
        mixed, mixed_scale = layer_norm(take_rows(plan, b.product_two, block, inner))
        mixed_low = (mixed * gain[1]).astype(BF16)
        gating, branch = close_triangle((normed * gain[0]).astype(BF16), mixed_low, b.gate_side_two, b.out_side_two)
        held = before + gating * branch

        held_normed, held_scale = layer_norm(held)
        held_low = (held_normed * gain[2]).astype(BF16)
        projected = dot(b.attend_side[...], held_low)
        b.query[...] = (projected[:c] * depth ** (-0.5)).astype(BF16)
        b.keys[...] = projected[c : 2 * c].astype(BF16)
        b.values[...] = projected[2 * c : 3 * c].astype(BF16)
        attend_gate = jax.nn.sigmoid(projected[3 * c :])
        bias = beside([b.places_bias[...]] * (length // 128))
        parts_of = [
            (slice(head * depth, (head + 1) * depth), slice(k * length, (k + 1) * length), k * NH + head)
            for k in range(count)
            for head in range(NH)
        ]
        for part, lanes, slot in parts_of:
            b.probs[slot] = dot(b.keys[part, lanes], b.query[part, lanes], TN)
        for part, lanes, slot in parts_of:
            scores = b.probs[slot] + bias
            powers = jnp.exp(scores - jnp.max(scores, axis=0, keepdims=True))
            share = powers * (1.0 / jnp.sum(powers, axis=0, keepdims=True))
            b.probs[slot] = share
            b.probs_low[slot] = share.astype(BF16)
        for part, lanes, slot in parts_of:
            b.attended[part, lanes] = dot(b.values[part, lanes], b.probs_low[slot])
        gated_low = (b.attended[...] * attend_gate).astype(BF16)
        last = held + dot(b.last_side[...], gated_low)

        last_normed, last_scale = layer_norm(last)
        last_low = (last_normed * gain[3]).astype(BF16)
        edges = split_rows(plan, dot(b.struct[...], last_low), count)
        grad_edges = []
        for k, i in enumerate(rows):
            here = places == plan.position(i)
            frame_here = jnp.sum(jnp.where(here, frames_all, 0.0), axis=1, keepdims=True)
            target_here = jnp.sum(jnp.where(here, target_all, 0.0), axis=1, keepdims=True)
            weight_here = jnp.sum(jnp.where(here, weight_row, 0.0), axis=1, keepdims=True)
            weighted = b.counts[pl.ds(i, 1), :] * (frames_all - frame_here)
            residual = frame_here + jnp.sum(weighted * edges[k], axis=1, keepdims=True) - target_here
            lost = weight_here * residual * residual
            b.losses[0:1, :] += jnp.broadcast_to(jnp.sum(lost, axis=0, keepdims=True), (1, 128))
            grad_update = 2.0 * residual * (weight_here * (1.0 / loss_count))
            grad_edges.append((grad_update * weighted).astype(BF16))
        grad_edges = beside(grad_edges)
        b.grad_struct[...] += dot(grad_edges, last_low, NT)
        grad_low = dot(b.struct[...], grad_edges, TN)
        b.grad_gains[5] += lane_fold(grad_low * last_normed)
        grad_last = layer_norm_back(grad_low, last_normed, last_scale, gain[3])

        grad_branch = grad_last.astype(BF16)
        b.grad_attend_out[...] += dot(gated_low, grad_branch, NT)
        grad_gated = dot(b.last_rows[...], grad_branch)
        b.grad_sides[3 * c :, :] = (
            grad_gated * b.attended[...] * attend_gate * (1.0 - attend_gate)
        ).astype(BF16)
        b.grad_att[...] = (grad_gated * attend_gate).astype(BF16)
        for part, lanes, slot in parts_of:
            b.grad_probs[slot] = dot(b.values[part, lanes], b.grad_att[part, lanes], TN)
        for part, lanes, slot in parts_of:
            share = b.probs[slot]
            weighed = share * b.grad_probs[slot]
            b.grad_scores[slot] = (weighed - share * jnp.sum(weighed, axis=0, keepdims=True)).astype(BF16)
        for part, lanes, slot in parts_of:
            first = part.start
            b.grad_sides[first : first + depth, lanes] = (
                dot(b.keys[part, lanes], b.grad_scores[slot]) * depth ** (-0.5)
            ).astype(BF16)
            b.grad_sides[c + first : c + first + depth, lanes] = dot(
                b.query[part, lanes], b.grad_scores[slot], NT
            ).astype(BF16)
            b.grad_sides[2 * c + first : 2 * c + first + depth, lanes] = dot(
                b.grad_att[part, lanes], b.probs_low[slot], NT
            ).astype(BF16)
        b.grad_attend[...] += dot(b.grad_sides[...], held_low, NT)
        grad_low = dot(b.attend_rows[...], b.grad_sides[...])
        b.grad_gains[4] += lane_fold(grad_low * held_normed)
        grad_held = grad_last + layer_norm_back(grad_low, held_normed, held_scale, gain[2])
        gate_back, grad_product = close_triangle_back(
            grad_held, gating, branch, mixed, mixed_scale, mixed_low, b.out_rows_two, gain[1],
            b.grad_out_two, b.grad_gains.at[3],
        )
        keep_rows(plan, rows, ((b.grad_state, grad_held), (b.grad_gate, gate_back)))
        send_sides(plan, b.parts_one, block, inner, grad_product)

    each_group(plan, ATTEND_WIDTH, into.arrive, body, out.start)
    b.losses[1:2, :] = jnp.broadcast_to(loss_count, (1, 128))


def turn_phase(plan, b, into, out):
    sides = b.grad_sides_wide

    def body(block, inner, rows):
        count = len(rows)
        gain = [wide_gain(b.gains[k], count) for k in range(3)]
        normed, scale = layer_norm(beside([b.state_one[i] for i in rows]))
        low = (normed * gain[2]).astype(BF16)
        grad_low = open_triangle_back(
            plan, take_rows(plan, b.grad_parts_two, block, inner), beside([b.grad_gate[i] for i in rows]),
            low, b.side_two, b.in_rows_two, row_masks(plan, b.limits, rows), b.grad_in_two, sides,
        )
        b.grad_gains[2] += lane_fold(grad_low * normed)
        grad = beside([b.grad_state[i] for i in rows]) + layer_norm_back(grad_low, normed, scale, gain[2])

        normed, _ = layer_norm(beside([b.state_zero[i].astype(F32) for i in rows]))
        mixed, mixed_scale = layer_norm(take_rows(plan, b.product_one, block, inner))
        mixed_low = (mixed * gain[1]).astype(BF16)
        gating, branch = close_triangle(
            (normed * gain[0]).astype(BF16), mixed_low, b.gate_side_one, b.out_side_one
        )
        gate_back, grad_product = close_triangle_back(
            grad, gating, branch, mixed, mixed_scale, mixed_low, b.out_rows_one, gain[1],
            b.grad_out_one, b.grad_gains.at[1],
        )
        keep_rows(plan, rows, ((b.grad_gate, gate_back),))
        send_sides(plan, b.parts_one, block, inner, grad_product)

    each_group(plan, WIDTH, into.arrive, body, out.start)


def last_phase(plan, b, into):
    def body(block, inner, rows):
        normed, _ = layer_norm(beside([b.state_zero[i].astype(F32) for i in rows]))
        grad_low = open_triangle_back(
            plan, take_rows(plan, b.grad_parts_one, block, inner), beside([b.grad_gate[i] for i in rows]),
            (normed * wide_gain(b.gains[0], len(rows))).astype(BF16), b.side_one, b.in_rows_one,
            row_masks(plan, b.limits, rows), b.grad_in_one, b.grad_sides_wide,
        )
        b.grad_gains[0] += lane_fold(grad_low * normed)

    each_group(plan, WIDTH, into.arrive, body, lambda block: None)


def put(plan, packed, first, number, value):
    group, slot = plan.place(number)
    blocks = value.reshape(2, plan.half_rows, plan.shard, plan.channels).astype(BF16)
    for half in range(2):
        for row in range(plan.half_rows):
            packed[row * plan.cols + group, 0, half, slot - first] = blocks[half, row]


def put_sides(plan, packed, first_slot, first, grads):
    c = plan.channels
    mix = mixing(plan)
    for place in range(2):
        mixed = grads[2 * c * place : 2 * c * (place + 1), :].astype(BF16)
        columns = dot(mix, mixed, TN)
        put(plan, packed, first_slot, first + place, columns[:c].T)
        put(plan, packed, first_slot, first + place + 2, columns[c:].T)
    put(plan, packed, first_slot, first + 4, grads[4 * c :, :].T)


def pack_early(plan, b):
    c = plan.channels
    b.packed_early[...] = jnp.zeros_like(b.packed_early)
    put(plan, b.packed_early, 0, 5, b.grad_out_one[...])
    put_sides(plan, b.packed_early, 0, 6, b.grad_in_two)
    put(plan, b.packed_early, 0, 11, b.grad_out_two[...])
    for m in range(4):
        put(plan, b.packed_early, 0, 12 + m, b.grad_attend[m * c : (m + 1) * c, :].T)
    put(plan, b.packed_early, 0, 16, b.grad_attend_out[...])


def pack_late(plan, b):
    c, first = plan.channels, plan.early_slots
    put_sides(plan, b.packed_late, first, 0, b.grad_in_one)
    lanes = lax.broadcasted_iota(jnp.int32, (c, 128), 1)
    extra = jnp.zeros((c, 128), F32)
    for m in range(N_GAINS):
        extra += jnp.where(lanes == m, jnp.sum(b.grad_gains[m], axis=1, keepdims=True), 0.0)
    padded = jnp.concatenate(
        [
            jnp.zeros((STRUCT_LANE, c), F32),
            b.grad_struct[...],
            jnp.zeros((128 - STRUCT_LANE - 16, c), F32),
        ],
        axis=0,
    )
    extra += padded.T
    extra += jnp.where(lanes == LOSS_LANE, b.losses[0:1, :], 0.0)
    high = extra.astype(BF16)
    put(plan, b.packed_late, first, HIGH, high.astype(F32))
    put(plan, b.packed_late, first, LOW, extra - high.astype(F32))


def fill_late(plan, b):
    fill_columns(plan, b, (4,), b.gate_side_one)
    fill_columns(plan, b, (5,), b.out_side_one)
    fill_sides(plan, b, 6, b.side_two, b.in_rows_two)
    c = plan.channels
    b.in_rows_one[:, 4 * c :] = whole_mat(plan, b, 4).astype(BF16)
    b.in_rows_two[:, 4 * c :] = whole_mat(plan, b, 10).astype(BF16)
    fill_rows(plan, b, (5,), b.out_rows_one)
    fill_columns(plan, b, (10,), b.gate_side_two)
    fill_columns(plan, b, (11,), b.out_side_two)
    fill_rows(plan, b, (11,), b.out_rows_two)
    fill_columns(plan, b, range(12, 16), b.attend_side)
    fill_rows(plan, b, range(12, 16), b.attend_rows)
    fill_columns(plan, b, (16,), b.last_side)
    fill_rows(plan, b, (16,), b.last_rows)
    b.struct[...] = whole_mat(plan, b, HIGH).T[STRUCT_LANE : STRUCT_LANE + 16].astype(BF16)
    for ref in (
        b.grad_attend, b.grad_attend_out, b.grad_in_one, b.grad_in_two, b.grad_out_one, b.grad_out_two,
        b.grad_gains, b.grad_struct, b.losses, b.packed_late,
    ):
        ref[...] = jnp.zeros_like(ref)


def step_kernel(plan, names, *refs):
    b = types.SimpleNamespace(**dict(zip(names, refs)))
    _, _, half, me = plan.here()

    def swap(number, src, dst):
        sems = [ref.at[number] for ref in (b.swap_sends, b.swap_recvs, b.swap_locals)]
        return Swap(plan, half, me, src, dst, sems)

    sides_one = swap(0, b.parts_two, b.full_one)
    products_one = swap(1, b.staged_one, b.product_one)
    sides_two = swap(2, b.parts_two, b.full_two)
    products_two = swap(3, b.staged_one, b.product_two)
    grads_two = swap(4, b.parts_one, b.full_grad_two)
    parts_two = swap(5, b.staged_two, b.grad_parts_two)
    grads_one = swap(6, b.parts_one, b.full_grad_one)
    parts_one = swap(7, b.staged_two, b.grad_parts_one)
    early = swap(8, b.packed_early, b.got_early)
    late = swap(9, b.packed_late, b.got_late)

    enter_start(plan, b)
    share_mats(plan, b)
    fill_sides(plan, b, 0, b.side_one, b.in_rows_one)
    fill_gains(plan, b, b.gains)
    first_phase(plan, b, sides_one)
    fill_late(plan, b)
    enter_finish(plan, b)
    sides_one.arrive_all()
    sides_one.finish()

    make_product(plan, True, b.full_one, b.sides_one, b.turned_out, b.staged_one)
    products_one.start_all()
    middle_phase(plan, b, products_one, sides_two)
    products_one.finish()
    sides_two.arrive_all()

    make_product(plan, False, b.full_two, b.sides_two, b.turned_out, b.staged_one)
    products_two.start_all()
    attend_phase(plan, b, products_two, grads_two)
    sides_two.finish()
    products_two.finish()
    grads_two.arrive_all()
    grads_two.finish()

    make_product_back(
        plan, False, b.full_grad_two, b.sides_two, b.grad_turned, b.turned_out, b.staged_two
    )
    parts_two.start_all()
    turn_phase(plan, b, parts_two, grads_one)
    parts_two.finish()
    pack_early(plan, b)
    grads_one.arrive_all()
    grads_one.finish()

    make_product_back(
        plan, True, b.full_grad_one, b.sides_one, b.grad_turned, b.turned_out, b.staged_two
    )
    parts_one.start_all()
    early.start(0)
    last_phase(plan, b, parts_one)
    pack_late(plan, b)
    late.start(0)
    parts_one.finish()
    early.arrive(0)
    b.sums[:, : plan.early_slots] = jnp.sum(b.got_early[:, 0].astype(F32), axis=0)
    late.arrive(0)
    b.sums[:, plan.early_slots :] = jnp.sum(b.got_late[:, 0].astype(F32), axis=0)
    add_grads(plan, b)
    early.whole(0).wait_send()
    late.whole(0).wait_send()


def step_buffers(plan, lists):
    c, length, own, members = plan.channels, plan.length, plan.own_channels, plan.members
    wide_lanes = min(WIDTH, plan.block_own) * length
    many = min(ATTEND_WIDTH, plan.block_own) * length
    slots = NH * many // length
    by_row = (plan.own_rows, c, length)
    two = (members, plan.blocks, plan.block_own, 2 * own, length)
    one = (members, plan.blocks, plan.block_own, own, length)
    early = (members, 1, 2, plan.early_slots, plan.shard, c)
    late = (members, 1, 2, plan.late_slots, plan.shard, c)
    group = (plan.slots, plan.shard, c)
    dma = pltpu.SemaphoreType.DMA

    def low(*shape):
        return pltpu.VMEM(shape, BF16)

    def wide(*shape):
        return pltpu.VMEM(shape, F32)

    return dict(
        pair_in=low(plan.blocks, plan.block_own, length, c),
        near_far=pltpu.VMEM((plan.side_rows, lists), jnp.int32),
        mats_own=low(plan.cols, *group),
        mats_in=low(plan.rows * plan.cols, *group),
        state_zero=low(*by_row), state_one=wide(*by_row), grad_state=wide(*by_row), grad_gate=low(*by_row),
        parts_two=low(*two), parts_one=low(*one), staged_one=low(*one), staged_two=low(*two),
        full_one=low(*two), full_two=low(*two), product_one=low(*one), product_two=low(*one),
        full_grad_one=low(*one), full_grad_two=low(*one), grad_parts_one=low(*two), grad_parts_two=low(*two),
        sides_one=low(2 * own, length, length), sides_two=low(2 * own, length, length),
        turned_out=low(2 * own, length, length), grad_turned=low(own, length, length),
        side_one=low(4 * c, c), side_two=low(4 * c, c), in_rows_one=low(c, 5 * c), in_rows_two=low(c, 5 * c),
        gate_side_one=low(c, c), gate_side_two=low(c, c), out_side_one=low(c, c), out_side_two=low(c, c),
        out_rows_one=low(c, c), out_rows_two=low(c, c), attend_side=low(4 * c, c), attend_rows=low(c, 4 * c),
        last_side=low(c, c), last_rows=low(c, c), struct=low(16, c), gains=wide(N_GAINS, c, length),
        counts=wide(plan.own_rows, length), places_bias=wide(length, 128),
        query=low(c, many), keys=low(c, many), values=low(c, many),
        probs=wide(slots, length, length), probs_low=low(slots, length, length),
        grad_probs=wide(slots, length, length), grad_scores=low(slots, length, length),
        attended=wide(c, many), grad_att=low(c, many), grad_sides=low(4 * c, many),
        grad_sides_wide=low(5 * c, wide_lanes),
        grad_attend=wide(4 * c, c), grad_attend_out=wide(c, c), grad_in_one=wide(5 * c, c),
        grad_in_two=wide(5 * c, c), grad_out_one=wide(c, c), grad_out_two=wide(c, c),
        grad_gains=wide(N_GAINS, c, 128), grad_struct=wide(16, c),
        packed_early=low(*early), packed_late=low(*late), got_early=low(*early), got_late=low(*late),
        sums=wide(2, *group), crossed=wide(*group), total=wide(plan.cols, *group),
        pair_sends=dma((2,)), pair_recvs=dma((plan.blocks,)), pair_local=dma((plan.side_blocks,)),
        near_sems=dma((2,)), cross_sems=dma((2,)), share_sems=dma((2,)), add_sems=dma((4,)),
        swap_sends=dma((10, plan.blocks)), swap_recvs=dma((10, plan.blocks)), swap_locals=dma((10, plan.blocks)),
    )


def step_call(plan, pair, near, weights, extra, limits, frames, target, motif):
    buffers = step_buffers(plan, near.shape[-1])
    spec = pl.BlockSpec(memory_space=pltpu.VMEM)
    names = ["pair", "near", "weights", "extra", "limits", "frames", "target", "motif", "summed", "losses"]
    return pl.pallas_call(
        functools.partial(step_kernel, plan, names + list(buffers)),
        out_shape=(
            jax.ShapeDtypeStruct((N_MATS + 1, plan.shard, plan.channels), F32),
            jax.ShapeDtypeStruct((8, 128), F32),
        ),
        in_specs=[
            pl.BlockSpec(memory_space=pl.ANY), spec, spec, spec,
            pl.BlockSpec(memory_space=pltpu.SMEM), spec, spec, spec,
        ],
        out_specs=(spec, spec),
        scratch_shapes=list(buffers.values()),
        compiler_params=pltpu.CompilerParams(
            collective_id=0, has_side_effects=True, vmem_limit_bytes=VMEM_LIMIT
        ),
    )(pair, near, weights, extra, limits, frames, target, motif)


def adam_update(param, first, second, gradient, rate, decay):
    first_new = BETA_ONE * first + (1.0 - BETA_ONE) * gradient
    second_new = BETA_TWO * second + (1.0 - BETA_TWO) * gradient * gradient
    first_hat = first_new / (1.0 - BETA_ONE**STEP)
    second_hat = second_new / (1.0 - BETA_TWO**STEP)
    return (
        first_new,
        second_new,
        param - rate * (first_hat / (jnp.sqrt(second_hat) + ADAM_EPS) + decay * param),
    )


def per_device(
    plan, pair, frames, target, lengths, motif, neighbours, weights, weights_m, weights_v,
    struct_w, struct_m, struct_v, gains, gains_m, gains_v,
):
    c, shard = plan.channels, plan.shard
    comps = struct_w.shape[0]
    extra = jnp.concatenate(
        [
            gains.T,
            jnp.zeros((shard, STRUCT_LANE - N_GAINS), F32),
            struct_w.T,
            jnp.zeros((shard, c - STRUCT_LANE - comps), F32),
        ],
        axis=1,
    )
    near = neighbours.reshape(plan.crops, plan.cols, plan.side_rows, neighbours.shape[-1])
    summed, losses = step_call(plan, pair, near, weights, extra, lengths, frames, target, motif)
    small = summed[N_MATS]
    own_gains = small[:, :N_GAINS].T
    own_struct = small[:, STRUCT_LANE : STRUCT_LANE + comps].T
    weight_new = adam_update(weights, weights_m, weights_v, summed[:N_MATS], 0.1, 0.01)
    struct_new = adam_update(struct_w, struct_m, struct_v, own_struct, 0.1, 0.01)
    gain_new = adam_update(gains, gains_m, gains_v, own_gains, 0.4, 0.0)
    return (small[0, LOSS_LANE], losses[1, 0]) + weight_new + struct_new + gain_new


def solution(mesh):
    in_specs = (
        P(None, "row", "col", None), P(), P(), P(), P(), P(None, "row", None),
        P(None, "row", None), P(None, "row", None), P(None, "row", None),
    ) + (P(None, "row"),) * 6
    out_specs = (P(), P()) + (P(None, "row", None),) * 3 + (P(None, "row"),) * 6

    def step(pair, *rest):
        plan = Plan(mesh, pair.shape)
        return jax.shard_map(
            functools.partial(per_device, plan),
            mesh=mesh, in_specs=in_specs, out_specs=out_specs, check_vma=False,
        )(pair, *rest)

    return step
```

time: 275 us -> 239 us (0.87)
  Pallas kernels: 265 us -> 224 us
  local copies, waits for them, and re-layouts: 5.58 us -> 11.4 us
    pallas_call x7 -> x1, Pallas kernels: 265 us -> 224 us  [step_call(): pl.pallas_call(functools.partial(step_kernel, plan, names + list(buffers)...]
    unnamed x28 -> x36, local copies, waits for them, and re-layouts: 3.01 us -> 8.71 us
where the time goes in v4:
time: 239 us; the launch traced here: 238 us
  Pallas kernels  224 us (94%)
  local copies, waits for them, and re-layouts  11.4 us (5%)
  other arithmetic  2.48 us (1%)
    pallas_call x1, Pallas kernels, step_call(): pl.pallas_call(functools.partial(step_kernel, plan, names + list(buffers)...  224 us
    unnamed x36, local copies, waits for them, and re-layouts  8.71 us

profile of v4, /device:TPU:0, one launch (start us, length us, event | category | flops | bytes accessed | tf_op | source)
XLA Modules:
  0.0 238.1 jit_solution(12796326836142047028)
XLA Ops:
  0.8 0.5 copy-done.5
  1.4 0.6 copy-done.6
  2.0 0.1 copy.44
  2.1 0.7 maximum_maximum_fusion.refs_3_
  2.9 0.6 copy-done.8
  3.5 0.1 copy.51
  3.6 0.6 copy-done.9
  4.2 0.1 copy.55
  4.3 0.5 copy-done.3
  4.9 0.6 copy.46.refs_5_
  5.5 0.1 copy-done.4
  5.6 0.6 copy.47.refs_6_
  6.2 223.6 %shard_map.230 = (f32[18,16,128]{2,1,0:T(8,128)}, f32[8,128]{1,0:T(8,128)}) custom-call(bf16[2,32,64,128]{3,2,1,0:T(8,128)(2,1)} %refs_0_.1, s32[2,4,8,32]{3,2,1,0:T(8,128)} %bitcast.25, f32[17,16,128]{2,1,0:T(8,128)} %refs_2_.1, f32[16,128]{1,0:T(8,128)} %maximum_maximum_fusion.refs_3_, s32[2]{0:T(128)} %refs_4_.1, f32[2,6,256]{2,1,0:T(8,128)} %copy.46.refs_5_, ...), custom_call_target="tpu_custom_call" | custom-call | tf_op jit(solution)/shard_map/pallas_call | solution.py:916
  229.8 1.2 slice.20
  231.0 0.7 slice_bitcast_fusion.2
  231.7 0.6 slice.24
  232.3 0.1 multiply_subtract_fusion.1
  232.4 0.7 copy.67
  233.1 0.7 copy.66
  233.7 0.7 copy.65
  234.4 0.7 copy.64
  235.1 0.7 copy.63
  235.7 0.7 copy.62
  236.4 1.7 multiply_subtract_fusion
  (23 shorter events, 0.4 us)
Async XLA Ops:
  0.6 0.7 copy-start.5
  1.3 0.7 copy-start.6
  2.1 0.7 copy-start.7
  2.8 0.7 copy-start.8
  3.5 0.7 copy-start.9
  3.5 0.8 copy-start.10
  4.2 0.7 copy-start.3
  4.9 0.7 copy-start.4
  6.2 230.2 %copy-start.1 = (f32[17,16,128]{2,1,0:T(8,128)S(1)}, f32[17,16,128]{2,1,0:T(8,128)}, u32[]{:S(2)}) copy-start(f32[17,16,128]{2,1,0:T(8,128)} %param.23) | copy-start | bytes 417796
  6.2 230.2 %copy-start.2 = (f32[17,16,128]{2,1,0:T(8,128)S(1)}, f32[17,16,128]{2,1,0:T(8,128)}, u32[]{:S(2)}) copy-start(f32[17,16,128]{2,1,0:T(8,128)} %param.22) | copy-start | bytes 417796
  229.8 6.6 %copy-start = (f32[17,16,128]{2,1,0:T(8,128)S(1)}, f32[17,16,128]{2,1,0:T(8,128)}, u32[]{:S(2)}) copy-start(f32[17,16,128]{2,1,0:T(8,128)} %refs_2_.1) | copy-start | bytes 417796

commit v5 on v4

--- a/solution.py
+++ b/solution.py
@@ -242,49 +242,112 @@
     )
 
 
+def send_far(plan, b, k):
+    for off in range(plan.cols):
+        src, dst, slot, to = pair_copies(plan, b, True, off, k)
+        remote(src, dst, b.pair_sends.at[0], b.pair_recvs.at[slot], to).start()
+
+
+def send_near(plan, b, k):
+    for off in range(1, plan.cols):
+        src, dst, slot, to = pair_copies(plan, b, False, off, k)
+        remote(src, dst, b.pair_sends.at[1], b.pair_recvs.at[slot], to).start()
+    src, dst, slot, _ = pair_copies(plan, b, False, 0, k)
+    pltpu.make_async_copy(src, dst, b.pair_local.at[slot]).start()
+
+
+def mat_spot(plan, b, shard, col):
+    return b.mats_in.at[shard * (plan.cols // 2) + col // 2, col % 2]
+
+
+def both_shards(plan):
+    row, _, half, _ = plan.here()
+    return row, (1 - half) * plan.half_rows + row % plan.half_rows
+
+
+def cross_copy(plan, b, shard):
+    _, col, _, _ = plan.here()
+    _, other = both_shards(plan)
+    to = mat_spot(plan, b, shard, col)
+    return remote(b.mats_own.at[col], to, b.cross_sems.at[0], b.cross_sems.at[1], (other, col))
+
+
 def enter_start(plan, b):
     row, col, half, _ = plan.here()
-    other = (1 - half) * plan.half_rows + row % plan.half_rows
+    _, other = both_shards(plan)
+    b.corner[...] = jnp.zeros_like(b.corner)
+    b.corner[:N_GAINS, : plan.shard] = b.gains_own[...]
+    b.corner[STRUCT_LANE : STRUCT_LANE + b.struct_own.shape[0], : plan.shard] = b.struct_own[...]
     b.mats_own[...] = jnp.zeros_like(b.mats_own)
     for m in range(N_MATS):
         b.mats_own[plan.place(m)] = b.weights[m].astype(BF16)
-    b.mats_own[plan.place(HIGH)] = b.extra[...].astype(BF16)
+    b.mats_own[plan.place(HIGH)] = b.corner[...].T[: plan.shard].astype(BF16)
     greet(plan)
-    spot = row * plan.cols + col
-    remote(b.mats_own.at[col], b.mats_in.at[spot], b.cross_sems.at[0], b.cross_sems.at[1], (other, col)).start()
-    for k in range(plan.side_blocks):
-        for off in range(plan.cols):
-            src, dst, slot, to = pair_copies(plan, b, True, off, k)
-            remote(src, dst, b.pair_sends.at[0], b.pair_recvs.at[slot], to).start()
-        for off in range(1, plan.cols):
-            src, dst, slot, to = pair_copies(plan, b, False, off, k)
-            remote(src, dst, b.pair_sends.at[1], b.pair_recvs.at[slot], to).start()
-        src, dst, slot, _ = pair_copies(plan, b, False, 0, k)
-        pltpu.make_async_copy(src, dst, b.pair_local.at[slot]).start()
+    cross_copy(plan, b, row).start()
+    b.mats_in[row * (plan.cols // 2) + col // 2, col % 2] = b.mats_own[col]
+    send_near(plan, b, 0)
+    b.mix[...] = mixing(plan)
+    cross_copy(plan, b, other).wait_recv()
+    first_share(plan, b)
+    second_share(plan, b)
+    send_far(plan, b, 0)
+    for k in range(1, plan.side_blocks):
+        send_near(plan, b, k)
+        send_far(plan, b, k)
     remote(b.near.at[1 - half, col], b.near_far, b.near_sems.at[0], b.near_sems.at[1], (other, col)).start()
-    b.mats_in[spot] = b.mats_own[col]
-
-
-def share_mats(plan, b):
-    row, col, half, me = plan.here()
-    other = (1 - half) * plan.half_rows + row % plan.half_rows
-    spot = other * plan.cols + col
-    cross = remote(b.mats_own.at[col], b.mats_in.at[spot], b.cross_sems.at[0], b.cross_sems.at[1], (other, col))
-    cross.wait_recv()
+
+
+def first_share(plan, b):
+    _, col, half, me = plan.here()
 
     def share(off, carry):
         to = plan.member(half, (me + off) % plan.members)
-        for shard in (row, other):
-            block = b.mats_in.at[shard * plan.cols + col]
+        for shard in both_shards(plan):
+            block = mat_spot(plan, b, shard, col).at[pl.ds(plan.early_slots, plan.late_slots)]
             remote(block, block, b.share_sems.at[0], b.share_sems.at[1], to).start()
         return carry
 
     lax.fori_loop(1, plan.members, share, 0)
-    blocks = b.mats_in.at[pl.ds(0, 2 * plan.members - 2)]
-    whole = remote(blocks, blocks, b.share_sems.at[0], b.share_sems.at[1], plan.member(half, (me + 1) % plan.members))
-    cross.wait_send()
+
+
+def first_share_wait(plan, b):
+    _, _, half, me = plan.here()
+    away = plan.member(half, (me + 1) % plan.members)
+    slots = pl.ds(plan.early_slots, plan.late_slots)
+    blocks = b.mats_in.at[pl.ds(0, plan.members - 1), :, slots]
+    whole = remote(blocks, blocks, b.share_sems.at[0], b.share_sems.at[1], away)
     whole.wait_recv()
     whole.wait_send()
+
+
+def second_share(plan, b):
+    _, col, half, me = plan.here()
+    chips = plan.members // 2
+
+    def share(off, carry):
+        to = plan.member(half, (me // 2 + off) % chips * 2 + me % 2)
+        for shard in both_shards(plan):
+            block = mat_spot(plan, b, shard, col).at[pl.ds(0, plan.early_slots)]
+            remote(block, block, b.share_sems.at[2], b.share_sems.at[3], to).start()
+        return carry
+
+    lax.fori_loop(1, chips, share, 0)
+
+
+def second_share_wait(plan, b):
+    row, col, half, me = plan.here()
+    away = plan.member(half, (me + 2) % plan.members)
+    slots = pl.ds(0, plan.early_slots)
+    blocks = b.mats_in.at[pl.ds(0, plan.members - 2), 0, slots]
+    whole = remote(blocks, blocks, b.share_sems.at[2], b.share_sems.at[3], away)
+    whole.wait_recv()
+    whole.wait_send()
+    core = col % 2
+    part = b.mats_in.at[:, core, slots]
+    there = remote(part, part, b.share_sems.at[4], b.share_sems.at[5], (row, col + 1 - 2 * core))
+    there.start()
+    there.wait()
+    cross_copy(plan, b, both_shards(plan)[1]).wait_send()
 
 
 def pair_arrive(plan, b, block):
@@ -343,7 +406,8 @@
 
 def whole_mat(plan, b, number):
     group, slot = plan.place(number)
-    shards = [b.mats_in[row * plan.cols + group, slot].astype(F32) for row in range(plan.rows)]
+    places = [row * plan.cols + group for row in range(plan.rows)]
+    shards = [b.mats_in[place // 2, place % 2, slot].astype(F32) for place in places]
     return jnp.concatenate(shards, axis=0)
 
 
@@ -361,9 +425,9 @@
         ).astype(BF16)
 
 
-def fill_gains(plan, b, into):
+def fill_gains(plan, b, into, numbers):
     extra = whole_mat(plan, b, HIGH)
-    for number in range(N_GAINS):
+    for number in numbers:
         into[number] = jnp.broadcast_to(
             extra[:, number : number + 1], (plan.channels, plan.length)
         )
@@ -378,7 +442,7 @@
 
 def fill_sides(plan, b, first, side, rows=None):
     c = plan.channels
-    mix = mixing(plan)
+    mix = b.mix[...]
     for place in range(2):
         columns = [whole_mat(plan, b, first + place + 2 * k).T.astype(BF16) for k in range(2)]
         mixed = dot(mix, jnp.concatenate(columns, axis=0))
@@ -538,8 +602,29 @@
     grad_sides[:count, :] = (shared * projected[count:] * (1.0 - gate)).astype(BF16)
     grad_sides[count : 2 * count, :] = shared.astype(BF16)
     grad_sides[2 * count :, :] = grad_gate
-    grad_in[...] += dot(grad_sides[...], low, NT)
+    grad_in[...] += dot(low, grad_sides[...], NT)
     return dot(in_rows[...], grad_sides[...])
+
+
+def of_crop(ref, half):
+    return ref[:, pl.ds(half, 1), :].reshape(ref.shape[0], ref.shape[2])
+
+
+def staggered(items, distance, stages):
+    for step in range(len(items) + distance * (len(stages) - 1)):
+        for number, stage in enumerate(stages):
+            index = step - number * distance
+            if 0 <= index < len(items):
+                stage(*items[index])
+
+
+def gates_ahead(plan, b):
+    def body(block, inner, rows):
+        normed, _ = layer_norm(beside([b.state_one[i] for i in rows]))
+        low = (normed * wide_gain(b.gains[2], len(rows))).astype(BF16)
+        keep_rows(plan, rows, ((b.grad_state, jax.nn.sigmoid(dot(b.gate_side_two[...], low))),))
+
+    each_group(plan, ATTEND_WIDTH, lambda block: None, body, lambda block: None)
 
 
 def attend_phase(plan, b, into, out):
@@ -566,9 +651,9 @@
     weight_row = jnp.where(places < limit, 1.0, 0.0).astype(F32) * (
         1 - b.motif[pl.ds(half, 1), :]
     ).astype(F32)
-    spare = jnp.zeros((16 - b.frames.shape[1], length), F32)
-    frames_all = from_middle(plan, jnp.concatenate([b.frames[half], spare], axis=0))
-    target_all = from_middle(plan, jnp.concatenate([b.target[half], spare], axis=0))
+    spare = jnp.zeros((16 - b.frames.shape[0], length), F32)
+    frames_all = from_middle(plan, jnp.concatenate([of_crop(b.frames, half), spare], axis=0))
+    target_all = from_middle(plan, jnp.concatenate([of_crop(b.target, half), spare], axis=0))
     weight_row = from_middle(plan, weight_row)
 
 
@@ -576,10 +661,10 @@
         count = len(rows)
         gain = [wide_gain(b.gains[k], count) for k in range(2, 6)]
         before = beside([b.state_one[i] for i in rows])
-        normed, _ = layer_norm(before)
+        gating = beside([b.grad_state[i] for i in rows])
         mixed, mixed_scale = layer_norm(take_rows(plan, b.product_two, block, inner))
         mixed_low = (mixed * gain[1]).astype(BF16)
-        gating, branch = close_triangle((normed * gain[0]).astype(BF16), mixed_low, b.gate_side_two, b.out_side_two)
+        branch = dot(b.out_side_two[...], mixed_low)
         held = before + gating * branch
 
         held_normed, held_scale = layer_norm(held)
@@ -595,16 +680,21 @@
             for k in range(count)
             for head in range(NH)
         ]
-        for part, lanes, slot in parts_of:
+
+        def score(part, lanes, slot):
             b.probs[slot] = dot(b.keys[part, lanes], b.query[part, lanes], TN)
-        for part, lanes, slot in parts_of:
+
+        def normalise(part, lanes, slot):
             scores = b.probs[slot] + bias
             powers = jnp.exp(scores - jnp.max(scores, axis=0, keepdims=True))
             share = powers * (1.0 / jnp.sum(powers, axis=0, keepdims=True))
             b.probs[slot] = share
             b.probs_low[slot] = share.astype(BF16)
-        for part, lanes, slot in parts_of:
+
+        def attend(part, lanes, slot):
             b.attended[part, lanes] = dot(b.values[part, lanes], b.probs_low[slot])
+
+        staggered(parts_of, 2, (score, normalise, attend))
         gated_low = (b.attended[...] * attend_gate).astype(BF16)
         last = held + dot(b.last_side[...], gated_low)
 
@@ -636,13 +726,22 @@
             grad_gated * b.attended[...] * attend_gate * (1.0 - attend_gate)
         ).astype(BF16)
         b.grad_att[...] = (grad_gated * attend_gate).astype(BF16)
-        for part, lanes, slot in parts_of:
+
+        def share_back(part, lanes, slot):
             b.grad_probs[slot] = dot(b.values[part, lanes], b.grad_att[part, lanes], TN)
-        for part, lanes, slot in parts_of:
+            first = 2 * c + part.start
+            b.grad_sides[first : first + depth, lanes] = dot(
+                b.grad_att[part, lanes], b.probs_low[slot], NT
+            ).astype(BF16)
+
+        def normalise_back(part, lanes, slot):
             share = b.probs[slot]
             weighed = share * b.grad_probs[slot]
-            b.grad_scores[slot] = (weighed - share * jnp.sum(weighed, axis=0, keepdims=True)).astype(BF16)
-        for part, lanes, slot in parts_of:
+            b.grad_scores[slot] = (
+                weighed - share * jnp.sum(weighed, axis=0, keepdims=True)
+            ).astype(BF16)
+
+        def score_back(part, lanes, slot):
             first = part.start
             b.grad_sides[first : first + depth, lanes] = (
                 dot(b.keys[part, lanes], b.grad_scores[slot]) * depth ** (-0.5)
@@ -650,9 +749,8 @@
             b.grad_sides[c + first : c + first + depth, lanes] = dot(
                 b.query[part, lanes], b.grad_scores[slot], NT
             ).astype(BF16)
-            b.grad_sides[2 * c + first : 2 * c + first + depth, lanes] = dot(
-                b.grad_att[part, lanes], b.probs_low[slot], NT
-            ).astype(BF16)
+
+        staggered(parts_of, 2, (share_back, normalise_back, score_back))
         b.grad_attend[...] += dot(b.grad_sides[...], held_low, NT)
         grad_low = dot(b.attend_rows[...], b.grad_sides[...])
         b.grad_gains[4] += lane_fold(grad_low * held_normed)
@@ -720,22 +818,22 @@
             packed[row * plan.cols + group, 0, half, slot - first] = blocks[half, row]
 
 
-def put_sides(plan, packed, first_slot, first, grads):
+def put_sides(plan, b, packed, first_slot, first, grads):
     c = plan.channels
-    mix = mixing(plan)
+    mix = b.mix[...]
     for place in range(2):
-        mixed = grads[2 * c * place : 2 * c * (place + 1), :].astype(BF16)
-        columns = dot(mix, mixed, TN)
-        put(plan, packed, first_slot, first + place, columns[:c].T)
-        put(plan, packed, first_slot, first + place + 2, columns[c:].T)
-    put(plan, packed, first_slot, first + 4, grads[4 * c :, :].T)
+        mixed = grads[:, 2 * c * place : 2 * c * (place + 1)].astype(BF16)
+        columns = dot(mixed, mix)
+        put(plan, packed, first_slot, first + place, columns[:, :c])
+        put(plan, packed, first_slot, first + place + 2, columns[:, c:])
+    put(plan, packed, first_slot, first + 4, grads[:, 4 * c :])
 
 
 def pack_early(plan, b):
     c = plan.channels
     b.packed_early[...] = jnp.zeros_like(b.packed_early)
     put(plan, b.packed_early, 0, 5, b.grad_out_one[...])
-    put_sides(plan, b.packed_early, 0, 6, b.grad_in_two)
+    put_sides(plan, b, b.packed_early, 0, 6, b.grad_in_two)
     put(plan, b.packed_early, 0, 11, b.grad_out_two[...])
     for m in range(4):
         put(plan, b.packed_early, 0, 12 + m, b.grad_attend[m * c : (m + 1) * c, :].T)
@@ -744,7 +842,7 @@
 
 def pack_late(plan, b):
     c, first = plan.channels, plan.early_slots
-    put_sides(plan, b.packed_late, first, 0, b.grad_in_one)
+    put_sides(plan, b, b.packed_late, first, 0, b.grad_in_one)
     lanes = lax.broadcasted_iota(jnp.int32, (c, 128), 1)
     extra = jnp.zeros((c, 128), F32)
     for m in range(N_GAINS):
@@ -769,6 +867,10 @@
     fill_columns(plan, b, (5,), b.out_side_one)
     fill_sides(plan, b, 6, b.side_two, b.in_rows_two)
     c = plan.channels
+    for place in range(2):
+        part = slice(2 * c * place, 2 * c * (place + 1))
+        b.in_rows_one[:, part] = b.side_one[part, :].astype(F32).T.astype(BF16)
+    fill_gains(plan, b, b.gains, range(1, N_GAINS))
     b.in_rows_one[:, 4 * c :] = whole_mat(plan, b, 4).astype(BF16)
     b.in_rows_two[:, 4 * c :] = whole_mat(plan, b, 10).astype(BF16)
     fill_rows(plan, b, (5,), b.out_rows_one)
@@ -807,10 +909,11 @@
     late = swap(9, b.packed_late, b.got_late)
 
     enter_start(plan, b)
-    share_mats(plan, b)
-    fill_sides(plan, b, 0, b.side_one, b.in_rows_one)
-    fill_gains(plan, b, b.gains)
+    first_share_wait(plan, b)
+    fill_sides(plan, b, 0, b.side_one)
+    fill_gains(plan, b, b.gains, (0,))
     first_phase(plan, b, sides_one)
+    second_share_wait(plan, b)
     fill_late(plan, b)
     enter_finish(plan, b)
     sides_one.arrive_all()
@@ -824,6 +927,7 @@
 
     make_product(plan, False, b.full_two, b.sides_two, b.turned_out, b.staged_one)
     products_two.start_all()
+    gates_ahead(plan, b)
     attend_phase(plan, b, products_two, grads_two)
     sides_two.finish()
     products_two.finish()
@@ -881,7 +985,8 @@
         pair_in=low(plan.blocks, plan.block_own, length, c),
         near_far=pltpu.VMEM((plan.side_rows, lists), jnp.int32),
         mats_own=low(plan.cols, *group),
-        mats_in=low(plan.rows * plan.cols, *group),
+        mats_in=low(plan.members, 2, *group),
+        corner=wide(128, 128), mix=low(2 * c, 2 * c),
         state_zero=low(*by_row), state_one=wide(*by_row), grad_state=wide(*by_row), grad_gate=low(*by_row),
         parts_two=low(*two), parts_one=low(*one), staged_one=low(*one), staged_two=low(*two),
         full_one=low(*two), full_two=low(*two), product_one=low(*one), product_two=low(*one),
@@ -898,21 +1003,22 @@
         grad_probs=wide(slots, length, length), grad_scores=low(slots, length, length),
         attended=wide(c, many), grad_att=low(c, many), grad_sides=low(4 * c, many),
         grad_sides_wide=low(5 * c, wide_lanes),
-        grad_attend=wide(4 * c, c), grad_attend_out=wide(c, c), grad_in_one=wide(5 * c, c),
-        grad_in_two=wide(5 * c, c), grad_out_one=wide(c, c), grad_out_two=wide(c, c),
+        grad_attend=wide(4 * c, c), grad_attend_out=wide(c, c), grad_in_one=wide(c, 5 * c),
+        grad_in_two=wide(c, 5 * c), grad_out_one=wide(c, c), grad_out_two=wide(c, c),
         grad_gains=wide(N_GAINS, c, 128), grad_struct=wide(16, c),
         packed_early=low(*early), packed_late=low(*late), got_early=low(*early), got_late=low(*late),
         sums=wide(2, *group), crossed=wide(*group), total=wide(plan.cols, *group),
         pair_sends=dma((2,)), pair_recvs=dma((plan.blocks,)), pair_local=dma((plan.side_blocks,)),
-        near_sems=dma((2,)), cross_sems=dma((2,)), share_sems=dma((2,)), add_sems=dma((4,)),
+        near_sems=dma((2,)), cross_sems=dma((2,)), share_sems=dma((6,)), add_sems=dma((4,)),
         swap_sends=dma((10, plan.blocks)), swap_recvs=dma((10, plan.blocks)), swap_locals=dma((10, plan.blocks)),
     )
 
 
-def step_call(plan, pair, near, weights, extra, limits, frames, target, motif):
+def step_call(plan, pair, near, weights, gains, struct, limits, frames, target, motif):
     buffers = step_buffers(plan, near.shape[-1])
     spec = pl.BlockSpec(memory_space=pltpu.VMEM)
-    names = ["pair", "near", "weights", "extra", "limits", "frames", "target", "motif", "summed", "losses"]
+    names = ["pair", "near", "weights", "gains_own", "struct_own", "limits", "frames", "target", "motif"]
+    names += ["summed", "losses"]
     return pl.pallas_call(
         functools.partial(step_kernel, plan, names + list(buffers)),
         out_shape=(
@@ -920,7 +1026,7 @@
             jax.ShapeDtypeStruct((8, 128), F32),
         ),
         in_specs=[
-            pl.BlockSpec(memory_space=pl.ANY), spec, spec, spec,
+            pl.BlockSpec(memory_space=pl.ANY), spec, spec, spec, spec,
             pl.BlockSpec(memory_space=pltpu.SMEM), spec, spec, spec,
         ],
         out_specs=(spec, spec),
@@ -928,7 +1034,7 @@
         compiler_params=pltpu.CompilerParams(
             collective_id=0, has_side_effects=True, vmem_limit_bytes=VMEM_LIMIT
         ),
-    )(pair, near, weights, extra, limits, frames, target, motif)
+    )(pair, near, weights, gains, struct, limits, frames, target, motif)
 
 
 def adam_update(param, first, second, gradient, rate, decay):
@@ -943,30 +1049,50 @@
     )
 
 
+def adam_kernel(summed, losses, *refs):
+    params, outs = refs[:9], refs[9:]
+    small = summed[N_MATS]
+    turned_small = small.T
+    comps = params[3].shape[0]
+    grads = (
+        (summed[:N_MATS], 0.1, 0.01),
+        (turned_small[STRUCT_LANE : STRUCT_LANE + comps], 0.1, 0.01),
+        (turned_small[:N_GAINS], 0.4, 0.0),
+    )
+    outs[0][...] = small[0:1, LOSS_LANE : LOSS_LANE + 1]
+    outs[1][...] = losses[1:2, 0:1]
+    for k, (grad, rate, decay) in enumerate(grads):
+        param, first, second = (ref[...] for ref in params[3 * k : 3 * k + 3])
+        for ref, value in zip(outs[2 + 3 * k :], adam_update(param, first, second, grad, rate, decay)):
+            ref[...] = value
+
+
+def adam_call(summed, losses, params):
+    scalar = jax.ShapeDtypeStruct((1, 1), F32)
+    outs = [scalar, scalar] + [jax.ShapeDtypeStruct(value.shape, F32) for value in params]
+    spec = pl.BlockSpec(memory_space=pltpu.VMEM)
+    results = pl.pallas_call(
+        adam_kernel,
+        out_shape=tuple(outs),
+        in_specs=[spec] * (2 + len(params)),
+        out_specs=(spec,) * len(outs),
+    )(summed, losses, *params)
+    return (results[0].reshape(()), results[1].reshape(())) + tuple(results[2:])
+
+
 def per_device(
     plan, pair, frames, target, lengths, motif, neighbours, weights, weights_m, weights_v,
     struct_w, struct_m, struct_v, gains, gains_m, gains_v,
 ):
-    c, shard = plan.channels, plan.shard
-    comps = struct_w.shape[0]
-    extra = jnp.concatenate(
-        [
-            gains.T,
-            jnp.zeros((shard, STRUCT_LANE - N_GAINS), F32),
-            struct_w.T,
-            jnp.zeros((shard, c - STRUCT_LANE - comps), F32),
-        ],
-        axis=1,
+    near = neighbours.reshape(plan.crops, plan.cols, plan.side_rows, neighbours.shape[-1])
+    by_component = [jnp.swapaxes(value, 0, 1) for value in (frames, target)]
+    summed, losses = step_call(
+        plan, pair, near, weights, gains, struct_w, lengths, *by_component, motif
     )
-    near = neighbours.reshape(plan.crops, plan.cols, plan.side_rows, neighbours.shape[-1])
-    summed, losses = step_call(plan, pair, near, weights, extra, lengths, frames, target, motif)
-    small = summed[N_MATS]
-    own_gains = small[:, :N_GAINS].T
-    own_struct = small[:, STRUCT_LANE : STRUCT_LANE + comps].T
-    weight_new = adam_update(weights, weights_m, weights_v, summed[:N_MATS], 0.1, 0.01)
-    struct_new = adam_update(struct_w, struct_m, struct_v, own_struct, 0.1, 0.01)
-    gain_new = adam_update(gains, gains_m, gains_v, own_gains, 0.4, 0.0)
-    return (small[0, LOSS_LANE], losses[1, 0]) + weight_new + struct_new + gain_new
+    return adam_call(
+        summed, losses,
+        (weights, weights_m, weights_v, struct_w, struct_m, struct_v, gains, gains_m, gains_v),
+    )
 
 
 def solution(mesh):

time: 239 us -> 217 us (0.908)
  local copies, waits for them, and re-layouts: 11.4 us -> 0 us
  Pallas kernels: 224 us -> 216 us
  other arithmetic: 2.48 us -> 0 us
    pallas_call x1, Pallas kernels: 224 us -> 214 us  [step_call(): pl.pallas_call(functools.partial(step_kernel, plan, names + list(buffers)...]
    unnamed x36 -> x0, local copies, waits for them, and re-layouts: 8.71 us -> none
where the time goes in v5:
time: 217 us
  Pallas kernels  216 us (100%)
    pallas_call x1, Pallas kernels, step_call(): pl.pallas_call(functools.partial(step_kernel, plan, names + list(buffers)...  214 us

profile of v5, /device:TPU:0, one launch (start us, length us, event | category | flops | bytes accessed | tf_op | source)
XLA Modules:
  0.0 216.8 jit_solution(13137749190200042589)
XLA Ops:
  0.6 213.9 %shard_map.230 = (f32[18,16,128]{2,1,0:T(8,128)}, f32[8,128]{1,0:T(8,128)}) custom-call(bf16[2,32,64,128]{3,2,1,0:T(8,128)(2,1)} %refs_0_.2, s32[2,4,8,32]{3,2,1,0:T(8,128)} %bitcast.5, f32[17,16,128]{2,1,0:T(8,128)} %refs_0_.3, f32[6,16]{1,0:T(8,128)} %refs_6_.1, f32[6,16]{1,0:T(8,128)} %refs_3_.3, s32[2]{0:T(128)} %refs_5_.2, f32[6,2,256]{2,1,0:T(2,128)} %bitcast.6, ...), custom_call_target="tpu_custom_call" | custom-call | tf_op jit(solution)/shard_map/pallas_call | solution.py:1022
  214.6 2.0 shard_map.231

commit v6 on v5

--- a/solution.py
+++ b/solution.py
@@ -1,4 +1,5 @@
 import functools
+import math
 import types
 
 import jax
@@ -27,6 +28,8 @@
 VMEM_LIMIT = 62 * 2**20
 WIDTH = 2
 ATTEND_WIDTH = 4
+STRIDE = 7
+RING = 8
 NN = ((1,), (0,))
 NT = ((1,), (1,))
 TN = ((0,), (0,))
@@ -80,13 +83,6 @@
         _, _, half, _ = self.here()
         return (position + half * self.middle) % self.length
 
-    def pieces(self):
-        for side in range(2):
-            for member in range(self.members):
-                row, col = member // self.cols, member % self.cols
-                first = side * self.middle + row * self.block_rows + col * self.side_rows
-                yield first, member, side * self.side_blocks
-
 
 def layer_norm(values):
     center = values - jnp.mean(values, axis=0, keepdims=True)
@@ -115,26 +111,23 @@
 
 
 class Swap:
-    def __init__(self, plan, half, me, src, dst, sems):
-        self.plan, self.half, self.me, self.src, self.dst = plan, half, me, src, dst
+    def __init__(self, plan, half, me, src, dst, sems, step=1):
+        self.plan, self.src, self.dst, self.count = plan, src, dst, plan.members // step
+        self.me = me // step
+        self.stride = STRIDE if math.gcd(STRIDE, self.count) == 1 else 1
+        self.device = lambda index: plan.member(half, index * step + me % step)
         self.send, self.recv, self.local = sems
 
     def start(self, block):
-        plan, half, me = self.plan, self.half, self.me
-
         def one(off, carry):
-            to = (me + off) % plan.members
-            pltpu.make_async_remote_copy(
-                src_ref=self.src.at[to, block],
-                dst_ref=self.dst.at[me, block],
-                send_sem=self.send.at[block],
-                recv_sem=self.recv.at[block],
-                device_id=plan.member(half, to),
-                device_id_type=MESH,
+            to = (self.me + off * self.stride) % self.count
+            remote(
+                self.src.at[to, block], self.dst.at[self.me, block],
+                self.send.at[block], self.recv.at[block], self.device(to),
             ).start()
             return carry
 
-        lax.fori_loop(1, plan.members, one, 0)
+        lax.fori_loop(1, self.count, one, 0)
         self.own(block).start()
 
     def own(self, block):
@@ -144,33 +137,15 @@
         )
 
     def whole(self, block):
-        others = pl.ds(0, self.plan.members - 1)
-        return pltpu.make_async_remote_copy(
-            src_ref=self.src.at[others, block],
-            dst_ref=self.dst.at[others, block],
-            send_sem=self.send.at[block],
-            recv_sem=self.recv.at[block],
-            device_id=self.plan.member(self.half, (self.me + 1) % self.plan.members),
-            device_id_type=MESH,
+        others = pl.ds(0, self.count - 1)
+        return remote(
+            self.src.at[others, block], self.dst.at[others, block],
+            self.send.at[block], self.recv.at[block], self.device((self.me + 1) % self.count),
         )
 
     def arrive(self, block):
         self.whole(block).wait_recv()
         self.own(block).wait()
-
-    def arrive_all(self):
-        def one(block, carry):
-            self.arrive(block)
-            return carry
-
-        lax.fori_loop(0, self.plan.blocks, one, 0)
-
-    def start_all(self):
-        def one(block, carry):
-            self.start(block)
-            return carry
-
-        lax.fori_loop(0, self.plan.blocks, one, 0)
 
     def finish(self):
         def one(block, carry):
@@ -385,23 +360,65 @@
     near.wait_recv()
 
 
-def add_grads(plan, b):
-    row, col, half, _ = plan.here()
-    other = (1 - half) * plan.half_rows + row % plan.half_rows
-    cross = remote(b.sums.at[1 - half], b.crossed, b.add_sems.at[0], b.add_sems.at[1], (other, col))
-    cross.start()
-    cross.wait()
-    b.total[col] = b.sums[half] + b.crossed[...]
-    for off in range(1, plan.cols):
-        to = (col + off) % plan.cols
-        remote(b.total.at[col], b.total.at[col], b.add_sems.at[2], b.add_sems.at[3], (row, to)).start()
-    blocks = b.total.at[pl.ds(0, plan.cols - 1)]
-    whole = remote(blocks, blocks, b.add_sems.at[2], b.add_sems.at[3], (row, (col + 1) % plan.cols))
-    whole.wait_send()
-    whole.wait_recv()
-    for m in range(N_MATS):
-        b.summed[m] = b.total[plan.place(m)]
-    b.summed[N_MATS] = b.total[plan.place(HIGH)] + b.total[plan.place(LOW)]
+class Adding:
+    def __init__(self, plan, sums, crossed, total, sems):
+        row, col, half, _ = plan.here()
+        _, other = both_shards(plan)
+        self.plan, self.sums, self.crossed, self.total, self.sems = plan, sums, crossed, total, sems
+        self.row, self.col, self.half = row, col, half
+        self.cross = remote(sums.at[1 - half], crossed, sems.at[0], sems.at[1], (other, col))
+
+    def gather(self):
+        plan, col, total, sems = self.plan, self.col, self.total, self.sems
+        self.cross.wait()
+        total[col] = self.sums[self.half] + self.crossed[...]
+        for off in range(1, plan.cols):
+            to = (self.row, (col + off) % plan.cols)
+            remote(total.at[col], total.at[col], sems.at[2], sems.at[3], to).start()
+
+    def finish(self):
+        plan = self.plan
+        blocks = self.total.at[pl.ds(0, plan.cols - 1)]
+        to = (self.row, (self.col + 1) % plan.cols)
+        whole = remote(blocks, blocks, self.sems.at[2], self.sems.at[3], to)
+        whole.wait_send()
+        whole.wait_recv()
+
+
+def late_copy(plan, b, half, me, off):
+    to = (me + off) % plan.members
+    return remote(
+        b.packed_late.at[to // 2, to % 2], b.got_late.at[me // 2, me % 2],
+        b.late_sems.at[0, off], b.late_sems.at[1, off], plan.member(half, to),
+    )
+
+
+def start_late(plan, b, half, me):
+    def one(off, carry):
+        late_copy(plan, b, half, me, off).start()
+        return carry
+
+    lax.fori_loop(1, plan.members, one, 0)
+    b.got_late[me // 2, me % 2] = b.packed_late[me // 2, me % 2]
+
+
+def arrive_late(plan, b, half, me):
+    def one(off, carry):
+        late_copy(plan, b, half, me, off).wait()
+        return carry
+
+    lax.fori_loop(1, plan.members, one, 0)
+
+
+def add_in_chip(plan, b):
+    row, col, _, _ = plan.here()
+    core = col % 2
+    other = (row, col + 1 - 2 * core)
+    copy = remote(b.packed_early.at[:, 1 - core], b.got_core, b.core_sems.at[0], b.core_sems.at[1], other)
+    copy.start()
+    copy.wait()
+    both = b.packed_early[:, core].astype(F32) + b.got_core[...].astype(F32)
+    b.chip_early[:, 0] = both.astype(BF16)
 
 
 def whole_mat(plan, b, number):
@@ -498,50 +515,60 @@
     return beside([from_members(plan, product[:, block, r]) for r in inner])
 
 
-def turned(plan, ref):
+def turn_in(plan, swap, ref, into):
     count = ref.shape[3]
-    pieces = [
-        ref[member, first : first + plan.side_blocks].reshape(plan.side_rows, count, plan.length)
-        for _, member, first in plan.pieces()
-    ]
-    return jnp.swapaxes(jnp.concatenate(pieces, axis=0), 0, 1)
-
-
-def turned_back(plan, channels, into):
-    values = jnp.swapaxes(channels, 0, 1)
-    shape = (plan.side_blocks, plan.block_own) + values.shape[1:]
-    for place, member, first in plan.pieces():
-        into[member, first : first + plan.side_blocks] = values[place : place + plan.side_rows].reshape(shape)
-
-
-def make_product(plan, outgoing, full, sides, turned_out, staged):
-    sides[...] = turned(plan, full)
+    for side in range(2):
+        for k in range(plan.side_blocks):
+            swap.arrive(side * plan.side_blocks + k)
+        first = side * plan.side_blocks
+        pieces = [
+            ref[member, first : first + plan.side_blocks].reshape(plan.side_rows, count, plan.length)
+            for member in range(plan.members)
+        ]
+        rows = jnp.concatenate(pieces, axis=0)
+        into[:, side * plan.middle : (side + 1) * plan.middle, :] = jnp.swapaxes(rows, 0, 1)
+
+
+def turn_out(plan, channels, count, into, swap):
+    shape = (plan.side_blocks, plan.block_own, count, plan.length)
+    for side in range(2):
+        first = side * plan.side_blocks
+        rows = jnp.swapaxes(channels[:count, side * plan.middle : (side + 1) * plan.middle, :], 0, 1)
+        for member in range(plan.members):
+            part = rows[member * plan.side_rows : (member + 1) * plan.side_rows]
+            into[member, first : first + plan.side_blocks] = part.reshape(shape)
+        for k in range(plan.side_blocks):
+            swap.start(first + k)
+
+
+def make_product(plan, b, outgoing, arriving, sides, leaving):
     own = plan.own_channels
+    turn_in(plan, arriving, arriving.dst, sides)
 
     def channel(h, carry):
-        turned_out[h] = dot(sides[h], sides[own + h], NT if outgoing else TN).astype(BF16)
+        b.turned_out[h] = dot(sides[h], sides[own + h], NT if outgoing else TN).astype(BF16)
         return carry
 
     lax.fori_loop(0, own, channel, 0)
-    turned_back(plan, turned_out[:own], staged)
-
-
-def make_product_back(plan, outgoing, grads, sides, grad_turned, turned_out, staged):
-    grad_turned[...] = turned(plan, grads)
+    turn_out(plan, b.turned_out, own, leaving.src, leaving)
+
+
+def make_product_back(plan, b, outgoing, arriving, sides, leaving):
     own = plan.own_channels
+    turn_in(plan, arriving, arriving.dst, b.grad_turned)
 
     def channel(h, carry):
-        left, right, grad = sides[h], sides[own + h], grad_turned[h]
+        left, right, grad = sides[h], sides[own + h], b.grad_turned[h]
         if outgoing:
             grad_left, grad_right = dot(grad, right), dot(grad, left, TN)
         else:
             grad_left, grad_right = dot(right, grad, NT), dot(left, grad)
-        turned_out[h] = grad_left.astype(BF16)
-        turned_out[own + h] = grad_right.astype(BF16)
+        b.turned_out[h] = grad_left.astype(BF16)
+        b.turned_out[own + h] = grad_right.astype(BF16)
         return carry
 
     lax.fori_loop(0, own, channel, 0)
-    turned_back(plan, turned_out[...], staged)
+    turn_out(plan, b.turned_out, 2 * own, leaving.src, leaving)
 
 
 def first_phase(plan, b, out):
@@ -659,6 +686,8 @@
 
     def body(block, inner, rows):
         count = len(rows)
+        group = rows[0] // count
+        grad_sides = b.grad_sides.at[group]
         gain = [wide_gain(b.gains[k], count) for k in range(2, 6)]
         before = beside([b.state_one[i] for i in rows])
         gating = beside([b.grad_state[i] for i in rows])
@@ -722,37 +751,37 @@
         grad_branch = grad_last.astype(BF16)
         b.grad_attend_out[...] += dot(gated_low, grad_branch, NT)
         grad_gated = dot(b.last_rows[...], grad_branch)
-        b.grad_sides[3 * c :, :] = (
+        grad_sides[3 * c :, :] = (
             grad_gated * b.attended[...] * attend_gate * (1.0 - attend_gate)
         ).astype(BF16)
         b.grad_att[...] = (grad_gated * attend_gate).astype(BF16)
 
         def share_back(part, lanes, slot):
-            b.grad_probs[slot] = dot(b.values[part, lanes], b.grad_att[part, lanes], TN)
+            b.grad_probs[slot % RING] = dot(b.values[part, lanes], b.grad_att[part, lanes], TN)
             first = 2 * c + part.start
-            b.grad_sides[first : first + depth, lanes] = dot(
+            grad_sides[first : first + depth, lanes] = dot(
                 b.grad_att[part, lanes], b.probs_low[slot], NT
             ).astype(BF16)
 
         def normalise_back(part, lanes, slot):
             share = b.probs[slot]
-            weighed = share * b.grad_probs[slot]
-            b.grad_scores[slot] = (
+            weighed = share * b.grad_probs[slot % RING]
+            b.grad_scores[slot % RING] = (
                 weighed - share * jnp.sum(weighed, axis=0, keepdims=True)
             ).astype(BF16)
 
         def score_back(part, lanes, slot):
             first = part.start
-            b.grad_sides[first : first + depth, lanes] = (
-                dot(b.keys[part, lanes], b.grad_scores[slot]) * depth ** (-0.5)
+            grad_sides[first : first + depth, lanes] = (
+                dot(b.keys[part, lanes], b.grad_scores[slot % RING]) * depth ** (-0.5)
             ).astype(BF16)
-            b.grad_sides[c + first : c + first + depth, lanes] = dot(
-                b.query[part, lanes], b.grad_scores[slot], NT
+            grad_sides[c + first : c + first + depth, lanes] = dot(
+                b.query[part, lanes], b.grad_scores[slot % RING], NT
             ).astype(BF16)
 
         staggered(parts_of, 2, (share_back, normalise_back, score_back))
-        b.grad_attend[...] += dot(b.grad_sides[...], held_low, NT)
-        grad_low = dot(b.attend_rows[...], b.grad_sides[...])
+        b.held_low[group] = held_low
+        grad_low = dot(b.attend_rows[...], grad_sides[...])
         b.grad_gains[4] += lane_fold(grad_low * held_normed)
         grad_held = grad_last + layer_norm_back(grad_low, held_normed, held_scale, gain[2])
         gate_back, grad_product = close_triangle_back(
@@ -763,6 +792,9 @@
         send_sides(plan, b.parts_one, block, inner, grad_product)
 
     each_group(plan, ATTEND_WIDTH, into.arrive, body, out.start)
+
+    for group in range(b.held_low.shape[0]):
+        b.grad_attend[...] += dot(b.grad_sides[group], b.held_low[group], NT)
     b.losses[1:2, :] = jnp.broadcast_to(loss_count, (1, 128))
 
 
@@ -815,7 +847,8 @@
     blocks = value.reshape(2, plan.half_rows, plan.shard, plan.channels).astype(BF16)
     for half in range(2):
         for row in range(plan.half_rows):
-            packed[row * plan.cols + group, 0, half, slot - first] = blocks[half, row]
+            member = row * plan.cols + group
+            packed[member // 2, member % 2, half, slot - first] = blocks[half, row]
 
 
 def put_sides(plan, b, packed, first_slot, first, grads):
@@ -893,9 +926,9 @@
     b = types.SimpleNamespace(**dict(zip(names, refs)))
     _, _, half, me = plan.here()
 
-    def swap(number, src, dst):
+    def swap(number, src, dst, step=1):
         sems = [ref.at[number] for ref in (b.swap_sends, b.swap_recvs, b.swap_locals)]
-        return Swap(plan, half, me, src, dst, sems)
+        return Swap(plan, half, me, src, dst, sems, step)
 
     sides_one = swap(0, b.parts_two, b.full_one)
     products_one = swap(1, b.staged_one, b.product_one)
@@ -905,8 +938,9 @@
     parts_two = swap(5, b.staged_two, b.grad_parts_two)
     grads_one = swap(6, b.parts_one, b.full_grad_one)
     parts_one = swap(7, b.staged_two, b.grad_parts_one)
-    early = swap(8, b.packed_early, b.got_early)
-    late = swap(9, b.packed_late, b.got_late)
+    early = swap(8, b.chip_early, b.got_early, 2)
+    add_early = Adding(plan, b.sums_early, b.crossed_early, b.total_early, b.add_sems.at[0])
+    add_late = Adding(plan, b.sums_late, b.crossed_late, b.total_late, b.add_sems.at[1])
 
     enter_start(plan, b)
     first_share_wait(plan, b)
@@ -916,50 +950,53 @@
     second_share_wait(plan, b)
     fill_late(plan, b)
     enter_finish(plan, b)
-    sides_one.arrive_all()
+
+    make_product(plan, b, True, sides_one, b.sides_one, products_one)
     sides_one.finish()
-
-    make_product(plan, True, b.full_one, b.sides_one, b.turned_out, b.staged_one)
-    products_one.start_all()
     middle_phase(plan, b, products_one, sides_two)
     products_one.finish()
-    sides_two.arrive_all()
-
-    make_product(plan, False, b.full_two, b.sides_two, b.turned_out, b.staged_one)
-    products_two.start_all()
+
+    make_product(plan, b, False, sides_two, b.sides_two, products_two)
     gates_ahead(plan, b)
     attend_phase(plan, b, products_two, grads_two)
     sides_two.finish()
     products_two.finish()
-    grads_two.arrive_all()
+
+    make_product_back(plan, b, False, grads_two, b.sides_two, parts_two)
     grads_two.finish()
-
-    make_product_back(
-        plan, False, b.full_grad_two, b.sides_two, b.grad_turned, b.turned_out, b.staged_two
-    )
-    parts_two.start_all()
     turn_phase(plan, b, parts_two, grads_one)
     parts_two.finish()
     pack_early(plan, b)
-    grads_one.arrive_all()
-    grads_one.finish()
-
-    make_product_back(
-        plan, True, b.full_grad_one, b.sides_one, b.grad_turned, b.turned_out, b.staged_two
-    )
-    parts_one.start_all()
+    add_in_chip(plan, b)
+
+    make_product_back(plan, b, True, grads_one, b.sides_one, parts_one)
     early.start(0)
     last_phase(plan, b, parts_one)
     pack_late(plan, b)
-    late.start(0)
+    start_late(plan, b, half, me)
+    grads_one.finish()
     parts_one.finish()
     early.arrive(0)
-    b.sums[:, : plan.early_slots] = jnp.sum(b.got_early[:, 0].astype(F32), axis=0)
-    late.arrive(0)
-    b.sums[:, plan.early_slots :] = jnp.sum(b.got_late[:, 0].astype(F32), axis=0)
-    add_grads(plan, b)
+    b.sums_early[...] = jnp.sum(b.got_early[:, 0].astype(F32), axis=0)
+    add_early.cross.start()
+    arrive_late(plan, b, half, me)
+    b.sums_late[...] = jnp.sum(b.got_late[...].astype(F32), axis=(0, 1))
+    add_late.cross.start()
+    add_early.gather()
+    add_late.gather()
+    add_early.finish()
+    add_late.finish()
     early.whole(0).wait_send()
-    late.whole(0).wait_send()
+    totals = (b.total_early, b.total_late)
+
+    def total_of(number):
+        group, slot = plan.place(number)
+        late = slot >= plan.early_slots
+        return totals[late][group, slot - plan.early_slots * late]
+
+    for m in range(N_MATS):
+        b.summed[m] = total_of(m)
+    b.summed[N_MATS] = total_of(HIGH) + total_of(LOW)
 
 
 def step_buffers(plan, lists):
@@ -967,11 +1004,12 @@
     wide_lanes = min(WIDTH, plan.block_own) * length
     many = min(ATTEND_WIDTH, plan.block_own) * length
     slots = NH * many // length
+    ring, groups = min(RING, slots), plan.own_rows * length // many
     by_row = (plan.own_rows, c, length)
     two = (members, plan.blocks, plan.block_own, 2 * own, length)
     one = (members, plan.blocks, plan.block_own, own, length)
-    early = (members, 1, 2, plan.early_slots, plan.shard, c)
-    late = (members, 1, 2, plan.late_slots, plan.shard, c)
+    chips = members // 2
+    early, late = ((2, slot_count, plan.shard, c) for slot_count in (plan.early_slots, plan.late_slots))
     group = (plan.slots, plan.shard, c)
     dma = pltpu.SemaphoreType.DMA
 
@@ -1000,17 +1038,19 @@
         counts=wide(plan.own_rows, length), places_bias=wide(length, 128),
         query=low(c, many), keys=low(c, many), values=low(c, many),
         probs=wide(slots, length, length), probs_low=low(slots, length, length),
-        grad_probs=wide(slots, length, length), grad_scores=low(slots, length, length),
-        attended=wide(c, many), grad_att=low(c, many), grad_sides=low(4 * c, many),
+        grad_probs=wide(ring, length, length), grad_scores=low(ring, length, length),
+        attended=wide(c, many), grad_att=low(c, many), grad_sides=low(groups, 4 * c, many), held_low=low(groups, c, many),
         grad_sides_wide=low(5 * c, wide_lanes),
         grad_attend=wide(4 * c, c), grad_attend_out=wide(c, c), grad_in_one=wide(c, 5 * c),
         grad_in_two=wide(c, 5 * c), grad_out_one=wide(c, c), grad_out_two=wide(c, c),
         grad_gains=wide(N_GAINS, c, 128), grad_struct=wide(16, c),
-        packed_early=low(*early), packed_late=low(*late), got_early=low(*early), got_late=low(*late),
-        sums=wide(2, *group), crossed=wide(*group), total=wide(plan.cols, *group),
+        packed_early=low(chips, 2, *early), packed_late=low(chips, 2, *late), got_core=low(chips, *early),
+        chip_early=low(chips, 1, *early), got_early=low(chips, 1, *early), got_late=low(chips, 2, *late),
+        sums_early=wide(*early), crossed_early=wide(*early[1:]), total_early=wide(plan.cols, *early[1:]),
+        sums_late=wide(*late), crossed_late=wide(*late[1:]), total_late=wide(plan.cols, *late[1:]),
         pair_sends=dma((2,)), pair_recvs=dma((plan.blocks,)), pair_local=dma((plan.side_blocks,)),
-        near_sems=dma((2,)), cross_sems=dma((2,)), share_sems=dma((6,)), add_sems=dma((4,)),
-        swap_sends=dma((10, plan.blocks)), swap_recvs=dma((10, plan.blocks)), swap_locals=dma((10, plan.blocks)),
+        near_sems=dma((2,)), cross_sems=dma((2,)), share_sems=dma((6,)), add_sems=dma((2, 4)), core_sems=dma((2,)), late_sems=dma((2, members)),
+        swap_sends=dma((9, plan.blocks)), swap_recvs=dma((9, plan.blocks)), swap_locals=dma((9, plan.blocks)),
     )
 
 

time: 217 us -> 212 us (0.977)
  Pallas kernels: 216 us -> 211 us
    pallas_call x1, Pallas kernels: 214 us -> 209 us  [step_call(): pl.pallas_call(functools.partial(step_kernel, plan, names + list(buffers)...]
where the time goes in v6:
time: 212 us; the launch traced here: 211 us
  Pallas kernels  211 us (100%)
    pallas_call x1, Pallas kernels, step_call(): pl.pallas_call(functools.partial(step_kernel, plan, names + list(buffers)...  209 us

profile of v6, /device:TPU:0, one launch (start us, length us, event | category | flops | bytes accessed | tf_op | source)
XLA Modules:
  0.0 211.5 jit_solution(15683405288844740796)
XLA Ops:
  0.6 208.6 %shard_map.230 = (f32[18,16,128]{2,1,0:T(8,128)}, f32[8,128]{1,0:T(8,128)}) custom-call(bf16[2,32,64,128]{3,2,1,0:T(8,128)(2,1)} %refs_0_.2, s32[2,4,8,32]{3,2,1,0:T(8,128)} %bitcast.5, f32[17,16,128]{2,1,0:T(8,128)} %refs_0_.3, f32[6,16]{1,0:T(8,128)} %refs_6_.1, f32[6,16]{1,0:T(8,128)} %refs_3_.3, s32[2]{0:T(128)} %refs_5_.2, f32[6,2,256]{2,1,0:T(2,128)} %bitcast.6, ...), custom_call_target="tpu_custom_call" | custom-call | tf_op jit(solution)/shard_map/pallas_call | solution.py:1062
  209.3 2.0 shard_map.231

commit v7 on v6

--- a/solution.py
+++ b/solution.py
@@ -545,11 +545,8 @@
     own = plan.own_channels
     turn_in(plan, arriving, arriving.dst, sides)
 
-    def channel(h, carry):
+    for h in range(own):
         b.turned_out[h] = dot(sides[h], sides[own + h], NT if outgoing else TN).astype(BF16)
-        return carry
-
-    lax.fori_loop(0, own, channel, 0)
     turn_out(plan, b.turned_out, own, leaving.src, leaving)
 
 
@@ -557,17 +554,14 @@
     own = plan.own_channels
     turn_in(plan, arriving, arriving.dst, b.grad_turned)
 
-    def channel(h, carry):
-        left, right, grad = sides[h], sides[own + h], b.grad_turned[h]
-        if outgoing:
-            grad_left, grad_right = dot(grad, right), dot(grad, left, TN)
-        else:
-            grad_left, grad_right = dot(right, grad, NT), dot(left, grad)
+    for h in range(own):
+        right, grad = sides[own + h], b.grad_turned[h]
+        grad_left = dot(grad, right) if outgoing else dot(right, grad, NT)
         b.turned_out[h] = grad_left.astype(BF16)
+    for h in range(own):
+        left, grad = sides[h], b.grad_turned[h]
+        grad_right = dot(grad, left, TN) if outgoing else dot(left, grad)
         b.turned_out[own + h] = grad_right.astype(BF16)
-        return carry
-
-    lax.fori_loop(0, own, channel, 0)
     turn_out(plan, b.turned_out, 2 * own, leaving.src, leaving)
 
 

time: 212 us -> 206 us (0.972)
  Pallas kernels: 211 us -> 205 us
    pallas_call x1, Pallas kernels: 209 us -> 203 us  [step_call(): pl.pallas_call(functools.partial(step_kernel, plan, names + list(buffers)...]
where the time goes in v7:
time: 206 us
  Pallas kernels  205 us (100%)
    pallas_call x1, Pallas kernels, step_call(): pl.pallas_call(functools.partial(step_kernel, plan, names + list(buffers)...  203 us

profile of v7, /device:TPU:0, one launch (start us, length us, event | category | flops | bytes accessed | tf_op | source)
XLA Modules:
  0.0 205.7 jit_solution(13335018314617395323)
XLA Ops:
  0.6 202.9 %shard_map.230 = (f32[18,16,128]{2,1,0:T(8,128)}, f32[8,128]{1,0:T(8,128)}) custom-call(bf16[2,32,64,128]{3,2,1,0:T(8,128)(2,1)} %refs_0_.2, s32[2,4,8,32]{3,2,1,0:T(8,128)} %bitcast.5, f32[17,16,128]{2,1,0:T(8,128)} %refs_0_.3, f32[6,16]{1,0:T(8,128)} %refs_6_.1, f32[6,16]{1,0:T(8,128)} %refs_3_.3, s32[2]{0:T(128)} %refs_5_.2, f32[6,2,256]{2,1,0:T(2,128)} %bitcast.6, ...), custom_call_target="tpu_custom_call" | custom-call | tf_op jit(solution)/shard_map/pallas_call | solution.py:1056
  203.5 2.0 shard_map.231

commit v8 on v7

--- a/solution.py
+++ b/solution.py
@@ -26,9 +26,10 @@
 BF16 = jnp.bfloat16
 MESH = pl.DeviceIdType.MESH
 VMEM_LIMIT = 62 * 2**20
-WIDTH = 2
+WIDTH = 4
 ATTEND_WIDTH = 4
 STRIDE = 7
+UNROLLED = 16
 RING = 8
 NN = ((1,), (0,))
 NT = ((1,), (1,))
@@ -127,7 +128,11 @@
             ).start()
             return carry
 
-        lax.fori_loop(1, self.count, one, 0)
+        if self.count <= UNROLLED:
+            for off in range(1, self.count):
+                one(off, 0)
+        else:
+            lax.fori_loop(1, self.count, one, 0)
         self.own(block).start()
 
     def own(self, block):
@@ -198,7 +203,10 @@
     lax.fori_loop(1, plan.members, member, 0)
     for col in range(plan.cols):
         pl.semaphore_signal(barrier, inc=1, device_id=(other, col), device_id_type=MESH)
-    pl.semaphore_wait(barrier, plan.members - 1 + plan.cols)
+
+
+def greeted(plan):
+    pl.semaphore_wait(pltpu.get_barrier_semaphore(), plan.members - 1 + plan.cols)
 
 
 def pair_copies(plan, b, far, off, k):
@@ -250,6 +258,7 @@
 def enter_start(plan, b):
     row, col, half, _ = plan.here()
     _, other = both_shards(plan)
+    greet(plan)
     b.corner[...] = jnp.zeros_like(b.corner)
     b.corner[:N_GAINS, : plan.shard] = b.gains_own[...]
     b.corner[STRUCT_LANE : STRUCT_LANE + b.struct_own.shape[0], : plan.shard] = b.struct_own[...]
@@ -257,7 +266,7 @@
     for m in range(N_MATS):
         b.mats_own[plan.place(m)] = b.weights[m].astype(BF16)
     b.mats_own[plan.place(HIGH)] = b.corner[...].T[: plan.shard].astype(BF16)
-    greet(plan)
+    greeted(plan)
     cross_copy(plan, b, row).start()
     b.mats_in[row * (plan.cols // 2) + col // 2, col % 2] = b.mats_own[col]
     send_near(plan, b, 0)
@@ -743,7 +752,8 @@
         grad_last = layer_norm_back(grad_low, last_normed, last_scale, gain[3])
 
         grad_branch = grad_last.astype(BF16)
-        b.grad_attend_out[...] += dot(gated_low, grad_branch, NT)
+        b.gated_low[group] = gated_low
+        b.grad_last_low[group] = grad_branch
         grad_gated = dot(b.last_rows[...], grad_branch)
         grad_sides[3 * c :, :] = (
             grad_gated * b.attended[...] * attend_gate * (1.0 - attend_gate)
@@ -789,6 +799,7 @@
 
     for group in range(b.held_low.shape[0]):
         b.grad_attend[...] += dot(b.grad_sides[group], b.held_low[group], NT)
+        b.grad_attend_out[...] += dot(b.gated_low[group], b.grad_last_low[group], NT)
     b.losses[1:2, :] = jnp.broadcast_to(loss_count, (1, 128))
 
 
@@ -867,12 +878,11 @@
     put(plan, b.packed_early, 0, 16, b.grad_attend_out[...])
 
 
-def pack_late(plan, b):
-    c, first = plan.channels, plan.early_slots
-    put_sides(plan, b, b.packed_late, first, 0, b.grad_in_one)
+def pack_small(plan, b):
+    c = plan.channels
     lanes = lax.broadcasted_iota(jnp.int32, (c, 128), 1)
-    extra = jnp.zeros((c, 128), F32)
-    for m in range(N_GAINS):
+    extra = jnp.where(lanes == LOSS_LANE, b.losses[0:1, :], 0.0)
+    for m in range(1, N_GAINS):
         extra += jnp.where(lanes == m, jnp.sum(b.grad_gains[m], axis=1, keepdims=True), 0.0)
     padded = jnp.concatenate(
         [
@@ -882,8 +892,14 @@
         ],
         axis=0,
     )
-    extra += padded.T
-    extra += jnp.where(lanes == LOSS_LANE, b.losses[0:1, :], 0.0)
+    b.corner[...] = extra + padded.T
+
+
+def pack_late(plan, b):
+    c, first = plan.channels, plan.early_slots
+    put_sides(plan, b, b.packed_late, first, 0, b.grad_in_one)
+    lanes = lax.broadcasted_iota(jnp.int32, (c, 128), 1)
+    extra = b.corner[...] + jnp.where(lanes == 0, jnp.sum(b.grad_gains[0], axis=1, keepdims=True), 0.0)
     high = extra.astype(BF16)
     put(plan, b.packed_late, first, HIGH, high.astype(F32))
     put(plan, b.packed_late, first, LOW, extra - high.astype(F32))
@@ -965,6 +981,7 @@
 
     make_product_back(plan, b, True, grads_one, b.sides_one, parts_one)
     early.start(0)
+    pack_small(plan, b)
     last_phase(plan, b, parts_one)
     pack_late(plan, b)
     start_late(plan, b, half, me)
@@ -1034,6 +1051,7 @@
         probs=wide(slots, length, length), probs_low=low(slots, length, length),
         grad_probs=wide(ring, length, length), grad_scores=low(ring, length, length),
         attended=wide(c, many), grad_att=low(c, many), grad_sides=low(groups, 4 * c, many), held_low=low(groups, c, many),
+        gated_low=low(groups, c, many), grad_last_low=low(groups, c, many),
         grad_sides_wide=low(5 * c, wide_lanes),
         grad_attend=wide(4 * c, c), grad_attend_out=wide(c, c), grad_in_one=wide(c, 5 * c),
         grad_in_two=wide(c, 5 * c), grad_out_one=wide(c, c), grad_out_two=wide(c, c),

time: 206 us -> 205 us (level)
  no operation moved by 1% of the time
where the time goes in v8:
time: 205 us
  Pallas kernels  204 us (100%)
    pallas_call x1, Pallas kernels, step_call(): pl.pallas_call(functools.partial(step_kernel, plan, names + list(buffers)...  202 us

profile of v8, /device:TPU:0, one launch (start us, length us, event | category | flops | bytes accessed | tf_op | source)
XLA Modules:
  0.0 205.0 jit_solution(10338310523721933674)
XLA Ops:
  0.6 202.1 %shard_map.230 = (f32[18,16,128]{2,1,0:T(8,128)}, f32[8,128]{1,0:T(8,128)}) custom-call(bf16[2,32,64,128]{3,2,1,0:T(8,128)(2,1)} %refs_0_.2, s32[2,4,8,32]{3,2,1,0:T(8,128)} %bitcast.5, f32[17,16,128]{2,1,0:T(8,128)} %refs_0_.3, f32[6,16]{1,0:T(8,128)} %refs_6_.1, f32[6,16]{1,0:T(8,128)} %refs_3_.3, s32[2]{0:T(128)} %refs_5_.2, f32[6,2,256]{2,1,0:T(2,128)} %bitcast.6, ...), custom_call_target="tpu_custom_call" | custom-call | tf_op jit(solution)/shard_map/pallas_call | solution.py:1074
  202.8 2.0 shard_map.231

commit v9 on v8

--- a/solution.py
+++ b/solution.py
@@ -121,7 +121,8 @@
 
     def start(self, block):
         def one(off, carry):
-            to = (self.me + off * self.stride) % self.count
+            turn = 1 + (off - 1 + 2 * (self.me // 2)) % (self.count - 1)
+            to = (self.me + turn * self.stride) % self.count
             remote(
                 self.src.at[to, block], self.dst.at[self.me, block],
                 self.send.at[block], self.recv.at[block], self.device(to),

time: 205 us -> 203 us (level)
    pallas_call x1, Pallas kernels: 202 us -> 200 us  [step_call(): pl.pallas_call(functools.partial(step_kernel, plan, names + list(buffers)...]
where the time goes in v9:
time: 203 us
  Pallas kernels  202 us (100%)
    pallas_call x1, Pallas kernels, step_call(): pl.pallas_call(functools.partial(step_kernel, plan, names + list(buffers)...  200 us

profile of v9, /device:TPU:0, one launch (start us, length us, event | category | flops | bytes accessed | tf_op | source)
XLA Modules:
  0.0 202.9 jit_solution(12049163199299437565)
XLA Ops:
  0.6 200.0 %shard_map.230 = (f32[18,16,128]{2,1,0:T(8,128)}, f32[8,128]{1,0:T(8,128)}) custom-call(bf16[2,32,64,128]{3,2,1,0:T(8,128)(2,1)} %refs_0_.2, s32[2,4,8,32]{3,2,1,0:T(8,128)} %bitcast.5, f32[17,16,128]{2,1,0:T(8,128)} %refs_0_.3, f32[6,16]{1,0:T(8,128)} %refs_6_.1, f32[6,16]{1,0:T(8,128)} %refs_3_.3, s32[2]{0:T(128)} %refs_5_.2, f32[6,2,256]{2,1,0:T(2,128)} %bitcast.6, ...), custom_call_target="tpu_custom_call" | custom-call | tf_op jit(solution)/shard_map/pallas_call | solution.py:1075
  200.7 2.0 %shard_map.231 = (f32[1,1]{1,0:T(1,128)}, f32[1,1]{1,0:T(1,128)}, f32[17,16,128]{2,1,0:T(8,128)}, f32[17,16,128]{2,1,0:T(8,128)}, f32[17,16,128]{2,1,0:T(8,128)}...) custom-call(f32[18,16,128]{2,1,0:T(8,128)} %get-tuple-element.24.sum, ...), custom_call_target="tpu_custom_call" | custom-call | tf_op jit(solution)/shard_map/pallas_call | solution.py:1127

commit v10 on v9

--- a/solution.py
+++ b/solution.py
@@ -727,7 +727,7 @@
         def attend(part, lanes, slot):
             b.attended[part, lanes] = dot(b.values[part, lanes], b.probs_low[slot])
 
-        staggered(parts_of, 2, (score, normalise, attend))
+        staggered(parts_of, 4, (score, normalise, attend))
         gated_low = (b.attended[...] * attend_gate).astype(BF16)
         last = held + dot(b.last_side[...], gated_low)
 

time: 203 us -> 202 us (level)
  no operation moved by 1% of the time
where the time goes in v10:
time: 202 us
  Pallas kernels  202 us (100%)
    pallas_call x1, Pallas kernels, step_call(): pl.pallas_call(functools.partial(step_kernel, plan, names + list(buffers)...  199 us

profile of v10, /device:TPU:0, one launch (start us, length us, event | category | flops | bytes accessed | tf_op | source)
XLA Modules:
  0.0 202.3 jit_solution(8581647187562983780)
XLA Ops:
  0.6 199.5 %shard_map.230 = (f32[18,16,128]{2,1,0:T(8,128)}, f32[8,128]{1,0:T(8,128)}) custom-call(bf16[2,32,64,128]{3,2,1,0:T(8,128)(2,1)} %refs_0_.2, s32[2,4,8,32]{3,2,1,0:T(8,128)} %bitcast.5, f32[17,16,128]{2,1,0:T(8,128)} %refs_0_.3, f32[6,16]{1,0:T(8,128)} %refs_6_.1, f32[6,16]{1,0:T(8,128)} %refs_3_.3, s32[2]{0:T(128)} %refs_5_.2, f32[6,2,256]{2,1,0:T(2,128)} %bitcast.6, ...), custom_call_target="tpu_custom_call" | custom-call | tf_op jit(solution)/shard_map/pallas_call | solution.py:1075
  200.1 2.0 %shard_map.231 = (f32[1,1]{1,0:T(1,128)}, f32[1,1]{1,0:T(1,128)}, f32[17,16,128]{2,1,0:T(8,128)}, f32[17,16,128]{2,1,0:T(8,128)}, f32[17,16,128]{2,1,0:T(8,128)}...) custom-call(f32[18,16,128]{2,1,0:T(8,128)} %get-tuple-element.24.sum, ...), custom_call_target="tpu_custom_call" | custom-call | tf_op jit(solution)/shard_map/pallas_call | solution.py:1127
